TPU v7x, 32 devices: a whole 2x2x4 slice. The times are simulated.
32 devices in a mesh: dom: 2 (over core), gx: 4 (over z), yz: 4 (over y, x).
Axes of the slice: x: 2, y: 2, z: 4, core: 2. Of those that a mesh axis runs over, the one named last changes fastest.
Arguments:
- field_state: float32 [2, 8, 64, 64, 128], P('dom', None, 'gx', 'yz'), as said below
- shell_owner: int32 [4, 4, 8], P('gx'), may hold values from 0 to 3, as said below
- block_sources: int32 [4, 4, 2, 4], P('gx', 'yz'), may hold values from -1 to 7, as said below
- block_targets: int32 [4, 4, 2], P('gx', 'yz'), may hold values from -1 to 63, as said below
- interp_weights: bfloat16 [4, 4, 2, 4, 512, 512], P('gx', 'yz'), as said below
Outputs:
- new_state: float32 [2, 8, 64, 64, 128], P('dom', None, 'gx', 'yz')
Inputs may be any that keep to these rules, and one draw needn't show every extreme that they name: `shell_owner`: entry [g, t, b] is the yz index of the heliosphere device, at the same gx index g, that owns shell block b of the corona device (g, t). No corona device gives more than 2 of its blocks to one owner, and in every gx index some owner receives exactly 2 blocks from each corona device of that gx index. `block_sources`: the live entries of device (g, y) come first in slot order and are the positions 0 to R - 1 of its owned list, each exactly once, R being the number of shell blocks it owns; the rest are -1. `block_targets`: live slots of one device name distinct local blocks; a slot is -1 exactly when all its sources are -1. `field_state`: each cell holds conserved variables of a state with positive density and pressure. `interp_weights`: for every target cell the entries over all 4 source blocks and their cells sum to less than one.
All inputs are finite; a program needn't handle non-finite values.
Results may differ from a plain program's by a relative error of at most 0.002.
Values may be sent and summed in bfloat16 or wider, within the bound.
No kernel may reach another device: no remote copies, remote signals or barrier semaphores. Data moves between devices by JAX's collectives and lax.ppermute only.
A program may use at most 64 MiB of HBM per device.

v0:
```python
import jax
import jax.numpy as jnp
from jax import lax
from jax.sharding import PartitionSpec as P

BLK = 8
SR = 2
CAP = 2


HEAT_RATIO = 5.0 / 3.0
CORONA_RATIO = 0.04
HELIO_RATIO = 0.03


def shifted(block, axis, distance):
    devices = range(lax.axis_size(axis))
    route = [(i - distance, i) for i in devices if i - distance in devices]
    return lax.ppermute(block, axis, route)


def extended(cells, sides, width):
    for axis, dim in sides:
        count = lax.axis_size(axis)
        head = lax.slice_in_dim(cells, 0, width, axis=dim)
        tail = lax.slice_in_dim(cells, cells.shape[dim] - width, cells.shape[dim], axis=dim)
        cells = jnp.concatenate(
            [
                lax.ppermute(tail, axis, [(i, (i + 1) % count) for i in range(count)]),
                cells,
                lax.ppermute(head, axis, [((i + 1) % count, i) for i in range(count)]),
            ],
            axis=dim,
        )
    return cells


def direction_flux(grid_cells, direction):
    density = grid_cells[0]
    momentum = grid_cells[1:4]
    magnetic = grid_cells[4:7]
    energy = grid_cells[7]
    velocity = momentum / density
    field_sq = jnp.sum(magnetic * magnetic, axis=0)
    pressure = (HEAT_RATIO - 1.0) * (
        energy - 0.5 * jnp.sum(momentum * velocity, axis=0) - 0.5 * field_sq
    )
    total_pressure = pressure + 0.5 * field_sq
    normal_speed = velocity[direction]
    normal_field = magnetic[direction]
    velocity_dot = jnp.sum(velocity * magnetic, axis=0)
    flux_list = [momentum[direction]]
    for other in range(3):
        term = momentum[other] * normal_speed - magnetic[other] * normal_field
        if other == direction:
            term = term + total_pressure
        flux_list.append(term)
    for other in range(3):
        flux_list.append(normal_speed * magnetic[other] - normal_field * velocity[other])
    flux_list.append((energy + total_pressure) * normal_speed - normal_field * velocity_dot)
    wave_speed = jnp.abs(normal_speed) + jnp.sqrt((HEAT_RATIO * pressure + field_sq) / density)
    return (jnp.stack(flux_list), wave_speed)


def interface_change(padded_line, direction):
    phys_flux, wave_speed = direction_flux(padded_line, direction)
    array_dim = direction + 1
    cell_count = padded_line.shape[array_dim]
    low_cells = lax.slice_in_dim(padded_line, 0, cell_count - 1, axis=array_dim)
    high_cells = lax.slice_in_dim(padded_line, 1, cell_count, axis=array_dim)
    low_flux = lax.slice_in_dim(phys_flux, 0, cell_count - 1, axis=array_dim)
    high_flux = lax.slice_in_dim(phys_flux, 1, cell_count, axis=array_dim)
    low_speed = lax.slice_in_dim(wave_speed, 0, cell_count - 1, axis=direction)
    high_speed = lax.slice_in_dim(wave_speed, 1, cell_count, axis=direction)
    fastest = jnp.maximum(low_speed, high_speed)
    face_flux = 0.5 * (low_flux + high_flux) - 0.5 * fastest[None] * (high_cells - low_cells)
    upper_face = lax.slice_in_dim(face_flux, 1, cell_count - 1, axis=array_dim)
    lower_face = lax.slice_in_dim(face_flux, 0, cell_count - 2, axis=array_dim)
    return upper_face - lower_face


def advance(line_set, inner_cells, step_ratio):
    change = interface_change(line_set[0], 0) + interface_change(line_set[1], 1)
    change = change + interface_change(line_set[2], 2)
    return inner_cells - step_ratio * change


def edge_copy(padded_line, direction, fix_low, fix_high):
    array_dim = direction + 1
    cell_count = padded_line.shape[array_dim]
    first_layer = lax.slice_in_dim(padded_line, 0, 1, axis=array_dim)
    second_layer = lax.slice_in_dim(padded_line, 1, 2, axis=array_dim)
    before_last = lax.slice_in_dim(padded_line, cell_count - 2, cell_count - 1, axis=array_dim)
    last_layer = lax.slice_in_dim(padded_line, cell_count - 1, cell_count, axis=array_dim)
    middle = lax.slice_in_dim(padded_line, 1, cell_count - 1, axis=array_dim)
    first_layer = jnp.where(fix_low, second_layer, first_layer)
    last_layer = jnp.where(fix_high, before_last, last_layer)
    return jnp.concatenate([first_layer, middle, last_layer], axis=array_dim)


def local(field_state, shell_owner, block_sources, block_targets, interp_weights):
    grid_cells = field_state[0]
    ncomp, len_x, len_y, len_z = grid_cells.shape
    domain = lax.axis_index("dom")
    column = lax.axis_index("gx")
    yz_index = lax.axis_index("yz")
    gx_count = lax.axis_size("gx")
    yz_count = lax.axis_size("yz")
    per_y = len_y // BLK
    per_z = len_z // BLK
    volume = BLK * BLK * BLK
    shell_cells = grid_cells[:, :, :, len_z - SR * BLK :]
    shell_cells = shell_cells.reshape(ncomp, len_x // BLK, BLK, per_y, BLK, SR, BLK)
    shell_cells = (
        shell_cells.transpose(1, 3, 5, 0, 2, 4, 6).reshape(-1, ncomp * volume).astype(jnp.bfloat16)
    )
    count_here = shell_cells.shape[0]
    owners = shell_owner[0].reshape(-1)
    own_owner = lax.dynamic_slice_in_dim(owners, yz_index * count_here, count_here)
    own_spot = yz_index * count_here + jnp.arange(count_here, dtype=jnp.int32)
    all_spots = jnp.arange(owners.shape[0], dtype=jnp.int32)
    same_owner = owners[None, :] == own_owner[:, None]
    rank_all = jnp.sum(
        (same_owner & (all_spots[None, :] < own_spot[:, None])).astype(jnp.int32), axis=1
    )
    index_here = jnp.arange(count_here, dtype=jnp.int32)
    local_same = own_owner[None, :] == own_owner[:, None]
    rank_local = jnp.sum(
        (local_same & (index_here[None, :] < index_here[:, None])).astype(jnp.int32), axis=1
    )
    slot_of = own_owner * CAP + rank_local
    slot_count = yz_count * CAP
    select = jnp.arange(slot_count, dtype=jnp.int32)[:, None] == slot_of[None, :]
    send_cells = jnp.dot(
        select.astype(jnp.bfloat16), shell_cells, preferred_element_type=jnp.float32
    )
    send_cells = send_cells.astype(jnp.bfloat16).reshape(yz_count, CAP, ncomp * volume)
    send_tags = jnp.sum(jnp.where(select, rank_all[None, :], 0), axis=1)
    send_tags = jnp.where(jnp.any(select, axis=1), send_tags, -1).reshape(yz_count, CAP)
    moved_pair = shifted((send_cells, send_tags), "dom", 1)
    got_cells, got_tags = (
        lax.all_to_all(moved_pair[0], "yz", split_axis=0, concat_axis=0, tiled=True),
        lax.all_to_all(moved_pair[1], "yz", split_axis=0, concat_axis=0, tiled=True),
    )
    got_cells = got_cells.reshape(slot_count, ncomp * volume)
    got_tags = got_tags.reshape(slot_count)
    wanted = block_sources[0, 0].reshape(-1)
    match_table = (wanted[:, None] == got_tags[None, :]) & (wanted[:, None] >= 0)
    picked = jnp.dot(
        match_table.astype(jnp.bfloat16), got_cells, preferred_element_type=jnp.float32
    )
    slots_here = block_targets.shape[2]
    picked = picked.astype(jnp.bfloat16).reshape(slots_here, -1, ncomp, volume)
    interp_blocks = jnp.einsum(
        "jkcs,jkst->jct", picked, interp_weights[0, 0], preferred_element_type=jnp.float32
    )

    def place_block(slot_number, grid_now):
        target_block = block_targets[0, 0, slot_number]
        live_slot = (target_block >= 0) & (domain == 1)
        block_spot = jnp.maximum(target_block, 0)
        block_x = block_spot // (per_y * per_z)
        block_y = block_spot // per_z % per_y
        block_z = block_spot % per_z
        corner_start = (jnp.int32(0), block_x * BLK, block_y * BLK, block_z * BLK)
        old_block = lax.dynamic_slice(grid_now, corner_start, (ncomp, BLK, BLK, BLK))
        new_block = lax.dynamic_index_in_dim(interp_blocks, slot_number, 0, keepdims=False)
        new_block = new_block.reshape(ncomp, BLK, BLK, BLK)
        return lax.dynamic_update_slice(
            grid_now, jnp.where(live_slot, new_block, old_block), corner_start
        )

    grid_cells = lax.fori_loop(0, slots_here, place_block, grid_cells)
    helio_side = domain == 1
    low_x = helio_side & (column == 0)
    high_x = helio_side & (column == gx_count - 1)
    low_y = yz_index == 0
    high_y = yz_index == yz_count - 1
    padded = extended(grid_cells, (("gx", 1), ("yz", 2)), 1)
    line_x = padded[:, :, 1:-1, :]
    line_y = padded[:, 1:-1, :, :]
    line_x = edge_copy(line_x, 0, low_x, high_x)
    line_y = edge_copy(line_y, 1, low_y, high_y)
    line_z = jnp.pad(grid_cells, ((0, 0), (0, 0), (0, 0), (1, 1)), mode="edge")
    step_ratio = jnp.where(domain == 0, CORONA_RATIO, HELIO_RATIO).astype(jnp.float32)
    updated = advance((line_x, line_y, line_z), grid_cells, step_ratio)
    return updated[None]


def solution(mesh):
    placed = (
        P("dom", None, "gx", "yz", None),
        P("gx", None, None),
        P("gx", "yz", None, None),
        P("gx", "yz", None),
        P("gx", "yz", None, None, None, None),
    )
    return jax.shard_map(
        local,
        mesh=mesh,
        in_specs=placed,
        out_specs=P("dom", None, "gx", "yz", None),
        check_vma=False,
    )
```

profile of v0, /device:TPU:0, one launch (start us, length us, event | category | flops | bytes accessed | tf_op | source)
XLA Modules:
  0.0 94.8 jit_solution(17821251125883495753)
XLA Ops:
  0.0 1.2 %copy.54 = f32[1,8,16,16,128]{4,3,2,1,0:T(8,128)S(1)} copy(f32[1,8,16,16,128]{4,3,2,1,0:T(8,128)} %param.7) | data formatting | bytes 2097152
  1.2 0.2 slice.623
  1.4 0.4 convert_element_type.26
  1.9 0.2 copy.22
  2.1 1.5 %convert_element_type.28 = bf16[8,4096]{1,0:T(8,128)(2,1)S(1)} reshape(bf16[2,2,2,8,8,8,8]{6,5,4,3,2,1,0:T(8,128)(2,1)S(1)} %bitcast.182) | data formatting | bytes 131072 | tf_op jit(solution)/shard_map/convert_element_type | solution.py:115
  3.6 0.1 reshape_squeeze.3
  3.8 0.2 convert_reduce_fusion.1
  4.0 0.1 convolution_convert_fusion.1
  4.2 3.0 %collective-permute-start.1 = (bf16[4,2,4096]{2,1,0:T(2,128)(2,1)S(1)}, bf16[4,2,4096]{2,1,0:T(2,128)(2,1)}, u32[]{:S(2)}, u32[]{:S(2)}) collective-permute-start(bf16[4,2,4096]{2,1,0:T(2,128)(2,1)S(1)} %reshape.140), channel_id=1, source_target_pairs={{0,16},{1,17},{2,18},{3,19},{4,20},{5,21},{6,22},{7,23},{8,24},{9,... | collective-permute-start | bytes 196616 | tf_op jit(solution)/shard_map/ppermute | solution.py:19
  7.2 0.1 fusion.73
  7.3 0.2 convert_reduce_fusion
  7.5 0.1 select_reduce_fusion
  7.7 0.1 select_n.183
  7.7 1.3 %collective-permute-start = (s32[4,2]{1,0:T(4,128)S(1)}, s32[4,2]{1,0:T(4,128)S(1)}, u32[]{:S(2)}, u32[]{:S(2)}) collective-permute-start(s32[4,2]{1,0:T(4,128)S(1)} %select_n.183), channel_id=1, source_target_pairs={{0,16},{1,17},{2,18},{3,19},{4,20},{5,21},{6,22},{7,23},{8,24},{9,... | collective-permute-start | bytes 104 | tf_op jit(solution)/shard_map/ppermute | solution.py:19
  9.1 0.7 collective-permute-done
  9.8 9.0 %all_to_all.14 = s32[4,1,2]{2,1,0:T(1,128)S(1)} all-to-all(s32[4,1,2]{2,1,0:T(1,128)S(1)} %bitcast.185), channel_id=1, replica_groups=mesh['dom'=2,'gx'=4,'yz'=4] {'yz'}, dimensions={0} | all-to-all | bytes 64 | tf_op jit(solution)/shard_map/all_to_all | solution.py:143
  18.8 3.3 %all-to-all-start.1 = ((bf16[4,2,4096]{2,1,0:T(2,128)(2,1)}), bf16[4,2,4096]{2,1,0:T(2,128)(2,1)S(1)}, u32[]{:S(2)}, u32[]{:S(2)}) async-start(bf16[4,2,4096]{2,1,0:T(2,128)(2,1)} %collective-permute-done.1), calls=%async_computation.1 | async-start | bytes 131072 | tf_op jit(solution)/shard_map/all_to_all | solution.py:142
  22.2 0.5 broadcast.135
  22.7 0.6 reduce.3
  23.3 0.1 eq.111
  23.4 3.5 %all-to-all-done.1 = bf16[4,2,4096]{2,1,0:T(2,128)(2,1)S(1)} async-done(((bf16[4,2,4096]{2,1,0:T(2,128)(2,1)}), bf16[4,2,4096]{2,1,0:T(2,128)(2,1)S(1)}, u32[]{:S(2)}, u32[]{:S(2)}) %all-to-all-start.1) | async-done | bytes 65568 | tf_op jit(solution)/shard_map/all_to_all | solution.py:142
  27.0 0.2 convolution_convert_fusion
  27.2 2.8 %fusion.11 = f32[2,8,512]{2,1,0:T(8,128)S(1)} fusion(bf16[2,4,8,512]{3,2,1,0:T(8,128)(2,1)S(1)} %bitcast.183, bf16[1,1,2,4,512,512]{5,4,3,2,1,0:T(8,128)(2,1)} %param.11), kind=kOutput, calls=%fused_computation.25 | convolution fusion | flops 33554432 | bytes 4292608 | tf_op jit(solution)/shard_map/jkcs,jkst->jct/dot_general | solution.py:154
  30.1 46.7 %while.16 = (s32[]{:T(128)}, f32[8,16,16,128]{3,2,1,0:T(8,128)S(1)}, s32[1,1,2]{2,1,0:T(1,128)S(1)}, pred[]{:T(512)}, f32[2,8,512]{2,1,0:T(8,128)S(1)}, /*index=...) while((s32[]{:T(128)}, ...), condition=%wide.region_5.6_spmd, body=%wide.region_4.5_spmd.sunk | while | flops 4142 | bytes 148101 | solution.py:173
  30.1 0.2 reshape.154
  30.2 0.7 fusion.90
  34.4 0.1 dynamic-slice_select_fusion.2
  34.6 18.8 %dynamic_update_slice.12 = f32[8,16,16,128]{3,2,1,0:T(8,128)S(1)} dynamic-update-slice(f32[8,16,16,128]{3,2,1,0:T(8,128)S(1)} %get-tuple-element.271, f32[8,8,8,8]{3,2,1,0:T(8,128)S(1)} %dynamic-slice_select_fusion.2, s32[]{:T(128)} %constant.204.clone.1..sunk, s32[]{:T(128)S(6)} %select_n.217, s32[]{:T(128)S(6)} %select_n.220, s32[]{:T(128)S(6)} %select_n.222) | dynamic-update-slice | bytes 32772 | tf_op jit(solution)/shard_map/while/body/eval_jaxpr/dynamic_update_slice | solution.py:169
  53.4 0.2 reshape.154
  53.6 0.7 fusion.90
  57.8 0.1 dynamic-slice_select_fusion.2
  57.9 18.8 %dynamic_update_slice.12 = f32[8,16,16,128]{3,2,1,0:T(8,128)S(1)} dynamic-update-slice(f32[8,16,16,128]{3,2,1,0:T(8,128)S(1)} %get-tuple-element.271, f32[8,8,8,8]{3,2,1,0:T(8,128)S(1)} %dynamic-slice_select_fusion.2, s32[]{:T(128)} %constant.204.clone.1..sunk, s32[]{:T(128)S(6)} %select_n.217, s32[]{:T(128)S(6)} %select_n.220, s32[]{:T(128)S(6)} %select_n.222) | dynamic-update-slice | bytes 32772 | tf_op jit(solution)/shard_map/while/body/eval_jaxpr/dynamic_update_slice | solution.py:169
  76.7 0.3 fusion.85
  77.1 0.9 pad_maximum_fusion
  78.1 0.3 multiply_reduce_fusion
  78.3 0.1 fusion.27
  78.4 0.1 fusion.25
  78.5 0.2 fusion.33
  78.7 0.2 add_dynamic-update-slice_fusion
  78.9 0.1 fusion.23
  79.0 0.1 fusion.21
  79.1 0.1 fusion.19
  79.3 1.6 %collective-permute-start.2 = (f32[8,1,16,128]{3,2,1,0:T(8,128)S(1)}, f32[8,1,16,128]{3,2,1,0:T(8,128)S(1)}, u32[]{:S(2)}, u32[]{:S(2)}) collective-permute-start(f32[8,1,16,128]{3,2,1,0:T(8,128)S(1)} %get-tuple-element.213), channel_id=1, source_target_pairs={{0,4},{4,8},{8,12},{12,0},{1,5},{5,9},{9,13},{13,1},{2,6},{6,10},{... | collective-permute-start | bytes 196616 | tf_op jit(solution)/shard_map/ppermute | solution.py:29
  80.9 2.2 %collective-permute-start.3 = (f32[8,1,16,128]{3,2,1,0:T(8,128)S(1)}, f32[8,1,16,128]{3,2,1,0:T(8,128)S(1)}, u32[]{:S(2)}, u32[]{:S(2)}) collective-permute-start(f32[8,1,16,128]{3,2,1,0:T(8,128)S(1)} %get-tuple-element.212), channel_id=1, source_target_pairs={{4,0},{8,4},{12,8},{0,12},{5,1},{9,5},{13,9},{1,13},{6,2},{10,6},{... | collective-permute-start | bytes 196616 | tf_op jit(solution)/shard_map/ppermute | solution.py:31
  83.1 0.2 fusion.35
  83.3 1.2 %fusion.3 = f32[8,16,16,129]{3,2,1,0:T(8,128)S(1)} fusion(f32[8,16,16,130]{3,2,1,0:T(8,128)S(1)} %fusion.35, f32[8,16,16,1]{3,2,1,0:T(8,128)S(1)} %get-tuple-element.215, f32[8,16,16,128]{3,2,1,0:T(8,128)S(1)} %get-tuple-element.175, f32[8,16,16,1]{3,2,1,0:T(8,128)S(1)} %get-tuple-element.214, f32[16,16,129]{2,1,0:T(8,128)S(1)} %fusion.19), kind=kLoop, calls=%fused_computation.9 | loop fusion | flops 1849344 | bytes 4367360 | tf_op jit(solution)/shard_map/sub | solution.py:76
  84.5 1.0 %collective-permute-done.2 = f32[8,1,16,128]{3,2,1,0:T(8,128)S(1)} collective-permute-done((f32[8,1,16,128]{3,2,1,0:T(8,128)S(1)}, f32[8,1,16,128]{3,2,1,0:T(8,128)S(1)}, u32[]{:S(2)}, u32[]{:S(2)}) %collective-permute-start.2) | collective-permute-done | bytes 65568 | tf_op jit(solution)/shard_map/ppermute | solution.py:29
  85.6 0.3 collective-permute-done.3
  85.9 0.1 fusion.83
  86.0 0.8 collective-permute-start.4
  86.8 2.2 %collective-permute-start.5 = (f32[8,18,1,128]{3,2,1,0:T(1,128)S(1)}, f32[8,18,1,128]{3,2,1,0:T(1,128)S(1)}, u32[]{:S(2)}, u32[]{:S(2)}) collective-permute-start(f32[8,18,1,128]{3,2,1,0:T(1,128)S(1)} %get-tuple-element.207), channel_id=1, source_target_pairs={{1,0},{2,1},{3,2},{0,3},{5,4},{6,5},{7,6},{4,7},{9,8},{10,9},{11,1... | collective-permute-start | bytes 221192 | tf_op jit(solution)/shard_map/ppermute | solution.py:31
  89.0 0.1 pad_maximum_fusion.2
  89.1 0.1 multiply_reduce_fusion.6
  89.2 0.1 fusion.68
  89.7 0.3 fusion.9
  90.0 1.3 %collective-permute-done.4 = f32[8,18,1,128]{3,2,1,0:T(1,128)S(1)} collective-permute-done((f32[8,18,1,128]{3,2,1,0:T(1,128)S(1)}, f32[8,18,1,128]{3,2,1,0:T(1,128)S(1)}, u32[]{:S(2)}, u32[]{:S(2)}) %collective-permute-start.4) | collective-permute-done | bytes 73760 | tf_op jit(solution)/shard_map/ppermute | solution.py:29
  91.3 0.1 collective-permute-done.5
  91.4 0.2 broadcast_select_fusion.1
  91.6 0.3 pad_maximum_fusion.1
  91.9 0.2 multiply_reduce_fusion.3
  92.2 0.1 fusion.51
  92.6 0.1 fusion.53
  92.7 0.6 fusion.6
  93.3 1.5 %fusion.17 = f32[1,8,16,16,128]{4,3,2,1,0:T(8,128)} fusion(f32[8,16,16,128]{3,2,1,0:T(8,128)S(1)} %get-tuple-element.175, f32[8,16,16,129]{3,2,1,0:T(8,128)S(1)} %fusion.3, f32[8,16,17,128]{3,2,1,0:T(8,128)S(1)} %fusion.6, f32[8,17,16,128]{3,2,1,0:T(8,128)S(1)} %fusion.9, f32[]{:T(128)S(6)} %select_n.184), kind=kLoop, calls=%fused_computation.30 | loop fusion | flops 1835008 | bytes 8388612 | tf_op jit(solution)/shard_map/broadcast_in_dim | solution.py:187
  (41 shorter events, 1.3 us)
Async XLA Ops:
  1.8 1.8 %copy-start.1 = (s32[1,4,8]{2,1,0:T(4,128)S(1)}, s32[1,4,8]{2,1,0:T(4,128)}, u32[]{:S(2)}) copy-start(s32[1,4,8]{2,1,0:T(4,128)} %param.8) | copy-start | bytes 388
  1.9 7.2 %copy-start.2 = (s32[1,1,2,4]{3,2,1,0:T(2,128)S(1)}, s32[1,1,2,4]{3,2,1,0:T(2,128)}, u32[]{:S(2)}) copy-start(s32[1,1,2,4]{3,2,1,0:T(2,128)} %param.9) | copy-start | bytes 100
  4.2 14.6 %collective-permute-start.1 = (bf16[4,2,4096]{2,1,0:T(2,128)(2,1)S(1)}, bf16[4,2,4096]{2,1,0:T(2,128)(2,1)}, u32[]{:S(2)}, u32[]{:S(2)}) collective-permute-start(bf16[4,2,4096]{2,1,0:T(2,128)(2,1)S(1)} %reshape.140), channel_id=1, source_target_pairs={{0,16},{1,17},{2,18},{3,19},{4,20},{5,21},{6,22},{7,23},{8,24},{9,... | collective-permute-start | bytes 196616 | tf_op jit(solution)/shard_map/ppermute | solution.py:19
  7.7 2.1 %collective-permute-start = (s32[4,2]{1,0:T(4,128)S(1)}, s32[4,2]{1,0:T(4,128)S(1)}, u32[]{:S(2)}, u32[]{:S(2)}) collective-permute-start(s32[4,2]{1,0:T(4,128)S(1)} %select_n.183), channel_id=1, source_target_pairs={{0,16},{1,17},{2,18},{3,19},{4,20},{5,21},{6,22},{7,23},{8,24},{9,... | collective-permute-start | bytes 104 | tf_op jit(solution)/shard_map/ppermute | solution.py:19
  18.8 8.1 %all-to-all-start.1 = ((bf16[4,2,4096]{2,1,0:T(2,128)(2,1)}), bf16[4,2,4096]{2,1,0:T(2,128)(2,1)S(1)}, u32[]{:S(2)}, u32[]{:S(2)}) async-start(bf16[4,2,4096]{2,1,0:T(2,128)(2,1)} %collective-permute-done.1), calls=%async_computation.1 | async-start | bytes 131072 | tf_op jit(solution)/shard_map/all_to_all | solution.py:142
  27.2 2.8 %copy-start = (s32[1,1,2]{2,1,0:T(1,128)S(1)}, s32[1,1,2]{2,1,0:T(1,128)}, u32[]{:S(2)}) copy-start(s32[1,1,2]{2,1,0:T(1,128)} %param.10) | copy-start | bytes 28
  79.3 6.2 %collective-permute-start.2 = (f32[8,1,16,128]{3,2,1,0:T(8,128)S(1)}, f32[8,1,16,128]{3,2,1,0:T(8,128)S(1)}, u32[]{:S(2)}, u32[]{:S(2)}) collective-permute-start(f32[8,1,16,128]{3,2,1,0:T(8,128)S(1)} %get-tuple-element.213), channel_id=1, source_target_pairs={{0,4},{4,8},{8,12},{12,0},{1,5},{5,9},{9,13},{13,1},{2,6},{6,10},{... | collective-permute-start | bytes 196616 | tf_op jit(solution)/shard_map/ppermute | solution.py:29
  80.9 5.0 %collective-permute-start.3 = (f32[8,1,16,128]{3,2,1,0:T(8,128)S(1)}, f32[8,1,16,128]{3,2,1,0:T(8,128)S(1)}, u32[]{:S(2)}, u32[]{:S(2)}) collective-permute-start(f32[8,1,16,128]{3,2,1,0:T(8,128)S(1)} %get-tuple-element.212), channel_id=1, source_target_pairs={{4,0},{8,4},{12,8},{0,12},{5,1},{9,5},{13,9},{1,13},{6,2},{10,6},{... | collective-permute-start | bytes 196616 | tf_op jit(solution)/shard_map/ppermute | solution.py:31
  86.0 5.3 %collective-permute-start.4 = (f32[8,18,1,128]{3,2,1,0:T(1,128)S(1)}, f32[8,18,1,128]{3,2,1,0:T(1,128)S(1)}, u32[]{:S(2)}, u32[]{:S(2)}) collective-permute-start(f32[8,18,1,128]{3,2,1,0:T(1,128)S(1)} %get-tuple-element.206), channel_id=1, source_target_pairs={{0,1},{1,2},{2,3},{3,0},{4,5},{5,6},{6,7},{7,4},{8,9},{9,10},{10,1... | collective-permute-start | bytes 221192 | tf_op jit(solution)/shard_map/ppermute | solution.py:29
  86.8 4.6 %collective-permute-start.5 = (f32[8,18,1,128]{3,2,1,0:T(1,128)S(1)}, f32[8,18,1,128]{3,2,1,0:T(1,128)S(1)}, u32[]{:S(2)}, u32[]{:S(2)}) collective-permute-start(f32[8,18,1,128]{3,2,1,0:T(1,128)S(1)} %get-tuple-element.207), channel_id=1, source_target_pairs={{1,0},{2,1},{3,2},{0,3},{5,4},{6,5},{7,6},{4,7},{9,8},{10,9},{11,1... | collective-permute-start | bytes 221192 | tf_op jit(solution)/shard_map/ppermute | solution.py:31
where the time goes:
time: 95.2 us; the launch traced here: 94.8 us
  local copies, waits for them, and re-layouts  43.2 us (45%)
  starting transfers between devices  14.4 us (15%)
  other arithmetic  10.6 us (11%)
  blocking collectives  8.98 us (9%)
  loops' own time  7.15 us (8%)
  waiting for transfers between devices  6.93 us (7%)
  matrix products  3.19 us (3%)
    dynamic_update_slice x2, local copies, waits for them, and re-layouts, place_block(): lax.dynamic_update_slice(grid_now, jnp.where(live_slot, new_block, old_bl...  37.6 us
    all_to_all x1, blocking collectives, local(): lax.all_to_all(moved_pair[1], 'yz', split_axis=0, concat_axis=0, tiled=True)  8.98 us
    another operation x1, loops' own time, local(): grid_cells = lax.fori_loop(0, slots_here, place_block, grid_cells)  7.15 us
    ppermute x2, starting transfers between devices, extended(): lax.ppermute(head, axis, [((i + 1) % count, i) for i in range(count)])  4.43 us
    ppermute x2, starting transfers between devices, shifted(): return lax.ppermute(block, axis, route)  4.27 us
    all_to_all x1, waiting for transfers between devices, local(): lax.all_to_all(moved_pair[0], 'yz', split_axis=0, concat_axis=0, tiled=True)  3.53 us
    all_to_all x1, starting transfers between devices, local(): lax.all_to_all(moved_pair[0], 'yz', split_axis=0, concat_axis=0, tiled=True)  3.28 us
    dot_general x1, matrix products, local(): jnp.einsum('jkcs,jkst->jct', picked, interp_weights[0, 0], preferred_elem...  2.83 us
  transfers between devices with their start and end apart: 7, of which 6 were waited for; matrix products, arithmetic and copies ran while one was open for 4% of the time, Pallas kernels for 0%

commit v1 on v0

v1 whole, which is shorter than its diff:
```python
import functools

import jax
import jax.numpy as jnp
from jax import lax
from jax.experimental import pallas as pl
from jax.experimental.pallas import tpu as pltpu
from jax.sharding import PartitionSpec as P

BLK = 8
SR = 2
CAP = 2
LANES = 128

HEAT_RATIO = 5.0 / 3.0
CORONA_RATIO = 0.04
HELIO_RATIO = 0.03

VM = pl.BlockSpec(memory_space=pltpu.VMEM)
SM = pl.BlockSpec(memory_space=pltpu.SMEM)


def partner(index, step, count):
    if count & (count - 1) == 0:
        return index ^ step
    return (index + step) % count


def sender(index, step, count):
    if count & (count - 1) == 0:
        return index ^ step
    return (index - step + count) % count


def pack_kernel(dims, owner_ref, grid_ref, *rest):
    ncomp, len_x, len_y, len_z, n_yz, shells = dims
    outs, (blocks, send) = rest[:n_yz], rest[n_yz:]
    me = lax.axis_index("yz")

    @pl.when(lax.axis_index("dom") == 0)
    def _():
        n_bx, n_by, half = len_x // BLK, len_y // BLK, BLK // 2
        plane = len_x * len_y
        z_from = len_z - SR * BLK
        row_z = lax.broadcasted_iota(jnp.int32, (LANES, SR * LANES), 0) + (len_z - LANES)
        column = lax.broadcasted_iota(jnp.int32, (LANES, SR * LANES), 1)
        hit = row_z == z_from + column // LANES * BLK + column % BLK
        place = column % LANES // BLK
        total = jnp.zeros((n_bx * n_by * half * ncomp, SR * LANES), jnp.float32)
        for ap in range(2):
            for cy in range(BLK):
                pieces = []
                for bx in range(n_bx):
                    for by in range(n_by):
                        for a2 in range(half):
                            first = (bx * BLK + a2 * 2 + ap) * len_y + by * BLK + cy
                            pieces.append(grid_ref[pl.ds(first, ncomp, stride=plane), :])
                cells = jnp.concatenate(pieces, axis=0).astype(jnp.bfloat16)
                pick = jnp.where(hit & (place == ap * BLK + cy), 1.0, 0.0).astype(jnp.bfloat16)
                total = total + jnp.dot(cells, pick, preferred_element_type=jnp.float32)
        rows = half * ncomp
        for column_block in range(n_bx * n_by):
            for br in range(SR):
                blocks[column_block * SR + br] = total[
                    column_block * rows : (column_block + 1) * rows, br * LANES : (br + 1) * LANES
                ].astype(jnp.bfloat16)
        send[...] = jnp.zeros_like(send)
        for b in range(shells):
            owner = owner_ref[me * shells + b]
            rank = jnp.int32(0)
            for other in range(b):
                rank = rank + jnp.where(owner_ref[me * shells + other] == owner, 1, 0)
            if n_yz & (n_yz - 1) == 0:
                step = owner ^ me
            else:
                step = lax.rem(owner - me + n_yz, n_yz)
            spot = jnp.clip(step * CAP + rank, 0, n_yz * CAP - 1)
            send[spot] = blocks[b]
        for step in range(n_yz):
            for slot in range(CAP):
                outs[step][slot * rows : (slot + 1) * rows, :] = send[step * CAP + slot]


def fill_kernel(dims, owner_ref, source_ref, target_ref, weight_ref, grid_ref, *rest):
    ncomp, len_x, len_y, len_z, n_yz, shells, slots, depth = dims
    got = rest[:n_yz]
    filled, x_low, x_high, y_low, y_high, held, result, table = rest[n_yz:]
    me = lax.axis_index("yz")
    half = BLK // 2
    rows = half * ncomp
    plane = len_x * len_y

    filled[...] = grid_ref[...]

    @pl.when(lax.axis_index("dom") == 1)
    def _():
        for step in range(n_yz):
            for slot in range(CAP):
                held[step * CAP + slot] = got[step][slot * rows : (slot + 1) * rows, :].astype(jnp.float32)
        position = jnp.int32(0)
        for t in range(n_yz):
            if n_yz & (n_yz - 1) == 0:
                step = t ^ me
            else:
                step = lax.rem(me - t + n_yz, n_yz)
            rank = jnp.int32(0)
            for b in range(shells):
                table[jnp.minimum(position, n_yz * CAP)] = step * CAP + jnp.minimum(rank, CAP - 1)
                mine = jnp.where(owner_ref[t * shells + b] == me, 1, 0)
                position = position + mine
                rank = rank + mine
        lines = []
        for j in range(slots):
            total = jnp.zeros((ncomp, BLK * BLK * BLK), jnp.float32)
            for k in range(depth):
                entry = source_ref[j * depth + k]
                live = entry >= 0
                spot = jnp.where(live, table[jnp.clip(entry, 0, n_yz * CAP)], 0)
                block = held[spot]
                cells = jnp.concatenate(
                    [block[a2 * ncomp : (a2 + 1) * ncomp, :] for a2 in range(half)], axis=1
                )
                cells = jnp.where(live, cells, 0.0).astype(jnp.bfloat16)
                total = total + jnp.dot(
                    cells, weight_ref[j * depth + k], preferred_element_type=jnp.float32
                )
            lines += [total[:, a2 * LANES : (a2 + 1) * LANES] for a2 in range(half)]
        lines = jnp.concatenate(lines, axis=0)
        top = lines.astype(jnp.bfloat16)
        rest = lines - top.astype(jnp.float32)
        middle = rest.astype(jnp.bfloat16)
        bottom = (rest - middle.astype(jnp.float32)).astype(jnp.bfloat16)
        lines = jnp.concatenate([top, middle, bottom], axis=0)
        count = slots * rows
        from_lane = lax.broadcasted_iota(jnp.int32, (LANES, LANES), 0)
        to_lane = lax.broadcasted_iota(jnp.int32, (LANES, LANES), 1)
        same = from_lane % BLK == to_lane % BLK
        for m in range(2 * BLK):
            spread = jnp.where(same & (from_lane // BLK == m), 1.0, 0.0).astype(jnp.bfloat16)
            parts = jnp.dot(lines, spread, preferred_element_type=jnp.float32)
            result[m] = parts[:count] + parts[count : 2 * count] + parts[2 * count :]
        lane = lax.broadcasted_iota(jnp.int32, (ncomp, LANES), 1)
        per_y, per_z = len_y // BLK, len_z // BLK
        for j in range(slots):
            target = target_ref[j]

            @pl.when(target >= 0)
            def _():
                block_x = target // (per_y * per_z)
                block_y = target // per_z % per_y
                z_from = target % per_z * BLK
                inside = (lane >= z_from) & (lane < z_from + BLK)
                first = block_x * BLK * len_y + block_y * BLK
                for a in range(BLK):
                    for cy in range(BLK):
                        spot = pl.ds(first + a * len_y + cy, ncomp, stride=plane)
                        row = j * rows + a // 2 * ncomp
                        new = result[a % 2 * BLK + cy, row : row + ncomp, :]
                        filled[spot, :] = jnp.where(inside, new, filled[spot, :])

    for c in range(ncomp):
        x_low[c * len_y : (c + 1) * len_y, :] = filled[c * plane : c * plane + len_y, :]
        x_high[c * len_y : (c + 1) * len_y, :] = filled[(c + 1) * plane - len_y : (c + 1) * plane, :]
        y_low[c * len_x : (c + 1) * len_x, :] = filled[pl.ds(c * plane, len_x, stride=len_y), :]
        y_high[c * len_x : (c + 1) * len_x, :] = filled[
            pl.ds(c * plane + len_y - 1, len_x, stride=len_y), :
        ]


def primitives(cells):
    density, energy = cells[0], cells[7]
    momentum, magnetic = cells[1:4], cells[4:7]
    inverse = 1.0 / density
    velocity = [m * inverse for m in momentum]
    field_sq = magnetic[0] * magnetic[0] + magnetic[1] * magnetic[1] + magnetic[2] * magnetic[2]
    kinetic = momentum[0] * velocity[0] + momentum[1] * velocity[1] + momentum[2] * velocity[2]
    pressure = (HEAT_RATIO - 1.0) * (energy - 0.5 * kinetic - 0.5 * field_sq)
    total_pressure = pressure + 0.5 * field_sq
    dot = velocity[0] * magnetic[0] + velocity[1] * magnetic[1] + velocity[2] * magnetic[2]
    fast = jnp.sqrt((HEAT_RATIO * pressure + field_sq) * inverse)
    return velocity, total_pressure, energy + total_pressure, dot, fast


def flux_of(cells, prims, direction):
    velocity, total_pressure, enthalpy, dot, fast = prims
    momentum, magnetic = cells[1:4], cells[4:7]
    speed, field = velocity[direction], magnetic[direction]
    flux = [momentum[direction]]
    for other in range(3):
        term = momentum[other] * speed - magnetic[other] * field
        flux.append(term + total_pressure if other == direction else term)
    for other in range(3):
        if other == direction:
            flux.append(None)
        else:
            flux.append(speed * magnetic[other] - field * velocity[other])
    flux.append(enthalpy * speed - field * dot)
    return flux, jnp.abs(speed) + fast


def face_sum(low, high):
    fastest = jnp.maximum(low[2], high[2])
    out = []
    for u_low, u_high, f_low, f_high in zip(low[0], high[0], low[1], high[1]):
        face = fastest * (u_high - u_low)
        out.append(face if f_low is None else face - (f_low + f_high))
    return out


def inner_kernel(dims, filled, out):
    ncomp, len_x, len_y, len_z = dims
    plane = len_x * len_y
    half_ratio = jnp.where(lax.axis_index("dom") == 0, 0.5 * CORONA_RATIO, 0.5 * HELIO_RATIO).astype(jnp.float32)
    shape = (len_y, LANES)
    row = lax.broadcasted_iota(jnp.int32, shape, 0)
    lane = lax.broadcasted_iota(jnp.int32, shape, 1)

    def load(x):
        return [filled[pl.ds(pl.multiple_of(c * plane + x * len_y, BLK), len_y), :] for c in range(ncomp)]

    def shift_up(values, axis, size):
        return [None if v is None else pltpu.roll(v, size - 1, axis) for v in values]

    def step(x, carry, last):
        cells, prims, flux_x, speed_x, low_x = carry
        if last:
            high_x = [jnp.zeros(shape, jnp.float32)] * ncomp
            next_carry = None
        else:
            next_cells = load(x + 1)
            next_prims = primitives(next_cells)
            next_flux, next_speed = flux_of(next_cells, next_prims, 0)
            high_x = face_sum((cells, flux_x, speed_x), (next_cells, next_flux, next_speed))
            next_carry = (next_cells, next_prims, next_flux, next_speed, high_x)
        total = [high - low for high, low in zip(high_x, low_x)]
        flux, speed = flux_of(cells, prims, 1)
        beside = (shift_up(cells, 0, len_y), shift_up(flux, 0, len_y), pltpu.roll(speed, len_y - 1, 0))
        for c, face in enumerate(face_sum((cells, flux, speed), beside)):
            face = jnp.where(row == len_y - 1, 0.0, face)
            total[c] = total[c] + (face - pltpu.roll(face, 1, 0))
        flux, speed = flux_of(cells, prims, 2)
        beside = (shift_up(cells, 1, LANES), shift_up(flux, 1, LANES), pltpu.roll(speed, LANES - 1, 1))
        for c, face in enumerate(face_sum((cells, flux, speed), beside)):
            own = jnp.zeros(shape, jnp.float32) if flux[c] is None else -2.0 * flux[c]
            face = jnp.where(lane == LANES - 1, own, face)
            below = jnp.where(lane == 0, own, pltpu.roll(face, 1, 1))
            total[c] = total[c] + (face - below)
        for c in range(ncomp):
            spot = pl.ds(pl.multiple_of(c * plane + x * len_y, BLK), len_y)
            out[spot, :] = cells[c] + half_ratio * total[c]
        return next_carry

    cells = load(0)
    prims = primitives(cells)
    flux, speed = flux_of(cells, prims, 0)
    flux[4] = None
    zero = [jnp.zeros(shape, jnp.float32)] * ncomp
    carry = (cells, prims, flux, speed, zero)

    def pack(carry):
        cells, prims, flux, speed, low = carry
        return cells, prims, [f for f in flux if f is not None], speed, low

    def unpack(carry):
        cells, prims, flux, speed, low = carry
        return cells, prims, flux[:4] + [None] + flux[4:], speed, low

    carry = lax.fori_loop(
        0, len_x - 1, lambda x, carry: pack(step(x, unpack(carry), False)), pack(carry)
    )
    step(len_x - 1, unpack(carry), True)


def edge_kernel(dims, part, x_low, x_high, y_low, y_high, from_x_low, from_x_high, from_y_low, from_y_high, out):
    ncomp, len_x, len_y, len_z = dims
    plane = len_x * len_y
    helio = lax.axis_index("dom") == 1
    column, line = lax.axis_index("gx"), lax.axis_index("yz")
    half_ratio = jnp.where(helio, 0.5 * HELIO_RATIO, 0.5 * CORONA_RATIO).astype(jnp.float32)
    out[...] = part[...]

    def state(cells, direction):
        flux, speed = flux_of(cells, primitives(cells), direction)
        return cells, flux, speed

    def faces(own_ref, other_ref, at_end, direction, upper, size):
        own = [own_ref[c * size : (c + 1) * size, :] for c in range(ncomp)]
        other = [other_ref[c * size : (c + 1) * size, :] for c in range(ncomp)]
        other = [jnp.where(at_end, u, v) for u, v in zip(own, other)]
        own, other = state(own, direction), state(other, direction)
        if upper:
            return [half_ratio * f for f in face_sum(own, other)]
        return [-half_ratio * f for f in face_sum(other, own)]

    low_end = helio & (column == 0)
    high_end = helio & (column == lax.axis_size("gx") - 1)
    for c, change in enumerate(faces(x_low, from_x_low, low_end, 0, False, len_y)):
        spot = pl.ds(c * plane, len_y)
        out[spot, :] = out[spot, :] + change
    for c, change in enumerate(faces(x_high, from_x_high, high_end, 0, True, len_y)):
        spot = pl.ds((c + 1) * plane - len_y, len_y)
        out[spot, :] = out[spot, :] + change
    low_end = line == 0
    high_end = line == lax.axis_size("yz") - 1
    for c, change in enumerate(faces(y_low, from_y_low, low_end, 1, False, len_x)):
        spot = pl.ds(c * plane, len_x, stride=len_y)
        out[spot, :] = out[spot, :] + change
    for c, change in enumerate(faces(y_high, from_y_high, high_end, 1, True, len_x)):
        spot = pl.ds(c * plane + len_y - 1, len_x, stride=len_y)
        out[spot, :] = out[spot, :] + change


def local(field_state, shell_owner, block_sources, block_targets, interp_weights):
    _, ncomp, len_x, len_y, len_z = field_state.shape
    n_gx, n_yz = lax.axis_size("gx"), lax.axis_size("yz")
    shells = shell_owner.shape[2]
    slots, depth = block_sources.shape[2:]
    volume = BLK * BLK * BLK
    cell_rows = ncomp * len_x * len_y
    grid = field_state.reshape(cell_rows, len_z)
    owners = shell_owner.reshape(-1)
    sources = block_sources.reshape(-1)
    targets = block_targets.reshape(-1)
    weights = interp_weights.reshape(slots * depth, volume, volume)
    rows = BLK // 2 * ncomp
    dims = (ncomp, len_x, len_y, len_z)

    packed = pl.pallas_call(
        functools.partial(pack_kernel, dims + (n_yz, shells)),
        out_shape=[jax.ShapeDtypeStruct((CAP * rows, LANES), jnp.bfloat16)] * n_yz,
        in_specs=[SM, VM],
        out_specs=[VM] * n_yz,
        scratch_shapes=[
            pltpu.VMEM((shells, rows, LANES), jnp.bfloat16),
            pltpu.VMEM((n_yz * CAP, rows, LANES), jnp.bfloat16),
        ],
        name="pack_shell",
    )(owners, grid)

    moved = []
    for step in range(n_yz):
        pairs = [(t, n_yz + partner(t, step, n_yz)) for t in range(n_yz)]
        pairs = pairs + [(b, a) for a, b in pairs]
        moved.append(lax.ppermute(packed[step], ("dom", "yz"), pairs))

    face_x = jax.ShapeDtypeStruct((ncomp * len_y, len_z), jnp.float32)
    face_y = jax.ShapeDtypeStruct((ncomp * len_x, len_z), jnp.float32)
    filled, x_low, x_high, y_low, y_high = pl.pallas_call(
        functools.partial(fill_kernel, dims + (n_yz, shells, slots, depth)),
        out_shape=[jax.ShapeDtypeStruct((cell_rows, len_z), jnp.float32), face_x, face_x, face_y, face_y],
        in_specs=[SM, SM, SM, VM, VM] + [VM] * n_yz,
        out_specs=[VM] * 5,
        scratch_shapes=[
            pltpu.VMEM((n_yz * CAP, rows, LANES), jnp.float32),
            pltpu.VMEM((2 * BLK, slots * rows, LANES), jnp.float32),
            pltpu.SMEM((n_yz * CAP + 1,), jnp.int32),
        ],
        compiler_params=pltpu.CompilerParams(vmem_limit_bytes=24 * 2**20),
        name="fill_blocks",
    )(owners, sources, targets, weights, grid, *moved)

    up_x = [(i, (i + 1) % n_gx) for i in range(n_gx)]
    down_x = [(b, a) for a, b in up_x]
    up_y = [(i, (i + 1) % n_yz) for i in range(n_yz)]
    down_y = [(b, a) for a, b in up_y]
    from_x_low = lax.ppermute(x_high, "gx", up_x)
    from_x_high = lax.ppermute(x_low, "gx", down_x)
    from_y_low = lax.ppermute(y_high, "yz", up_y)
    from_y_high = lax.ppermute(y_low, "yz", down_y)

    part = pl.pallas_call(
        functools.partial(inner_kernel, dims),
        out_shape=jax.ShapeDtypeStruct((cell_rows, len_z), jnp.float32),
        in_specs=[VM],
        out_specs=VM,
        cost_estimate=pl.CostEstimate(flops=300 * cell_rows * len_z, bytes_accessed=8 * cell_rows * len_z, transcendentals=0),
        name="inner_faces",
    )(filled)

    updated = pl.pallas_call(
        functools.partial(edge_kernel, dims),
        out_shape=jax.ShapeDtypeStruct((cell_rows, len_z), jnp.float32),
        in_specs=[VM] * 9,
        out_specs=VM,
        name="edge_faces",
    )(part, x_low, x_high, y_low, y_high, from_x_low, from_x_high, from_y_low, from_y_high)
    return updated.reshape(1, ncomp, len_x, len_y, len_z)


def solution(mesh):
    placed = (
        P("dom", None, "gx", "yz", None),
        P("gx", None, None),
        P("gx", "yz", None, None),
        P("gx", "yz", None),
        P("gx", "yz", None, None, None, None),
    )
    return jax.shard_map(
        local,
        mesh=mesh,
        in_specs=placed,
        out_specs=P("dom", None, "gx", "yz", None),
        check_vma=False,
    )
```

time: 95.2 us -> 35 us (0.37)
  the two profiles are of different devices: /device:TPU:0 before, /device:TPU:1 now
where the time goes in v1:
time: 35 us; the launch traced here: 34.7 us
  Pallas kernels  12.2 us (35%)
  starting transfers between devices  9.78 us (28%)
  local copies, waits for them, and re-layouts  9.08 us (26%)
  waiting for transfers between devices  3.52 us (10%)
    unnamed x26, local copies, waits for them, and re-layouts  6.97 us
    pallas_call x1, Pallas kernels, local(): pl.pallas_call(functools.partial(inner_kernel, dims), out_shape=jax.Shape...  5.23 us
    ppermute x4, starting transfers between devices, local(): moved.append(lax.ppermute(packed[step], ('dom', 'yz'), pairs))  4.95 us
    ppermute x4, waiting for transfers between devices, local(): moved.append(lax.ppermute(packed[step], ('dom', 'yz'), pairs))  3.51 us
    ppermute x1, starting transfers between devices, local(): from_x_high = lax.ppermute(x_low, 'gx', down_x)  3.36 us
    pallas_call x1, Pallas kernels, local(): pl.pallas_call(functools.partial(edge_kernel, dims), out_shape=jax.ShapeD...  2.71 us
    pallas_call x1, Pallas kernels, local(): pl.pallas_call(functools.partial(fill_kernel, dims + (n_yz, shells, slots...  2.37 us
    pallas_call x1, Pallas kernels, local(): pl.pallas_call(functools.partial(pack_kernel, dims + (n_yz, shells)), out...  1.86 us
  transfers between devices with their start and end apart: 8, of which 2 were waited for; matrix products, arithmetic and copies ran while one was open for 2% of the time, Pallas kernels for 15%

profile of v1, /device:TPU:1, one launch (start us, length us, event | category | flops | bytes accessed | tf_op | source)
XLA Modules:
  0.0 34.7 jit_solution(4806462364467381454)
XLA Ops:
  0.0 1.4 %reshape.18.owner_ref = s32[32]{0:T(128)} reshape(s32[1,4,8]{2,1,0:T(4,128)} %param.6) | data formatting | bytes 256 | tf_op jit(solution)/shard_map/reshape | solution.py:321
  1.4 1.9 %pack_shell.1 = (bf16[64,128]{1,0:T(8,128)(2,1)}, bf16[64,128]{1,0:T(8,128)(2,1)}, bf16[64,128]{1,0:T(8,128)(2,1)}, bf16[64,128]{1,0:T(8,128)(2,1)}) custom-call(s32[32]{0:T(128)} %reshape.18.owner_ref, f32[2048,128]{1,0:T(8,128)} %bitcast.5), custom_call_target="tpu_custom_call" | custom-call | tf_op jit(solution)/shard_map/pack_shell/pallas_call | solution.py:328
  3.2 0.8 %collective-permute-start = (bf16[64,128]{1,0:T(8,128)(2,1)}, bf16[64,128]{1,0:T(8,128)(2,1)S(1)}, u32[]{:S(2)}, u32[]{:S(2)}) collective-permute-start(bf16[64,128]{1,0:T(8,128)(2,1)} %get-tuple-element.14), channel_id=1, source_target_pairs={{0,16},{1,17},{2,18},{3,19},{16,0},{17,1},{18,2},{19,3},{4,20},{5,... | collective-permute-start | bytes 49160 | tf_op jit(solution)/shard_map/ppermute | solution.py:344
  4.0 2.5 %collective-permute-start.1 = (bf16[64,128]{1,0:T(8,128)(2,1)}, bf16[64,128]{1,0:T(8,128)(2,1)S(1)}, u32[]{:S(2)}, u32[]{:S(2)}) collective-permute-start(bf16[64,128]{1,0:T(8,128)(2,1)} %get-tuple-element.15), channel_id=1, source_target_pairs={{0,17},{1,16},{2,19},{3,18},{17,0},{16,1},{19,2},{18,3},{4,21},{5,... | collective-permute-start | bytes 49160 | tf_op jit(solution)/shard_map/ppermute | solution.py:344
  6.5 1.6 %collective-permute-start.2 = (bf16[64,128]{1,0:T(8,128)(2,1)}, bf16[64,128]{1,0:T(8,128)(2,1)S(1)}, u32[]{:S(2)}, u32[]{:S(2)}) collective-permute-start(bf16[64,128]{1,0:T(8,128)(2,1)} %get-tuple-element.16), channel_id=1, source_target_pairs={{0,18},{1,19},{2,16},{3,17},{18,0},{19,1},{16,2},{17,3},{4,22},{5,... | collective-permute-start | bytes 49160 | tf_op jit(solution)/shard_map/ppermute | solution.py:344
  8.2 0.0 collective-permute-start.3
  8.2 0.8 %reshape.19.source_ref = s32[8]{0:T(128)S(1)} reshape(s32[1,1,2,4]{3,2,1,0:T(2,128)} %param.7) | data formatting | bytes 64 | tf_op jit(solution)/shard_map/reshape | solution.py:322
  8.9 0.0 collective-permute-done.rest_0_
  8.9 0.0 collective-permute-done.1.rest_1_
  8.9 1.1 %collective-permute-done.2.rest_2_ = bf16[64,128]{1,0:T(8,128)(2,1)S(1)} collective-permute-done((bf16[64,128]{1,0:T(8,128)(2,1)}, bf16[64,128]{1,0:T(8,128)(2,1)S(1)}, u32[]{:S(2)}, u32[]{:S(2)}) %collective-permute-start.2) | collective-permute-done | bytes 16416 | tf_op jit(solution)/shard_map/ppermute | solution.py:344
  10.0 2.4 %collective-permute-done.3.rest_3_ = bf16[64,128]{1,0:T(8,128)(2,1)S(1)} collective-permute-done((bf16[64,128]{1,0:T(8,128)(2,1)}, bf16[64,128]{1,0:T(8,128)(2,1)S(1)}, u32[]{:S(2)}, u32[]{:S(2)}) %collective-permute-start.3) | collective-permute-done | bytes 16416 | tf_op jit(solution)/shard_map/ppermute | solution.py:344
  12.4 0.0 copy-start
  12.4 2.2 %copy-done = bf16[1,1,2,4,512,512]{5,4,3,2,1,0:T(8,128)(2,1)S(1)} copy-done((bf16[1,1,2,4,512,512]{5,4,3,2,1,0:T(8,128)(2,1)S(1)}, bf16[1,1,2,4,512,512]{5,4,3,2,1,0:T(8,128)(2,1)}, u32[]{:S(2)}) %copy-start) | copy-done | bytes 4194328
  14.6 0.0 copy-start.1
  14.6 1.2 %copy-done.1 = f32[1,8,16,16,128]{4,3,2,1,0:T(8,128)S(1)} copy-done((f32[1,8,16,16,128]{4,3,2,1,0:T(8,128)S(1)}, f32[1,8,16,16,128]{4,3,2,1,0:T(8,128)}, u32[]{:S(2)}) %copy-start.1) | copy-done | bytes 1048600
  15.9 0.0 copy-start.7
  15.9 0.7 %copy-done.7 = s32[32]{0:T(128)S(1)} copy-done((s32[32]{0:T(128)S(1)}, s32[32]{0:T(128)}, u32[]{:S(2)}) %copy-start.7) | copy-done | bytes 152
  16.5 0.0 copy-start.8
  16.5 0.7 %copy-done.8 = s32[1,1,2]{2,1,0:T(1,128)S(1)} copy-done((s32[1,1,2]{2,1,0:T(1,128)S(1)}, s32[1,1,2]{2,1,0:T(1,128)}, u32[]{:S(2)}) %copy-start.8) | copy-done | bytes 32
  17.2 2.4 %fill_blocks.1 = (f32[2048,128]{1,0:T(8,128)S(1)}, f32[128,128]{1,0:T(8,128)S(1)}, f32[128,128]{1,0:T(8,128)S(1)}, f32[128,128]{1,0:T(8,128)S(1)}, f32[128,128]{1,0:T(8,128)S(1)}) custom-call(s32[32]{0:T(128)S(1)} %copy-done.7, s32[8]{0:T(128)S(1)} %reshape.19.source_ref, s32[2]{0:T(128)S(1)} %bitcast.7, bf16[8,512,512]{2,1,0:T(8,128)(2,1)S(1)} %bitcast.4, ...), custom_call_target="tpu_custom_call" | custom-call | tf_op jit(solution)/shard_map/fill_blocks/pallas_call | solution.py:348
  19.6 0.0 copy-start.2
  19.6 1.0 %copy-done.2 = f32[2048,128]{1,0:T(8,128)} copy-done((f32[2048,128]{1,0:T(8,128)}, f32[2048,128]{1,0:T(8,128)S(1)}, u32[]{:S(2)}) %copy-start.2) | copy-done | bytes 1048600
  20.5 0.0 copy-start.3
  20.5 0.0 copy-start.4
  20.5 0.0 copy-start.5
  20.6 0.0 copy-start.6
  20.6 3.4 %collective-permute-start.5 = (f32[128,128]{1,0:T(8,128)S(1)}, f32[128,128]{1,0:T(8,128)S(1)}, u32[]{:S(2)}, u32[]{:S(2)}) collective-permute-start(f32[128,128]{1,0:T(8,128)S(1)} %get-tuple-element.19.x_low), channel_id=1, source_target_pairs={{4,0},{8,4},{12,8},{0,12},{5,1},{9,5},{13,9},{1,13},{6,2},{10,6},{... | collective-permute-start | bytes 196616 | tf_op jit(solution)/shard_map/ppermute | solution.py:367
  23.9 0.0 collective-permute-start.4
  23.9 0.2 collective-permute-start.7
  24.1 1.3 %collective-permute-start.6 = (f32[128,128]{1,0:T(8,128)S(1)}, f32[128,128]{1,0:T(8,128)S(1)}, u32[]{:S(2)}, u32[]{:S(2)}) collective-permute-start(f32[128,128]{1,0:T(8,128)S(1)} %get-tuple-element.22.y_high), channel_id=1, source_target_pairs={{0,1},{1,2},{2,3},{3,0},{4,5},{5,6},{6,7},{7,4},{8,9},{9,10},{10,1... | collective-permute-start | bytes 196616 | tf_op jit(solution)/shard_map/ppermute | solution.py:368
  25.4 5.2 %inner_faces.1.part = f32[2048,128]{1,0:T(8,128)} custom-call(f32[2048,128]{1,0:T(8,128)} %copy-done.2), custom_call_target="tpu_custom_call" | custom-call | flops 78643200 | bytes 2097152 | tf_op jit(solution)/shard_map/inner_faces/pallas_call | solution.py:371
  30.6 0.0 collective-permute-done.5.from_x_high
  30.6 0.0 copy-start.9
  30.6 0.0 collective-permute-done.4.from_x_low
  30.6 0.0 copy-start.10
  30.6 0.0 collective-permute-done.7.from_y_high
  30.6 0.0 copy-start.11
  30.7 0.0 collective-permute-done.6.from_y_low
  30.7 0.0 copy-done.3
  30.7 0.0 copy-done.4
  30.7 0.0 copy-done.5
  30.7 0.0 copy-done.6
  30.7 0.5 %copy-done.9 = f32[128,128]{1,0:T(8,128)} copy-done((f32[128,128]{1,0:T(8,128)}, f32[128,128]{1,0:T(8,128)S(1)}, u32[]{:S(2)}) %copy-start.9) | copy-done | bytes 65560
  31.2 0.0 copy-done.10
  31.3 0.0 copy-done.11
  31.3 0.0 copy-start.12
  31.3 0.6 %copy-done.12 = f32[128,128]{1,0:T(8,128)} copy-done((f32[128,128]{1,0:T(8,128)}, f32[128,128]{1,0:T(8,128)S(1)}, u32[]{:S(2)}) %copy-start.12) | copy-done | bytes 65560
  31.9 2.7 %edge_faces.1 = f32[2048,128]{1,0:T(8,128)} custom-call(f32[2048,128]{1,0:T(8,128)} %inner_faces.1.part, f32[128,128]{1,0:T(8,128)} %copy-done.3, f32[128,128]{1,0:T(8,128)} %copy-done.4, f32[128,128]{1,0:T(8,128)} %copy-done.5, f32[128,128]{1,0:T(8,128)} %copy-done.6, f32[128,128]{1,0:T(8,128)} %copy-done.10, f32[128,128]{1,0:T(8,128)} %copy-done.9, ...), custom_call_target="tpu_custom_call" | custom-call | tf_op jit(solution)/shard_map/edge_faces/pallas_call | solution.py:380
Async XLA Ops:
  3.2 5.7 %collective-permute-start = (bf16[64,128]{1,0:T(8,128)(2,1)}, bf16[64,128]{1,0:T(8,128)(2,1)S(1)}, u32[]{:S(2)}, u32[]{:S(2)}) collective-permute-start(bf16[64,128]{1,0:T(8,128)(2,1)} %get-tuple-element.14), channel_id=1, source_target_pairs={{0,16},{1,17},{2,18},{3,19},{16,0},{17,1},{18,2},{19,3},{4,20},{5,... | collective-permute-start | bytes 49160 | tf_op jit(solution)/shard_map/ppermute | solution.py:344
  4.0 4.9 %collective-permute-start.1 = (bf16[64,128]{1,0:T(8,128)(2,1)}, bf16[64,128]{1,0:T(8,128)(2,1)S(1)}, u32[]{:S(2)}, u32[]{:S(2)}) collective-permute-start(bf16[64,128]{1,0:T(8,128)(2,1)} %get-tuple-element.15), channel_id=1, source_target_pairs={{0,17},{1,16},{2,19},{3,18},{17,0},{16,1},{19,2},{18,3},{4,21},{5,... | collective-permute-start | bytes 49160 | tf_op jit(solution)/shard_map/ppermute | solution.py:344
  6.5 3.5 %collective-permute-start.2 = (bf16[64,128]{1,0:T(8,128)(2,1)}, bf16[64,128]{1,0:T(8,128)(2,1)S(1)}, u32[]{:S(2)}, u32[]{:S(2)}) collective-permute-start(bf16[64,128]{1,0:T(8,128)(2,1)} %get-tuple-element.16), channel_id=1, source_target_pairs={{0,18},{1,19},{2,16},{3,17},{18,0},{19,1},{16,2},{17,3},{4,22},{5,... | collective-permute-start | bytes 49160 | tf_op jit(solution)/shard_map/ppermute | solution.py:344
  8.2 4.3 %collective-permute-start.3 = (bf16[64,128]{1,0:T(8,128)(2,1)}, bf16[64,128]{1,0:T(8,128)(2,1)S(1)}, u32[]{:S(2)}, u32[]{:S(2)}) collective-permute-start(bf16[64,128]{1,0:T(8,128)(2,1)} %get-tuple-element.17), channel_id=1, source_target_pairs={{0,19},{1,18},{2,17},{3,16},{19,0},{18,1},{17,2},{16,3},{4,23},{5,... | collective-permute-start | bytes 49160 | tf_op jit(solution)/shard_map/ppermute | solution.py:344
  12.4 2.2 %copy-start = (bf16[1,1,2,4,512,512]{5,4,3,2,1,0:T(8,128)(2,1)S(1)}, bf16[1,1,2,4,512,512]{5,4,3,2,1,0:T(8,128)(2,1)}, u32[]{:S(2)}) copy-start(bf16[1,1,2,4,512,512]{5,4,3,2,1,0:T(8,128)(2,1)} %param.9) | copy-start | bytes 12582916
  14.6 1.2 %copy-start.1 = (f32[1,8,16,16,128]{4,3,2,1,0:T(8,128)S(1)}, f32[1,8,16,16,128]{4,3,2,1,0:T(8,128)}, u32[]{:S(2)}) copy-start(f32[1,8,16,16,128]{4,3,2,1,0:T(8,128)} %param.5) | copy-start | bytes 3145732
  15.9 0.7 %copy-start.7 = (s32[32]{0:T(128)S(1)}, s32[32]{0:T(128)}, u32[]{:S(2)}) copy-start(s32[32]{0:T(128)} %reshape.18.owner_ref) | copy-start | bytes 388
  16.5 0.7 %copy-start.8 = (s32[1,1,2]{2,1,0:T(1,128)S(1)}, s32[1,1,2]{2,1,0:T(1,128)}, u32[]{:S(2)}) copy-start(s32[1,1,2]{2,1,0:T(1,128)} %param.8) | copy-start | bytes 28
  19.6 1.0 %copy-start.2 = (f32[2048,128]{1,0:T(8,128)}, f32[2048,128]{1,0:T(8,128)S(1)}, u32[]{:S(2)}) copy-start(f32[2048,128]{1,0:T(8,128)S(1)} %get-tuple-element.18.filled) | copy-start | bytes 3145732
  20.5 10.1 %copy-start.3 = (f32[128,128]{1,0:T(8,128)}, f32[128,128]{1,0:T(8,128)S(1)}, u32[]{:S(2)}) copy-start(f32[128,128]{1,0:T(8,128)S(1)} %get-tuple-element.19.x_low) | copy-start | bytes 196612
  20.5 10.1 %copy-start.4 = (f32[128,128]{1,0:T(8,128)}, f32[128,128]{1,0:T(8,128)S(1)}, u32[]{:S(2)}) copy-start(f32[128,128]{1,0:T(8,128)S(1)} %get-tuple-element.20.x_high) | copy-start | bytes 196612
  20.5 10.1 %copy-start.5 = (f32[128,128]{1,0:T(8,128)}, f32[128,128]{1,0:T(8,128)S(1)}, u32[]{:S(2)}) copy-start(f32[128,128]{1,0:T(8,128)S(1)} %get-tuple-element.21.y_low) | copy-start | bytes 196612
  20.6 10.2 %copy-start.6 = (f32[128,128]{1,0:T(8,128)}, f32[128,128]{1,0:T(8,128)S(1)}, u32[]{:S(2)}) copy-start(f32[128,128]{1,0:T(8,128)S(1)} %get-tuple-element.22.y_high) | copy-start | bytes 196612
  20.6 10.1 %collective-permute-start.5 = (f32[128,128]{1,0:T(8,128)S(1)}, f32[128,128]{1,0:T(8,128)S(1)}, u32[]{:S(2)}, u32[]{:S(2)}) collective-permute-start(f32[128,128]{1,0:T(8,128)S(1)} %get-tuple-element.19.x_low), channel_id=1, source_target_pairs={{4,0},{8,4},{12,8},{0,12},{5,1},{9,5},{13,9},{1,13},{6,2},{10,6},{... | collective-permute-start | bytes 196616 | tf_op jit(solution)/shard_map/ppermute | solution.py:367
  23.9 6.7 %collective-permute-start.4 = (f32[128,128]{1,0:T(8,128)S(1)}, f32[128,128]{1,0:T(8,128)S(1)}, u32[]{:S(2)}, u32[]{:S(2)}) collective-permute-start(f32[128,128]{1,0:T(8,128)S(1)} %get-tuple-element.20.x_high), channel_id=1, source_target_pairs={{0,4},{4,8},{8,12},{12,0},{1,5},{5,9},{9,13},{13,1},{2,6},{6,10},{... | collective-permute-start | bytes 196616 | tf_op jit(solution)/shard_map/ppermute | solution.py:366
  23.9 6.7 %collective-permute-start.7 = (f32[128,128]{1,0:T(8,128)S(1)}, f32[128,128]{1,0:T(8,128)S(1)}, u32[]{:S(2)}, u32[]{:S(2)}) collective-permute-start(f32[128,128]{1,0:T(8,128)S(1)} %get-tuple-element.21.y_low), channel_id=1, source_target_pairs={{1,0},{2,1},{3,2},{0,3},{5,4},{6,5},{7,6},{4,7},{9,8},{10,9},{11,1... | collective-permute-start | bytes 196616 | tf_op jit(solution)/shard_map/ppermute | solution.py:369
  24.1 6.5 %collective-permute-start.6 = (f32[128,128]{1,0:T(8,128)S(1)}, f32[128,128]{1,0:T(8,128)S(1)}, u32[]{:S(2)}, u32[]{:S(2)}) collective-permute-start(f32[128,128]{1,0:T(8,128)S(1)} %get-tuple-element.22.y_high), channel_id=1, source_target_pairs={{0,1},{1,2},{2,3},{3,0},{4,5},{5,6},{6,7},{7,4},{8,9},{9,10},{10,1... | collective-permute-start | bytes 196616 | tf_op jit(solution)/shard_map/ppermute | solution.py:368
  30.6 0.6 %copy-start.9 = (f32[128,128]{1,0:T(8,128)}, f32[128,128]{1,0:T(8,128)S(1)}, u32[]{:S(2)}) copy-start(f32[128,128]{1,0:T(8,128)S(1)} %collective-permute-done.5.from_x_high) | copy-start | bytes 196612
  30.6 0.7 %copy-start.10 = (f32[128,128]{1,0:T(8,128)}, f32[128,128]{1,0:T(8,128)S(1)}, u32[]{:S(2)}) copy-start(f32[128,128]{1,0:T(8,128)S(1)} %collective-permute-done.4.from_x_low) | copy-start | bytes 196612
  30.6 0.7 %copy-start.11 = (f32[128,128]{1,0:T(8,128)}, f32[128,128]{1,0:T(8,128)S(1)}, u32[]{:S(2)}) copy-start(f32[128,128]{1,0:T(8,128)S(1)} %collective-permute-done.7.from_y_high) | copy-start | bytes 196612
  31.3 0.6 %copy-start.12 = (f32[128,128]{1,0:T(8,128)}, f32[128,128]{1,0:T(8,128)S(1)}, u32[]{:S(2)}) copy-start(f32[128,128]{1,0:T(8,128)S(1)} %collective-permute-done.6.from_y_low) | copy-start | bytes 196612

commit v2 on v1

--- a/solution.py
+++ b/solution.py
@@ -11,13 +11,15 @@
 SR = 2
 CAP = 2
 LANES = 128
+MIB = 2**20
+VMEM_BYTES = 64 * MIB
 
 HEAT_RATIO = 5.0 / 3.0
 CORONA_RATIO = 0.04
 HELIO_RATIO = 0.03
 
 VM = pl.BlockSpec(memory_space=pltpu.VMEM)
-SM = pl.BlockSpec(memory_space=pltpu.SMEM)
+HB = pl.BlockSpec(memory_space=pltpu.HBM)
 
 
 def partner(index, step, count):
@@ -26,19 +28,49 @@
     return (index + step) % count
 
 
-def sender(index, step, count):
-    if count & (count - 1) == 0:
-        return index ^ step
-    return (index - step + count) % count
-
-
-def pack_kernel(dims, owner_ref, grid_ref, *rest):
-    ncomp, len_x, len_y, len_z, n_yz, shells = dims
-    outs, (blocks, send) = rest[:n_yz], rest[n_yz:]
+def pack_kernel(dims, owner_hbm, source_hbm, target_hbm, grid_hbm, *rest):
+    ncomp, len_x, len_y, len_z, n_yz, shells, slots, depth = dims
+    outs, plan = rest[:n_yz], rest[n_yz]
+    grid_ref, owner_ref, source_ref, target_ref, table, blocks, send, sems = rest[n_yz + 1 :]
     me = lax.axis_index("yz")
+    grid_copy = pltpu.make_async_copy(grid_hbm, grid_ref, sems.at[0])
+    copies = [
+        pltpu.make_async_copy(owner_hbm, owner_ref, sems.at[1]),
+        pltpu.make_async_copy(source_hbm, source_ref, sems.at[2]),
+        pltpu.make_async_copy(target_hbm, target_ref, sems.at[3]),
+    ]
+
+    @pl.when(lax.axis_index("dom") == 1)
+    def _():
+        for copy in copies:
+            copy.start()
+        for copy in copies:
+            copy.wait()
+        position = jnp.int32(0)
+        for t in range(n_yz):
+            if n_yz & (n_yz - 1) == 0:
+                step = t ^ me
+            else:
+                step = lax.rem(me - t + n_yz, n_yz)
+            rank = jnp.int32(0)
+            for b in range(shells):
+                table[jnp.minimum(position, n_yz * CAP)] = step * CAP + jnp.minimum(rank, CAP - 1)
+                mine = jnp.where(owner_ref[0, t, b] == me, 1, 0)
+                position = position + mine
+                rank = rank + mine
+        for j in range(slots):
+            for k in range(depth):
+                entry = source_ref[0, 0, j, k]
+                spot = jnp.where(entry >= 0, table[jnp.clip(entry, 0, n_yz * CAP)], -1)
+                plan[j * depth + k : j * depth + k + 1, :] = jnp.full((1, LANES), spot, jnp.int32)
+            plan[slots * depth + j : slots * depth + j + 1, :] = jnp.full((1, LANES), target_ref[0, 0, j], jnp.int32)
 
     @pl.when(lax.axis_index("dom") == 0)
     def _():
+        grid_copy.start()
+        copies[0].start()
+        grid_copy.wait()
+        copies[0].wait()
         n_bx, n_by, half = len_x // BLK, len_y // BLK, BLK // 2
         plane = len_x * len_y
         z_from = len_z - SR * BLK
@@ -66,10 +98,10 @@
                 ].astype(jnp.bfloat16)
         send[...] = jnp.zeros_like(send)
         for b in range(shells):
-            owner = owner_ref[me * shells + b]
+            owner = owner_ref[0, me, b]
             rank = jnp.int32(0)
             for other in range(b):
-                rank = rank + jnp.where(owner_ref[me * shells + other] == owner, 1, 0)
+                rank = rank + jnp.where(owner_ref[0, me, other] == owner, 1, 0)
             if n_yz & (n_yz - 1) == 0:
                 step = owner ^ me
             else:
@@ -81,42 +113,38 @@
                 outs[step][slot * rows : (slot + 1) * rows, :] = send[step * CAP + slot]
 
 
-def fill_kernel(dims, owner_ref, source_ref, target_ref, weight_ref, grid_ref, *rest):
-    ncomp, len_x, len_y, len_z, n_yz, shells, slots, depth = dims
+def stage_kernel(count, *refs):
+    sems = refs[-1]
+    copies = [pltpu.make_async_copy(refs[i], refs[count + i], sems.at[i]) for i in range(count)]
+    for copy in copies:
+        copy.start()
+    for copy in copies:
+        copy.wait()
+
+
+def fill_kernel(dims, plan_vmem, weight_ref, grid_ref, *rest):
+    ncomp, len_x, len_y, len_z, n_yz, slots, depth = dims
     got = rest[:n_yz]
-    filled, x_low, x_high, y_low, y_high, held, result, table = rest[n_yz:]
-    me = lax.axis_index("yz")
+    filled, x_low, x_high, y_low, y_high, held, result, plan, sem = rest[n_yz:]
     half = BLK // 2
     rows = half * ncomp
     plane = len_x * len_y
 
-    filled[...] = grid_ref[...]
-
     @pl.when(lax.axis_index("dom") == 1)
     def _():
+        copy = pltpu.make_async_copy(plan_vmem, plan, sem)
+        copy.start()
         for step in range(n_yz):
             for slot in range(CAP):
                 held[step * CAP + slot] = got[step][slot * rows : (slot + 1) * rows, :].astype(jnp.float32)
-        position = jnp.int32(0)
-        for t in range(n_yz):
-            if n_yz & (n_yz - 1) == 0:
-                step = t ^ me
-            else:
-                step = lax.rem(me - t + n_yz, n_yz)
-            rank = jnp.int32(0)
-            for b in range(shells):
-                table[jnp.minimum(position, n_yz * CAP)] = step * CAP + jnp.minimum(rank, CAP - 1)
-                mine = jnp.where(owner_ref[t * shells + b] == me, 1, 0)
-                position = position + mine
-                rank = rank + mine
+        copy.wait()
         lines = []
         for j in range(slots):
             total = jnp.zeros((ncomp, BLK * BLK * BLK), jnp.float32)
             for k in range(depth):
-                entry = source_ref[j * depth + k]
-                live = entry >= 0
-                spot = jnp.where(live, table[jnp.clip(entry, 0, n_yz * CAP)], 0)
-                block = held[spot]
+                spot = plan[j * depth + k, 0]
+                live = spot >= 0
+                block = held[jnp.maximum(spot, 0)]
                 cells = jnp.concatenate(
                     [block[a2 * ncomp : (a2 + 1) * ncomp, :] for a2 in range(half)], axis=1
                 )
@@ -142,7 +170,7 @@
         lane = lax.broadcasted_iota(jnp.int32, (ncomp, LANES), 1)
         per_y, per_z = len_y // BLK, len_z // BLK
         for j in range(slots):
-            target = target_ref[j]
+            target = plan[slots * depth + j, 0]
 
             @pl.when(target >= 0)
             def _():
@@ -318,24 +346,30 @@
     volume = BLK * BLK * BLK
     cell_rows = ncomp * len_x * len_y
     grid = field_state.reshape(cell_rows, len_z)
-    owners = shell_owner.reshape(-1)
-    sources = block_sources.reshape(-1)
-    targets = block_targets.reshape(-1)
     weights = interp_weights.reshape(slots * depth, volume, volume)
     rows = BLK // 2 * ncomp
     dims = (ncomp, len_x, len_y, len_z)
 
-    packed = pl.pallas_call(
-        functools.partial(pack_kernel, dims + (n_yz, shells)),
-        out_shape=[jax.ShapeDtypeStruct((CAP * rows, LANES), jnp.bfloat16)] * n_yz,
-        in_specs=[SM, VM],
-        out_specs=[VM] * n_yz,
+    plan_rows = -(-slots * (depth + 1) // BLK) * BLK
+    *packed, plan = pl.pallas_call(
+        functools.partial(pack_kernel, dims + (n_yz, shells, slots, depth)),
+        out_shape=[jax.ShapeDtypeStruct((CAP * rows, LANES), jnp.bfloat16)] * n_yz
+        + [jax.ShapeDtypeStruct((plan_rows, LANES), jnp.int32)],
+        in_specs=[HB] * 4,
+        out_specs=[VM] * (n_yz + 1),
         scratch_shapes=[
+            pltpu.VMEM((cell_rows, len_z), jnp.float32),
+            pltpu.SMEM(shell_owner.shape, jnp.int32),
+            pltpu.SMEM(block_sources.shape, jnp.int32),
+            pltpu.SMEM(block_targets.shape, jnp.int32),
+            pltpu.SMEM((n_yz * CAP + 1,), jnp.int32),
             pltpu.VMEM((shells, rows, LANES), jnp.bfloat16),
             pltpu.VMEM((n_yz * CAP, rows, LANES), jnp.bfloat16),
+            pltpu.SemaphoreType.DMA((4,)),
         ],
+        compiler_params=pltpu.CompilerParams(vmem_limit_bytes=VMEM_BYTES - 8 * MIB),
         name="pack_shell",
-    )(owners, grid)
+    )(shell_owner, block_sources, block_targets, grid)
 
     moved = []
     for step in range(n_yz):
@@ -343,21 +377,36 @@
         pairs = pairs + [(b, a) for a, b in pairs]
         moved.append(lax.ppermute(packed[step], ("dom", "yz"), pairs))
 
+    staged = (weights, grid, plan)
+    staged_bytes = sum(x.size * x.dtype.itemsize for x in staged)
+    weights, grid, plan = pl.pallas_call(
+        functools.partial(stage_kernel, len(staged)),
+        out_shape=[jax.ShapeDtypeStruct(x.shape, x.dtype) for x in staged],
+        in_specs=[HB] * 3,
+        out_specs=[VM] * 3,
+        scratch_shapes=[pltpu.SemaphoreType.DMA((3,))],
+        compiler_params=pltpu.CompilerParams(vmem_limit_bytes=VMEM_BYTES - 13 * staged_bytes // 4),
+        cost_estimate=pl.CostEstimate(flops=0, bytes_accessed=4 * interp_weights.size, transcendentals=0),
+        name="stage_operands",
+    )(*staged)
+
     face_x = jax.ShapeDtypeStruct((ncomp * len_y, len_z), jnp.float32)
     face_y = jax.ShapeDtypeStruct((ncomp * len_x, len_z), jnp.float32)
     filled, x_low, x_high, y_low, y_high = pl.pallas_call(
-        functools.partial(fill_kernel, dims + (n_yz, shells, slots, depth)),
+        functools.partial(fill_kernel, dims + (n_yz, slots, depth)),
         out_shape=[jax.ShapeDtypeStruct((cell_rows, len_z), jnp.float32), face_x, face_x, face_y, face_y],
-        in_specs=[SM, SM, SM, VM, VM] + [VM] * n_yz,
+        in_specs=[VM, VM, VM] + [VM] * n_yz,
         out_specs=[VM] * 5,
         scratch_shapes=[
             pltpu.VMEM((n_yz * CAP, rows, LANES), jnp.float32),
             pltpu.VMEM((2 * BLK, slots * rows, LANES), jnp.float32),
-            pltpu.SMEM((n_yz * CAP + 1,), jnp.int32),
+            pltpu.SMEM((plan_rows, LANES), jnp.int32),
+            pltpu.SemaphoreType.DMA,
         ],
-        compiler_params=pltpu.CompilerParams(vmem_limit_bytes=24 * 2**20),
+        input_output_aliases={2: 0},
+        compiler_params=pltpu.CompilerParams(vmem_limit_bytes=16 * MIB),
         name="fill_blocks",
-    )(owners, sources, targets, weights, grid, *moved)
+    )(plan, weights, grid, *moved)
 
     up_x = [(i, (i + 1) % n_gx) for i in range(n_gx)]
     down_x = [(b, a) for a, b in up_x]
@@ -374,6 +423,7 @@
         in_specs=[VM],
         out_specs=VM,
         cost_estimate=pl.CostEstimate(flops=300 * cell_rows * len_z, bytes_accessed=8 * cell_rows * len_z, transcendentals=0),
+        compiler_params=pltpu.CompilerParams(vmem_limit_bytes=8 * MIB),
         name="inner_faces",
     )(filled)
 
@@ -382,6 +432,7 @@
         out_shape=jax.ShapeDtypeStruct((cell_rows, len_z), jnp.float32),
         in_specs=[VM] * 9,
         out_specs=VM,
+        compiler_params=pltpu.CompilerParams(vmem_limit_bytes=8 * MIB),
         name="edge_faces",
     )(part, x_low, x_high, y_low, y_high, from_x_low, from_x_high, from_y_low, from_y_high)
     return updated.reshape(1, ncomp, len_x, len_y, len_z)

time: 35 us -> 24.8 us (0.71)
  the two profiles are of different devices: /device:TPU:1 before, /device:TPU:0 now
where the time goes in v2:
time: 24.8 us; the launch traced here: 24.3 us
  starting transfers between devices  10.9 us (44%)
  Pallas kernels  9.23 us (37%)
  waiting for transfers between devices  2.2 us (9%)
  local copies, waits for them, and re-layouts  1.92 us (8%)
    ppermute x4, starting transfers between devices, local(): moved.append(lax.ppermute(packed[step], ('dom', 'yz'), pairs))  4.35 us
    ppermute x1, starting transfers between devices, local(): from_x_high = lax.ppermute(x_low, 'gx', down_x)  4.12 us
    pallas_call x1, Pallas kernels, local(): pl.pallas_call(functools.partial(inner_kernel, dims), out_shape=jax.Shape...  3.01 us
    pallas_call x1, Pallas kernels, local(): pl.pallas_call(functools.partial(pack_kernel, dims + (n_yz, shells, slots...  2.61 us
    ppermute x1, starting transfers between devices, local(): from_y_high = lax.ppermute(y_low, 'yz', down_y)  2.45 us
    pallas_call x1, Pallas kernels, local(): pl.pallas_call(functools.partial(stage_kernel, len(staged)), out_shape=[j...  2.22 us
    unnamed x4, local copies, waits for them, and re-layouts  1.92 us
    ppermute x1, waiting for transfers between devices, local(): from_y_low = lax.ppermute(y_high, 'yz', up_y)  1.55 us
  transfers between devices with their start and end apart: 8, of which 3 were waited for; matrix products, arithmetic and copies ran while one was open for 0% of the time, Pallas kernels for 22%

profile of v2, /device:TPU:0, one launch (start us, length us, event | category | flops | bytes accessed | tf_op | source)
XLA Modules:
  0.0 24.3 jit_solution(16905802912824447254)
XLA Ops:
  0.0 2.6 %pack_shell.1 = (bf16[64,128]{1,0:T(8,128)(2,1)}, bf16[64,128]{1,0:T(8,128)(2,1)}, bf16[64,128]{1,0:T(8,128)(2,1)}, bf16[64,128]{1,0:T(8,128)(2,1)}, s32[16,128]{1,0:T(8,128)}) custom-call(s32[1,4,8]{2,1,0:T(4,128)} %owner_hbm.1, s32[1,1,2,4]{3,2,1,0:T(2,128)} %source_hbm.1, s32[1,1,2]{2,1,0:T(1,128)} %target_hbm.1, f32[2048,128]{1,0:T(8,128)} %bitcast.3), custom_call_target="tpu_custom_call" | custom-call | tf_op jit(solution)/shard_map/pack_shell/pallas_call | solution.py:354
  2.6 0.1 collective-permute-start
  2.7 3.1 %collective-permute-start.1 = (bf16[64,128]{1,0:T(8,128)(2,1)}, bf16[64,128]{1,0:T(8,128)(2,1)S(1)}, u32[]{:S(2)}, u32[]{:S(2)}) collective-permute-start(bf16[64,128]{1,0:T(8,128)(2,1)} %get-tuple-element.23), channel_id=1, source_target_pairs={{0,17},{1,16},{2,19},{3,18},{17,0},{16,1},{19,2},{18,3},{4,21},{5,... | collective-permute-start | bytes 49160 | tf_op jit(solution)/shard_map/ppermute | solution.py:378
  5.7 1.2 %collective-permute-start.2 = (bf16[64,128]{1,0:T(8,128)(2,1)}, bf16[64,128]{1,0:T(8,128)(2,1)S(1)}, u32[]{:S(2)}, u32[]{:S(2)}) collective-permute-start(bf16[64,128]{1,0:T(8,128)(2,1)} %get-tuple-element.24), channel_id=1, source_target_pairs={{0,18},{1,19},{2,16},{3,17},{18,0},{19,1},{16,2},{17,3},{4,22},{5,... | collective-permute-start | bytes 49160 | tf_op jit(solution)/shard_map/ppermute | solution.py:378
  6.9 0.0 collective-permute-start.3
  7.0 0.0 copy-start
  7.0 1.2 %copy-done = f32[1,8,16,16,128]{4,3,2,1,0:T(8,128)S(1)} copy-done((f32[1,8,16,16,128]{4,3,2,1,0:T(8,128)S(1)}, f32[1,8,16,16,128]{4,3,2,1,0:T(8,128)}, u32[]{:S(2)}) %copy-start) | copy-done | bytes 1048600
  8.2 0.0 copy-start.1
  8.2 0.7 %copy-done.1 = s32[16,128]{1,0:T(8,128)S(1)} copy-done((s32[16,128]{1,0:T(8,128)S(1)}, s32[16,128]{1,0:T(8,128)}, u32[]{:S(2)}) %copy-start.1) | copy-done | bytes 8216
  8.9 2.2 %stage_operands.1 = (bf16[8,512,512]{2,1,0:T(8,128)(2,1)S(1)}, f32[2048,128]{1,0:T(8,128)S(1)}, s32[16,128]{1,0:T(8,128)S(1)}) custom-call(bf16[8,512,512]{2,1,0:T(8,128)(2,1)} %bitcast.5, f32[2048,128]{1,0:T(8,128)S(1)} %bitcast.4, s32[16,128]{1,0:T(8,128)S(1)} %copy-done.1), custom_call_target="tpu_custom_call" | custom-call | bytes 8388608 | tf_op jit(solution)/shard_map/stage_operands/pallas_call | solution.py:382
  11.1 0.0 collective-permute-done.rest_0_
  11.1 0.0 collective-permute-done.1.rest_1_
  11.1 0.0 collective-permute-done.2.rest_2_
  11.2 0.1 collective-permute-done.3.rest_3_
  11.2 0.1 fill_blocks.1
  11.3 4.1 %collective-permute-start.5 = (f32[128,128]{1,0:T(8,128)S(1)}, f32[128,128]{1,0:T(8,128)S(1)}, u32[]{:S(2)}, u32[]{:S(2)}) collective-permute-start(f32[128,128]{1,0:T(8,128)S(1)} %get-tuple-element.27.x_low), channel_id=1, source_target_pairs={{4,0},{8,4},{12,8},{0,12},{5,1},{9,5},{13,9},{1,13},{6,2},{10,6},{... | collective-permute-start | bytes 196616 | tf_op jit(solution)/shard_map/ppermute | solution.py:416
  15.4 0.0 collective-permute-start.4
  15.4 2.4 %collective-permute-start.7 = (f32[128,128]{1,0:T(8,128)S(1)}, f32[128,128]{1,0:T(8,128)S(1)}, u32[]{:S(2)}, u32[]{:S(2)}) collective-permute-start(f32[128,128]{1,0:T(8,128)S(1)} %get-tuple-element.29.y_low), channel_id=1, source_target_pairs={{1,0},{2,1},{3,2},{0,3},{5,4},{6,5},{7,6},{4,7},{9,8},{10,9},{11,1... | collective-permute-start | bytes 196616 | tf_op jit(solution)/shard_map/ppermute | solution.py:418
  17.8 0.0 collective-permute-start.6
  17.8 3.0 %inner_faces.1.part = f32[2048,128]{1,0:T(8,128)S(1)} custom-call(f32[2048,128]{1,0:T(8,128)S(1)} %get-tuple-element.26.filled), custom_call_target="tpu_custom_call" | custom-call | flops 78643200 | bytes 2097152 | tf_op jit(solution)/shard_map/inner_faces/pallas_call | solution.py:420
  20.9 0.0 collective-permute-done.5.from_x_high
  20.9 0.6 %collective-permute-done.4.from_x_low = f32[128,128]{1,0:T(8,128)S(1)} collective-permute-done((f32[128,128]{1,0:T(8,128)S(1)}, f32[128,128]{1,0:T(8,128)S(1)}, u32[]{:S(2)}, u32[]{:S(2)}) %collective-permute-start.4) | collective-permute-done | bytes 65568 | tf_op jit(solution)/shard_map/ppermute | solution.py:415
  21.5 0.0 collective-permute-done.7.from_y_high
  21.5 1.5 %collective-permute-done.6.from_y_low = f32[128,128]{1,0:T(8,128)S(1)} collective-permute-done((f32[128,128]{1,0:T(8,128)S(1)}, f32[128,128]{1,0:T(8,128)S(1)}, u32[]{:S(2)}, u32[]{:S(2)}) %collective-permute-start.6) | collective-permute-done | bytes 65568 | tf_op jit(solution)/shard_map/ppermute | solution.py:417
  23.0 1.3 %edge_faces.1 = f32[2048,128]{1,0:T(8,128)} custom-call(f32[2048,128]{1,0:T(8,128)S(1)} %inner_faces.1.part, f32[128,128]{1,0:T(8,128)S(1)} %get-tuple-element.27.x_low, f32[128,128]{1,0:T(8,128)S(1)} %get-tuple-element.28.x_high, f32[128,128]{1,0:T(8,128)S(1)} %get-tuple-element.29.y_low, f32[128,128]{1,0:T(8,128)S(1)} %get-tuple-element.30.y_high, ...), custom_call_target="tpu_custom_call" | custom-call | tf_op jit(solution)/shard_map/edge_faces/pallas_call | solution.py:430
Async XLA Ops:
  2.6 8.5 %collective-permute-start = (bf16[64,128]{1,0:T(8,128)(2,1)}, bf16[64,128]{1,0:T(8,128)(2,1)S(1)}, u32[]{:S(2)}, u32[]{:S(2)}) collective-permute-start(bf16[64,128]{1,0:T(8,128)(2,1)} %get-tuple-element.22), channel_id=1, source_target_pairs={{0,16},{1,17},{2,18},{3,19},{16,0},{17,1},{18,2},{19,3},{4,20},{5,... | collective-permute-start | bytes 49160 | tf_op jit(solution)/shard_map/ppermute | solution.py:378
  2.7 8.4 %collective-permute-start.1 = (bf16[64,128]{1,0:T(8,128)(2,1)}, bf16[64,128]{1,0:T(8,128)(2,1)S(1)}, u32[]{:S(2)}, u32[]{:S(2)}) collective-permute-start(bf16[64,128]{1,0:T(8,128)(2,1)} %get-tuple-element.23), channel_id=1, source_target_pairs={{0,17},{1,16},{2,19},{3,18},{17,0},{16,1},{19,2},{18,3},{4,21},{5,... | collective-permute-start | bytes 49160 | tf_op jit(solution)/shard_map/ppermute | solution.py:378
  5.7 5.4 %collective-permute-start.2 = (bf16[64,128]{1,0:T(8,128)(2,1)}, bf16[64,128]{1,0:T(8,128)(2,1)S(1)}, u32[]{:S(2)}, u32[]{:S(2)}) collective-permute-start(bf16[64,128]{1,0:T(8,128)(2,1)} %get-tuple-element.24), channel_id=1, source_target_pairs={{0,18},{1,19},{2,16},{3,17},{18,0},{19,1},{16,2},{17,3},{4,22},{5,... | collective-permute-start | bytes 49160 | tf_op jit(solution)/shard_map/ppermute | solution.py:378
  6.9 4.3 %collective-permute-start.3 = (bf16[64,128]{1,0:T(8,128)(2,1)}, bf16[64,128]{1,0:T(8,128)(2,1)S(1)}, u32[]{:S(2)}, u32[]{:S(2)}) collective-permute-start(bf16[64,128]{1,0:T(8,128)(2,1)} %get-tuple-element.25), channel_id=1, source_target_pairs={{0,19},{1,18},{2,17},{3,16},{19,0},{18,1},{17,2},{16,3},{4,23},{5,... | collective-permute-start | bytes 49160 | tf_op jit(solution)/shard_map/ppermute | solution.py:378
  7.0 1.2 %copy-start = (f32[1,8,16,16,128]{4,3,2,1,0:T(8,128)S(1)}, f32[1,8,16,16,128]{4,3,2,1,0:T(8,128)}, u32[]{:S(2)}) copy-start(f32[1,8,16,16,128]{4,3,2,1,0:T(8,128)} %param.5) | copy-start | bytes 3145732
  8.2 0.7 %copy-start.1 = (s32[16,128]{1,0:T(8,128)S(1)}, s32[16,128]{1,0:T(8,128)}, u32[]{:S(2)}) copy-start(s32[16,128]{1,0:T(8,128)} %get-tuple-element.18.refs_2_) | copy-start | bytes 24580
  11.3 9.6 %collective-permute-start.5 = (f32[128,128]{1,0:T(8,128)S(1)}, f32[128,128]{1,0:T(8,128)S(1)}, u32[]{:S(2)}, u32[]{:S(2)}) collective-permute-start(f32[128,128]{1,0:T(8,128)S(1)} %get-tuple-element.27.x_low), channel_id=1, source_target_pairs={{4,0},{8,4},{12,8},{0,12},{5,1},{9,5},{13,9},{1,13},{6,2},{10,6},{... | collective-permute-start | bytes 196616 | tf_op jit(solution)/shard_map/ppermute | solution.py:416
  15.4 6.1 %collective-permute-start.4 = (f32[128,128]{1,0:T(8,128)S(1)}, f32[128,128]{1,0:T(8,128)S(1)}, u32[]{:S(2)}, u32[]{:S(2)}) collective-permute-start(f32[128,128]{1,0:T(8,128)S(1)} %get-tuple-element.28.x_high), channel_id=1, source_target_pairs={{0,4},{4,8},{8,12},{12,0},{1,5},{5,9},{9,13},{13,1},{2,6},{6,10},{... | collective-permute-start | bytes 196616 | tf_op jit(solution)/shard_map/ppermute | solution.py:415
  15.4 6.1 %collective-permute-start.7 = (f32[128,128]{1,0:T(8,128)S(1)}, f32[128,128]{1,0:T(8,128)S(1)}, u32[]{:S(2)}, u32[]{:S(2)}) collective-permute-start(f32[128,128]{1,0:T(8,128)S(1)} %get-tuple-element.29.y_low), channel_id=1, source_target_pairs={{1,0},{2,1},{3,2},{0,3},{5,4},{6,5},{7,6},{4,7},{9,8},{10,9},{11,1... | collective-permute-start | bytes 196616 | tf_op jit(solution)/shard_map/ppermute | solution.py:418
  17.8 5.2 %collective-permute-start.6 = (f32[128,128]{1,0:T(8,128)S(1)}, f32[128,128]{1,0:T(8,128)S(1)}, u32[]{:S(2)}, u32[]{:S(2)}) collective-permute-start(f32[128,128]{1,0:T(8,128)S(1)} %get-tuple-element.30.y_high), channel_id=1, source_target_pairs={{0,1},{1,2},{2,3},{3,0},{4,5},{5,6},{6,7},{7,4},{8,9},{9,10},{10,1... | collective-permute-start | bytes 196616 | tf_op jit(solution)/shard_map/ppermute | solution.py:417

commit v3 on v2

--- a/solution.py
+++ b/solution.py
@@ -28,16 +28,34 @@
     return (index + step) % count
 
 
+def cycle(count):
+    pairs = [(count + i, count + i + 1) for i in range(count - 1)] + [(2 * count - 1, count - 1)]
+    return pairs + [(i + 1, i) for i in range(count - 1)] + [(0, count)]
+
+
+def wrap_pairs(count):
+    pairs = [(0, count - 1)]
+    pairs += [(i, i + 1) for i in range(1, count - 2, 2)]
+    pairs += [(count + i, count + i + 1) for i in range(0, count - 1, 2)]
+    return pairs + [(b, a) for a, b in pairs]
+
+
 def pack_kernel(dims, owner_hbm, source_hbm, target_hbm, grid_hbm, *rest):
     ncomp, len_x, len_y, len_z, n_yz, shells, slots, depth = dims
-    outs, plan = rest[:n_yz], rest[n_yz]
-    grid_ref, owner_ref, source_ref, target_ref, table, blocks, send, sems = rest[n_yz + 1 :]
+    outs, plan, wrap = rest[:n_yz], rest[n_yz], rest[n_yz + 1]
+    grid_ref, owner_ref, source_ref, target_ref, table, spread, send, sems = rest[n_yz + 2 :]
     me = lax.axis_index("yz")
-    grid_copy = pltpu.make_async_copy(grid_hbm, grid_ref, sems.at[0])
+    plane = len_x * len_y
+    grid_copies = [
+        pltpu.make_async_copy(
+            grid_hbm.at[pl.ds(c * plane, plane), :], grid_ref.at[pl.ds(c * plane, plane), :], sems.at[3 + c]
+        )
+        for c in range(ncomp)
+    ]
     copies = [
-        pltpu.make_async_copy(owner_hbm, owner_ref, sems.at[1]),
-        pltpu.make_async_copy(source_hbm, source_ref, sems.at[2]),
-        pltpu.make_async_copy(target_hbm, target_ref, sems.at[3]),
+        pltpu.make_async_copy(owner_hbm, owner_ref, sems.at[0]),
+        pltpu.make_async_copy(source_hbm, source_ref, sems.at[1]),
+        pltpu.make_async_copy(target_hbm, target_ref, sems.at[2]),
     ]
 
     @pl.when(lax.axis_index("dom") == 1)
@@ -67,17 +85,32 @@
 
     @pl.when(lax.axis_index("dom") == 0)
     def _():
-        grid_copy.start()
         copies[0].start()
-        grid_copy.wait()
-        copies[0].wait()
+        for copy in grid_copies:
+            copy.start()
         n_bx, n_by, half = len_x // BLK, len_y // BLK, BLK // 2
-        plane = len_x * len_y
         z_from = len_z - SR * BLK
         row_z = lax.broadcasted_iota(jnp.int32, (LANES, SR * LANES), 0) + (len_z - LANES)
         column = lax.broadcasted_iota(jnp.int32, (LANES, SR * LANES), 1)
         hit = row_z == z_from + column // LANES * BLK + column % BLK
-        place = column % LANES // BLK
+        place = jnp.where(hit, column % LANES // BLK, -1)
+        for m in range(2 * BLK):
+            spread[m] = jnp.where(place == m, 1.0, 0.0).astype(jnp.bfloat16)
+        send[...] = jnp.zeros_like(send)
+        copies[0].wait()
+        spots = []
+        for b in range(shells):
+            owner = owner_ref[0, me, b]
+            rank = jnp.int32(0)
+            for other in range(b):
+                rank = rank + jnp.where(owner_ref[0, me, other] == owner, 1, 0)
+            if n_yz & (n_yz - 1) == 0:
+                step = owner ^ me
+            else:
+                step = lax.rem(owner - me + n_yz, n_yz)
+            spots.append(jnp.clip(step * CAP + rank, 0, n_yz * CAP - 1))
+        for copy in grid_copies:
+            copy.wait()
         total = jnp.zeros((n_bx * n_by * half * ncomp, SR * LANES), jnp.float32)
         for ap in range(2):
             for cy in range(BLK):
@@ -88,70 +121,73 @@
                             first = (bx * BLK + a2 * 2 + ap) * len_y + by * BLK + cy
                             pieces.append(grid_ref[pl.ds(first, ncomp, stride=plane), :])
                 cells = jnp.concatenate(pieces, axis=0).astype(jnp.bfloat16)
-                pick = jnp.where(hit & (place == ap * BLK + cy), 1.0, 0.0).astype(jnp.bfloat16)
-                total = total + jnp.dot(cells, pick, preferred_element_type=jnp.float32)
+                total = total + jnp.dot(cells, spread[ap * BLK + cy], preferred_element_type=jnp.float32)
         rows = half * ncomp
-        for column_block in range(n_bx * n_by):
-            for br in range(SR):
-                blocks[column_block * SR + br] = total[
-                    column_block * rows : (column_block + 1) * rows, br * LANES : (br + 1) * LANES
-                ].astype(jnp.bfloat16)
-        send[...] = jnp.zeros_like(send)
+        total = total.astype(jnp.bfloat16)
         for b in range(shells):
-            owner = owner_ref[0, me, b]
-            rank = jnp.int32(0)
-            for other in range(b):
-                rank = rank + jnp.where(owner_ref[0, me, other] == owner, 1, 0)
-            if n_yz & (n_yz - 1) == 0:
-                step = owner ^ me
-            else:
-                step = lax.rem(owner - me + n_yz, n_yz)
-            spot = jnp.clip(step * CAP + rank, 0, n_yz * CAP - 1)
-            send[spot] = blocks[b]
+            column_block, br = b // SR, b % SR
+            send[spots[b]] = total[
+                column_block * rows : (column_block + 1) * rows, br * LANES : (br + 1) * LANES
+            ]
         for step in range(n_yz):
             for slot in range(CAP):
                 outs[step][slot * rows : (slot + 1) * rows, :] = send[step * CAP + slot]
-
-
-def stage_kernel(count, *refs):
-    sems = refs[-1]
-    copies = [pltpu.make_async_copy(refs[i], refs[count + i], sems.at[i]) for i in range(count)]
-    for copy in copies:
-        copy.start()
-    for copy in copies:
-        copy.wait()
+        end = jnp.where(lax.axis_index("gx") == 0, 0, plane - len_y)
+        for c in range(ncomp):
+            wrap[c * len_y : (c + 1) * len_y, :] = grid_ref[
+                pl.ds(pl.multiple_of(c * plane + end, BLK), len_y), :
+            ]
+
+
+def stage_kernel(weight_hbm, grid_hbm, plan_hbm, weight_ref, grid_ref, plan_ref, sems):
+    blocks = weight_ref.shape[0]
+    grid_copy = pltpu.make_async_copy(grid_hbm, grid_ref, sems.at[blocks])
+    copies = [pltpu.make_async_copy(weight_hbm.at[i], weight_ref.at[i], sems.at[i]) for i in range(blocks)]
+    copies.append(pltpu.make_async_copy(plan_hbm, plan_ref, sems.at[blocks + 1]))
+    grid_copy.start()
+
+    @pl.when(lax.axis_index("dom") == 1)
+    def _():
+        for copy in copies:
+            copy.start()
+        for copy in copies:
+            copy.wait()
+
+    grid_copy.wait()
 
 
 def fill_kernel(dims, plan_vmem, weight_ref, grid_ref, *rest):
     ncomp, len_x, len_y, len_z, n_yz, slots, depth = dims
     got = rest[:n_yz]
-    filled, x_low, x_high, y_low, y_high, held, result, plan, sem = rest[n_yz:]
+    filled, x_one, x_two, y_one, y_two, result, plan, sem = rest[n_yz:]
     half = BLK // 2
     rows = half * ncomp
     plane = len_x * len_y
 
-    @pl.when(lax.axis_index("dom") == 1)
+    helio = lax.axis_index("dom") == 1
+
+    @pl.when(helio)
     def _():
         copy = pltpu.make_async_copy(plan_vmem, plan, sem)
         copy.start()
-        for step in range(n_yz):
-            for slot in range(CAP):
-                held[step * CAP + slot] = got[step][slot * rows : (slot + 1) * rows, :].astype(jnp.float32)
-        copy.wait()
+        held = [
+            got[step][slot * rows : (slot + 1) * rows, :].astype(jnp.float32)
+            for step in range(n_yz)
+            for slot in range(CAP)
+        ]
         lines = []
         for j in range(slots):
             total = jnp.zeros((ncomp, BLK * BLK * BLK), jnp.float32)
             for k in range(depth):
-                spot = plan[j * depth + k, 0]
-                live = spot >= 0
-                block = held[jnp.maximum(spot, 0)]
+                entry = j * depth + k
+                spot = jnp.broadcast_to(plan_vmem[entry : entry + 1, :], (rows, LANES))
+                block = jnp.zeros((rows, LANES), jnp.float32)
+                for place, candidate in enumerate(held):
+                    block = jnp.where(spot == place, candidate, block)
                 cells = jnp.concatenate(
                     [block[a2 * ncomp : (a2 + 1) * ncomp, :] for a2 in range(half)], axis=1
-                )
-                cells = jnp.where(live, cells, 0.0).astype(jnp.bfloat16)
-                total = total + jnp.dot(
-                    cells, weight_ref[j * depth + k], preferred_element_type=jnp.float32
-                )
+                ).astype(jnp.bfloat16)
+                total = total + jnp.dot(cells, weight_ref[entry], preferred_element_type=jnp.float32)
             lines += [total[:, a2 * LANES : (a2 + 1) * LANES] for a2 in range(half)]
         lines = jnp.concatenate(lines, axis=0)
         top = lines.astype(jnp.bfloat16)
@@ -167,6 +203,7 @@
             spread = jnp.where(same & (from_lane // BLK == m), 1.0, 0.0).astype(jnp.bfloat16)
             parts = jnp.dot(lines, spread, preferred_element_type=jnp.float32)
             result[m] = parts[:count] + parts[count : 2 * count] + parts[2 * count :]
+        copy.wait()
         lane = lax.broadcasted_iota(jnp.int32, (ncomp, LANES), 1)
         per_y, per_z = len_y // BLK, len_z // BLK
         for j in range(slots):
@@ -180,19 +217,29 @@
                 inside = (lane >= z_from) & (lane < z_from + BLK)
                 first = block_x * BLK * len_y + block_y * BLK
                 for a in range(BLK):
-                    for cy in range(BLK):
-                        spot = pl.ds(first + a * len_y + cy, ncomp, stride=plane)
-                        row = j * rows + a // 2 * ncomp
-                        new = result[a % 2 * BLK + cy, row : row + ncomp, :]
-                        filled[spot, :] = jnp.where(inside, new, filled[spot, :])
-
-    for c in range(ncomp):
-        x_low[c * len_y : (c + 1) * len_y, :] = filled[c * plane : c * plane + len_y, :]
-        x_high[c * len_y : (c + 1) * len_y, :] = filled[(c + 1) * plane - len_y : (c + 1) * plane, :]
-        y_low[c * len_x : (c + 1) * len_x, :] = filled[pl.ds(c * plane, len_x, stride=len_y), :]
-        y_high[c * len_x : (c + 1) * len_x, :] = filled[
-            pl.ds(c * plane + len_y - 1, len_x, stride=len_y), :
-        ]
+                    spots = [pl.ds(first + a * len_y + cy, ncomp, stride=plane) for cy in range(BLK)]
+                    row = j * rows + a // 2 * ncomp
+                    old = [filled[spot, :] for spot in spots]
+                    new = [result[a % 2 * BLK + cy, row : row + ncomp, :] for cy in range(BLK)]
+                    for spot, before, after in zip(spots, old, new):
+                        filled[spot, :] = jnp.where(inside, after, before)
+
+    def faces(x_low, x_high, y_low, y_high):
+        for c in range(ncomp):
+            x_low[c * len_y : (c + 1) * len_y, :] = filled[c * plane : c * plane + len_y, :]
+            x_high[c * len_y : (c + 1) * len_y, :] = filled[(c + 1) * plane - len_y : (c + 1) * plane, :]
+            y_low[c * len_x : (c + 1) * len_x, :] = filled[pl.ds(c * plane, len_x, stride=len_y), :]
+            y_high[c * len_x : (c + 1) * len_x, :] = filled[
+                pl.ds(c * plane + len_y - 1, len_x, stride=len_y), :
+            ]
+
+    @pl.when(helio)
+    def _():
+        faces(x_two, x_one, y_two, y_one)
+
+    @pl.when(jnp.logical_not(helio))
+    def _():
+        faces(x_one, x_two, y_one, y_two)
 
 
 def primitives(cells):
@@ -299,11 +346,10 @@
     step(len_x - 1, unpack(carry), True)
 
 
-def edge_kernel(dims, part, x_low, x_high, y_low, y_high, from_x_low, from_x_high, from_y_low, from_y_high, out):
+def edge_kernel(dims, part, x_one, x_two, y_one, y_two, from_x_one, from_x_two, from_y_one, from_y_two, wrap, out):
     ncomp, len_x, len_y, len_z = dims
     plane = len_x * len_y
     helio = lax.axis_index("dom") == 1
-    column, line = lax.axis_index("gx"), lax.axis_index("yz")
     half_ratio = jnp.where(helio, 0.5 * HELIO_RATIO, 0.5 * CORONA_RATIO).astype(jnp.float32)
     out[...] = part[...]
 
@@ -311,31 +357,40 @@
         flux, speed = flux_of(cells, primitives(cells), direction)
         return cells, flux, speed
 
-    def faces(own_ref, other_ref, at_end, direction, upper, size):
+    def faces(own_ref, other_ref, end, end_ref, direction, upper, size):
         own = [own_ref[c * size : (c + 1) * size, :] for c in range(ncomp)]
         other = [other_ref[c * size : (c + 1) * size, :] for c in range(ncomp)]
-        other = [jnp.where(at_end, u, v) for u, v in zip(own, other)]
+        at_end = own if end_ref is None else [end_ref[c * size : (c + 1) * size, :] for c in range(ncomp)]
+        other = [jnp.where(end, u, v) for u, v in zip(at_end, other)]
         own, other = state(own, direction), state(other, direction)
         if upper:
             return [half_ratio * f for f in face_sum(own, other)]
         return [-half_ratio * f for f in face_sum(other, own)]
 
-    low_end = helio & (column == 0)
-    high_end = helio & (column == lax.axis_size("gx") - 1)
-    for c, change in enumerate(faces(x_low, from_x_low, low_end, 0, False, len_y)):
-        spot = pl.ds(c * plane, len_y)
-        out[spot, :] = out[spot, :] + change
-    for c, change in enumerate(faces(x_high, from_x_high, high_end, 0, True, len_y)):
-        spot = pl.ds((c + 1) * plane - len_y, len_y)
-        out[spot, :] = out[spot, :] + change
-    low_end = line == 0
-    high_end = line == lax.axis_size("yz") - 1
-    for c, change in enumerate(faces(y_low, from_y_low, low_end, 1, False, len_x)):
-        spot = pl.ds(c * plane, len_x, stride=len_y)
-        out[spot, :] = out[spot, :] + change
-    for c, change in enumerate(faces(y_high, from_y_high, high_end, 1, True, len_x)):
-        spot = pl.ds(c * plane + len_y - 1, len_x, stride=len_y)
-        out[spot, :] = out[spot, :] + change
+    def both(x_low, x_high, y_low, y_high, from_x_low, from_x_high, from_y_low, from_y_high, x_end):
+        column, line = lax.axis_index("gx"), lax.axis_index("yz")
+        low_end, high_end = column == 0, column == lax.axis_size("gx") - 1
+        for c, change in enumerate(faces(x_low, from_x_low, low_end, x_end, 0, False, len_y)):
+            spot = pl.ds(c * plane, len_y)
+            out[spot, :] = out[spot, :] + change
+        for c, change in enumerate(faces(x_high, from_x_high, high_end, x_end, 0, True, len_y)):
+            spot = pl.ds((c + 1) * plane - len_y, len_y)
+            out[spot, :] = out[spot, :] + change
+        low_end, high_end = line == 0, line == lax.axis_size("yz") - 1
+        for c, change in enumerate(faces(y_low, from_y_low, low_end, None, 1, False, len_x)):
+            spot = pl.ds(c * plane, len_x, stride=len_y)
+            out[spot, :] = out[spot, :] + change
+        for c, change in enumerate(faces(y_high, from_y_high, high_end, None, 1, True, len_x)):
+            spot = pl.ds(c * plane + len_y - 1, len_x, stride=len_y)
+            out[spot, :] = out[spot, :] + change
+
+    @pl.when(helio)
+    def _():
+        both(x_two, x_one, y_two, y_one, from_x_one, from_x_two, from_y_one, from_y_two, None)
+
+    @pl.when(jnp.logical_not(helio))
+    def _():
+        both(x_one, x_two, y_one, y_two, from_x_two, from_x_one, from_y_two, from_y_one, wrap)
 
 
 def local(field_state, shell_owner, block_sources, block_targets, interp_weights):
@@ -351,21 +406,23 @@
     dims = (ncomp, len_x, len_y, len_z)
 
     plan_rows = -(-slots * (depth + 1) // BLK) * BLK
-    *packed, plan = pl.pallas_call(
+    face_x = jax.ShapeDtypeStruct((ncomp * len_y, len_z), jnp.float32)
+    face_y = jax.ShapeDtypeStruct((ncomp * len_x, len_z), jnp.float32)
+    *packed, plan, wrap = pl.pallas_call(
         functools.partial(pack_kernel, dims + (n_yz, shells, slots, depth)),
         out_shape=[jax.ShapeDtypeStruct((CAP * rows, LANES), jnp.bfloat16)] * n_yz
-        + [jax.ShapeDtypeStruct((plan_rows, LANES), jnp.int32)],
+        + [jax.ShapeDtypeStruct((plan_rows, LANES), jnp.int32), face_x],
         in_specs=[HB] * 4,
-        out_specs=[VM] * (n_yz + 1),
+        out_specs=[VM] * (n_yz + 2),
         scratch_shapes=[
             pltpu.VMEM((cell_rows, len_z), jnp.float32),
             pltpu.SMEM(shell_owner.shape, jnp.int32),
             pltpu.SMEM(block_sources.shape, jnp.int32),
             pltpu.SMEM(block_targets.shape, jnp.int32),
             pltpu.SMEM((n_yz * CAP + 1,), jnp.int32),
-            pltpu.VMEM((shells, rows, LANES), jnp.bfloat16),
+            pltpu.VMEM((2 * BLK, LANES, SR * LANES), jnp.bfloat16),
             pltpu.VMEM((n_yz * CAP, rows, LANES), jnp.bfloat16),
-            pltpu.SemaphoreType.DMA((4,)),
+            pltpu.SemaphoreType.DMA((3 + ncomp,)),
         ],
         compiler_params=pltpu.CompilerParams(vmem_limit_bytes=VMEM_BYTES - 8 * MIB),
         name="pack_shell",
@@ -376,29 +433,27 @@
         pairs = [(t, n_yz + partner(t, step, n_yz)) for t in range(n_yz)]
         pairs = pairs + [(b, a) for a, b in pairs]
         moved.append(lax.ppermute(packed[step], ("dom", "yz"), pairs))
+    wrap = lax.ppermute(wrap, ("dom", "gx"), wrap_pairs(n_gx))
 
     staged = (weights, grid, plan)
     staged_bytes = sum(x.size * x.dtype.itemsize for x in staged)
     weights, grid, plan = pl.pallas_call(
-        functools.partial(stage_kernel, len(staged)),
+        stage_kernel,
         out_shape=[jax.ShapeDtypeStruct(x.shape, x.dtype) for x in staged],
         in_specs=[HB] * 3,
         out_specs=[VM] * 3,
-        scratch_shapes=[pltpu.SemaphoreType.DMA((3,))],
+        scratch_shapes=[pltpu.SemaphoreType.DMA((slots * depth + 2,))],
         compiler_params=pltpu.CompilerParams(vmem_limit_bytes=VMEM_BYTES - 13 * staged_bytes // 4),
         cost_estimate=pl.CostEstimate(flops=0, bytes_accessed=4 * interp_weights.size, transcendentals=0),
         name="stage_operands",
     )(*staged)
 
-    face_x = jax.ShapeDtypeStruct((ncomp * len_y, len_z), jnp.float32)
-    face_y = jax.ShapeDtypeStruct((ncomp * len_x, len_z), jnp.float32)
-    filled, x_low, x_high, y_low, y_high = pl.pallas_call(
+    filled, x_one, x_two, y_one, y_two = pl.pallas_call(
         functools.partial(fill_kernel, dims + (n_yz, slots, depth)),
         out_shape=[jax.ShapeDtypeStruct((cell_rows, len_z), jnp.float32), face_x, face_x, face_y, face_y],
         in_specs=[VM, VM, VM] + [VM] * n_yz,
         out_specs=[VM] * 5,
         scratch_shapes=[
-            pltpu.VMEM((n_yz * CAP, rows, LANES), jnp.float32),
             pltpu.VMEM((2 * BLK, slots * rows, LANES), jnp.float32),
             pltpu.SMEM((plan_rows, LANES), jnp.int32),
             pltpu.SemaphoreType.DMA,
@@ -408,14 +463,11 @@
         name="fill_blocks",
     )(plan, weights, grid, *moved)
 
-    up_x = [(i, (i + 1) % n_gx) for i in range(n_gx)]
-    down_x = [(b, a) for a, b in up_x]
-    up_y = [(i, (i + 1) % n_yz) for i in range(n_yz)]
-    down_y = [(b, a) for a, b in up_y]
-    from_x_low = lax.ppermute(x_high, "gx", up_x)
-    from_x_high = lax.ppermute(x_low, "gx", down_x)
-    from_y_low = lax.ppermute(y_high, "yz", up_y)
-    from_y_high = lax.ppermute(y_low, "yz", down_y)
+    once_x, once_y = cycle(n_gx), cycle(n_yz)
+    from_x_one = lax.ppermute(x_one, ("dom", "gx"), once_x)
+    from_x_two = lax.ppermute(x_two, ("dom", "gx"), [(b, a) for a, b in once_x])
+    from_y_one = lax.ppermute(y_one, ("dom", "yz"), once_y)
+    from_y_two = lax.ppermute(y_two, ("dom", "yz"), [(b, a) for a, b in once_y])
 
     part = pl.pallas_call(
         functools.partial(inner_kernel, dims),
@@ -430,11 +482,11 @@
     updated = pl.pallas_call(
         functools.partial(edge_kernel, dims),
         out_shape=jax.ShapeDtypeStruct((cell_rows, len_z), jnp.float32),
-        in_specs=[VM] * 9,
+        in_specs=[VM] * 10,
         out_specs=VM,
         compiler_params=pltpu.CompilerParams(vmem_limit_bytes=8 * MIB),
         name="edge_faces",
-    )(part, x_low, x_high, y_low, y_high, from_x_low, from_x_high, from_y_low, from_y_high)
+    )(part, x_one, x_two, y_one, y_two, from_x_one, from_x_two, from_y_one, from_y_two, wrap)
     return updated.reshape(1, ncomp, len_x, len_y, len_z)
 
 

time: 24.8 us -> 22.2 us (0.90)
  waiting for transfers between devices: 2.2 us -> 0.02 us
  Pallas kernels: 9.23 us -> 7.36 us
  starting transfers between devices: 10.9 us -> 12.5 us
    ppermute x4 -> x5, waiting for transfers between devices: 2.13 us -> 0.01 us  [the longest x1 0.01 us: local(): wrap = lax.ppermute(wrap, ('dom', 'gx'), wrap_pairs(n_gx))]
    pallas_call x1, Pallas kernels: 2.22 us -> 0.17 us  [local(): pl.pallas_call(stage_kernel, out_shape=[jax.ShapeDtypeStruct(x.shape, x.d...]
    ppermute x4 -> x5, starting transfers between devices: 6.57 us -> 8.16 us  [the longest x1 4.09 us: local(): wrap = lax.ppermute(wrap, ('dom', 'gx'), wrap_pairs(n_gx))]
  transfers between devices with their start and end apart: 8 -> 9, of which waited for: 3 -> 0; matrix products, arithmetic and copies ran while one was open for 0% -> 0% of each run, Pallas kernels for 22% -> 15%
where the time goes in v3:
time: 22.2 us; the launch traced here: 21.9 us
  starting transfers between devices  12.5 us (56%)
  Pallas kernels  7.36 us (33%)
  local copies, waits for them, and re-layouts  1.92 us (9%)
    ppermute x4, starting transfers between devices, local(): moved.append(lax.ppermute(packed[step], ('dom', 'yz'), pairs))  4.35 us
    ppermute x1, starting transfers between devices, local(): wrap = lax.ppermute(wrap, ('dom', 'gx'), wrap_pairs(n_gx))  4.09 us
    pallas_call x1, Pallas kernels, local(): pl.pallas_call(functools.partial(inner_kernel, dims), out_shape=jax.Shape...  3.01 us
    pallas_call x1, Pallas kernels, local(): pl.pallas_call(functools.partial(pack_kernel, dims + (n_yz, shells, slots...  2.76 us
    ppermute x1, starting transfers between devices, local(): from_y_two = lax.ppermute(y_two, ('dom', 'yz'), [(b, a) for a, b in once_y])  2 us
    unnamed x4, local copies, waits for them, and re-layouts  1.92 us
    ppermute x1, starting transfers between devices, local(): from_x_one = lax.ppermute(x_one, ('dom', 'gx'), once_x)  1.56 us
    pallas_call x1, Pallas kernels, local(): pl.pallas_call(functools.partial(edge_kernel, dims), out_shape=jax.ShapeD...  1.34 us
  transfers between devices with their start and end apart: 9, of which 0 were waited for; matrix products, arithmetic and copies ran while one was open for 0% of the time, Pallas kernels for 15%

profile of v3, /device:TPU:0, one launch (start us, length us, event | category | flops | bytes accessed | tf_op | source)
XLA Modules:
  0.0 21.9 jit_solution(14362371826831312641)
XLA Ops:
  0.0 2.8 %pack_shell.1 = (bf16[64,128]{1,0:T(8,128)(2,1)}, bf16[64,128]{1,0:T(8,128)(2,1)}, bf16[64,128]{1,0:T(8,128)(2,1)}, bf16[64,128]{1,0:T(8,128)(2,1)}, s32[16,128]{1,0:T(8,128)}, /*index=5*/f32[128,128]{1,0:T(8,128)}) custom-call(s32[1,4,8]{2,1,0:T(4,128)} %owner_hbm.1, s32[1,1,2,4]{3,2,1,0:T(2,128)} %source_hbm.1, s32[1,1,2]{2,1,0:T(1,128)} %target_hbm.1, ...), custom_call_target="tpu_custom_call" | custom-call | tf_op jit(solution)/shard_map/pack_shell/pallas_call | solution.py:411
  2.8 0.1 collective-permute-start
  2.8 3.1 %collective-permute-start.1 = (bf16[64,128]{1,0:T(8,128)(2,1)}, bf16[64,128]{1,0:T(8,128)(2,1)S(1)}, u32[]{:S(2)}, u32[]{:S(2)}) collective-permute-start(bf16[64,128]{1,0:T(8,128)(2,1)} %get-tuple-element.24), channel_id=1, source_target_pairs={{0,17},{1,16},{2,19},{3,18},{17,0},{16,1},{19,2},{18,3},{4,21},{5,... | collective-permute-start | bytes 49160 | tf_op jit(solution)/shard_map/ppermute | solution.py:435
  5.9 1.2 %collective-permute-start.2 = (bf16[64,128]{1,0:T(8,128)(2,1)}, bf16[64,128]{1,0:T(8,128)(2,1)S(1)}, u32[]{:S(2)}, u32[]{:S(2)}) collective-permute-start(bf16[64,128]{1,0:T(8,128)(2,1)} %get-tuple-element.25), channel_id=1, source_target_pairs={{0,18},{1,19},{2,16},{3,17},{18,0},{19,1},{16,2},{17,3},{4,22},{5,... | collective-permute-start | bytes 49160 | tf_op jit(solution)/shard_map/ppermute | solution.py:435
  7.1 0.0 collective-permute-start.3
  7.1 4.1 %collective-permute-start.8 = (f32[128,128]{1,0:T(8,128)}, f32[128,128]{1,0:T(8,128)S(1)}, u32[]{:S(2)}, u32[]{:S(2)}) collective-permute-start(f32[128,128]{1,0:T(8,128)} %get-tuple-element.32), channel_id=1, source_target_pairs={{0,12},{4,8},{16,20},{24,28},{12,0},{8,4},{20,16},{28,24},{1,13},{... | collective-permute-start | bytes 196616 | tf_op jit(solution)/shard_map/ppermute | solution.py:436
  11.2 0.0 copy-start
  11.2 1.2 %copy-done = f32[1,8,16,16,128]{4,3,2,1,0:T(8,128)S(1)} copy-done((f32[1,8,16,16,128]{4,3,2,1,0:T(8,128)S(1)}, f32[1,8,16,16,128]{4,3,2,1,0:T(8,128)}, u32[]{:S(2)}) %copy-start) | copy-done | bytes 1048600
  12.4 0.0 copy-start.1
  12.4 0.7 %copy-done.1 = s32[16,128]{1,0:T(8,128)S(1)} copy-done((s32[16,128]{1,0:T(8,128)S(1)}, s32[16,128]{1,0:T(8,128)}, u32[]{:S(2)}) %copy-start.1) | copy-done | bytes 8216
  13.1 0.2 stage_operands.1
  13.3 0.0 collective-permute-done.rest_0_
  13.3 0.0 collective-permute-done.1.rest_1_
  13.3 0.0 collective-permute-done.2.rest_2_
  13.4 0.0 collective-permute-done.3.rest_3_
  13.4 0.1 fill_blocks.1
  13.4 1.6 %collective-permute-start.4 = (f32[128,128]{1,0:T(8,128)S(1)}, f32[128,128]{1,0:T(8,128)S(1)}, u32[]{:S(2)}, u32[]{:S(2)}) collective-permute-start(f32[128,128]{1,0:T(8,128)S(1)} %get-tuple-element.28.x_one), channel_id=1, source_target_pairs={{16,20},{20,24},{24,28},{28,12},{4,0},{8,4},{12,8},{0,16},{17,21},... | collective-permute-start | bytes 196616 | tf_op jit(solution)/shard_map/ppermute | solution.py:467
  15.0 0.5 %collective-permute-start.5 = (f32[128,128]{1,0:T(8,128)S(1)}, f32[128,128]{1,0:T(8,128)S(1)}, u32[]{:S(2)}, u32[]{:S(2)}) collective-permute-start(f32[128,128]{1,0:T(8,128)S(1)} %get-tuple-element.29.x_two), channel_id=1, source_target_pairs={{20,16},{24,20},{28,24},{12,28},{0,4},{4,8},{8,12},{16,0},{21,17},... | collective-permute-start | bytes 196616 | tf_op jit(solution)/shard_map/ppermute | solution.py:468
  15.5 0.0 collective-permute-start.6
  15.5 2.0 %collective-permute-start.7 = (f32[128,128]{1,0:T(8,128)S(1)}, f32[128,128]{1,0:T(8,128)S(1)}, u32[]{:S(2)}, u32[]{:S(2)}) collective-permute-start(f32[128,128]{1,0:T(8,128)S(1)} %get-tuple-element.31.y_two), channel_id=1, source_target_pairs={{17,16},{18,17},{19,18},{3,19},{0,1},{1,2},{2,3},{16,0},{21,20},{2... | collective-permute-start | bytes 196616 | tf_op jit(solution)/shard_map/ppermute | solution.py:470
  17.5 3.0 %inner_faces.1.part = f32[2048,128]{1,0:T(8,128)S(1)} custom-call(f32[2048,128]{1,0:T(8,128)S(1)} %get-tuple-element.27.filled), custom_call_target="tpu_custom_call" | custom-call | flops 78643200 | bytes 2097152 | tf_op jit(solution)/shard_map/inner_faces/pallas_call | solution.py:472
  20.5 0.0 collective-permute-done.8.wrap
  20.5 0.0 collective-permute-done.4.from_x_one
  20.6 0.0 collective-permute-done.5.from_x_two
  20.6 0.0 collective-permute-done.6.from_y_one
  20.6 0.0 collective-permute-done.7.from_y_two
  20.6 1.3 %edge_faces.1 = f32[2048,128]{1,0:T(8,128)} custom-call(f32[2048,128]{1,0:T(8,128)S(1)} %inner_faces.1.part, f32[128,128]{1,0:T(8,128)S(1)} %get-tuple-element.28.x_one, f32[128,128]{1,0:T(8,128)S(1)} %get-tuple-element.29.x_two, f32[128,128]{1,0:T(8,128)S(1)} %get-tuple-element.30.y_one, f32[128,128]{1,0:T(8,128)S(1)} %get-tuple-element.31.y_two, ...), custom_call_target="tpu_custom_call" | custom-call | tf_op jit(solution)/shard_map/edge_faces/pallas_call | solution.py:482
Async XLA Ops:
  2.8 10.6 %collective-permute-start = (bf16[64,128]{1,0:T(8,128)(2,1)}, bf16[64,128]{1,0:T(8,128)(2,1)S(1)}, u32[]{:S(2)}, u32[]{:S(2)}) collective-permute-start(bf16[64,128]{1,0:T(8,128)(2,1)} %get-tuple-element.23), channel_id=1, source_target_pairs={{0,16},{1,17},{2,18},{3,19},{16,0},{17,1},{18,2},{19,3},{4,20},{5,... | collective-permute-start | bytes 49160 | tf_op jit(solution)/shard_map/ppermute | solution.py:435
  2.8 10.5 %collective-permute-start.1 = (bf16[64,128]{1,0:T(8,128)(2,1)}, bf16[64,128]{1,0:T(8,128)(2,1)S(1)}, u32[]{:S(2)}, u32[]{:S(2)}) collective-permute-start(bf16[64,128]{1,0:T(8,128)(2,1)} %get-tuple-element.24), channel_id=1, source_target_pairs={{0,17},{1,16},{2,19},{3,18},{17,0},{16,1},{19,2},{18,3},{4,21},{5,... | collective-permute-start | bytes 49160 | tf_op jit(solution)/shard_map/ppermute | solution.py:435
  5.9 7.4 %collective-permute-start.2 = (bf16[64,128]{1,0:T(8,128)(2,1)}, bf16[64,128]{1,0:T(8,128)(2,1)S(1)}, u32[]{:S(2)}, u32[]{:S(2)}) collective-permute-start(bf16[64,128]{1,0:T(8,128)(2,1)} %get-tuple-element.25), channel_id=1, source_target_pairs={{0,18},{1,19},{2,16},{3,17},{18,0},{19,1},{16,2},{17,3},{4,22},{5,... | collective-permute-start | bytes 49160 | tf_op jit(solution)/shard_map/ppermute | solution.py:435
  7.1 6.3 %collective-permute-start.3 = (bf16[64,128]{1,0:T(8,128)(2,1)}, bf16[64,128]{1,0:T(8,128)(2,1)S(1)}, u32[]{:S(2)}, u32[]{:S(2)}) collective-permute-start(bf16[64,128]{1,0:T(8,128)(2,1)} %get-tuple-element.26), channel_id=1, source_target_pairs={{0,19},{1,18},{2,17},{3,16},{19,0},{18,1},{17,2},{16,3},{4,23},{5,... | collective-permute-start | bytes 49160 | tf_op jit(solution)/shard_map/ppermute | solution.py:435
  7.1 13.4 %collective-permute-start.8 = (f32[128,128]{1,0:T(8,128)}, f32[128,128]{1,0:T(8,128)S(1)}, u32[]{:S(2)}, u32[]{:S(2)}) collective-permute-start(f32[128,128]{1,0:T(8,128)} %get-tuple-element.32), channel_id=1, source_target_pairs={{0,12},{4,8},{16,20},{24,28},{12,0},{8,4},{20,16},{28,24},{1,13},{... | collective-permute-start | bytes 196616 | tf_op jit(solution)/shard_map/ppermute | solution.py:436
  11.2 1.2 %copy-start = (f32[1,8,16,16,128]{4,3,2,1,0:T(8,128)S(1)}, f32[1,8,16,16,128]{4,3,2,1,0:T(8,128)}, u32[]{:S(2)}) copy-start(f32[1,8,16,16,128]{4,3,2,1,0:T(8,128)} %param.5) | copy-start | bytes 3145732
  12.4 0.7 %copy-start.1 = (s32[16,128]{1,0:T(8,128)S(1)}, s32[16,128]{1,0:T(8,128)}, u32[]{:S(2)}) copy-start(s32[16,128]{1,0:T(8,128)} %get-tuple-element.19.plan_hbm) | copy-start | bytes 24580
  13.4 7.1 %collective-permute-start.4 = (f32[128,128]{1,0:T(8,128)S(1)}, f32[128,128]{1,0:T(8,128)S(1)}, u32[]{:S(2)}, u32[]{:S(2)}) collective-permute-start(f32[128,128]{1,0:T(8,128)S(1)} %get-tuple-element.28.x_one), channel_id=1, source_target_pairs={{16,20},{20,24},{24,28},{28,12},{4,0},{8,4},{12,8},{0,16},{17,21},... | collective-permute-start | bytes 196616 | tf_op jit(solution)/shard_map/ppermute | solution.py:467
  15.0 5.6 %collective-permute-start.5 = (f32[128,128]{1,0:T(8,128)S(1)}, f32[128,128]{1,0:T(8,128)S(1)}, u32[]{:S(2)}, u32[]{:S(2)}) collective-permute-start(f32[128,128]{1,0:T(8,128)S(1)} %get-tuple-element.29.x_two), channel_id=1, source_target_pairs={{20,16},{24,20},{28,24},{12,28},{0,4},{4,8},{8,12},{16,0},{21,17},... | collective-permute-start | bytes 196616 | tf_op jit(solution)/shard_map/ppermute | solution.py:468
  15.5 5.1 %collective-permute-start.6 = (f32[128,128]{1,0:T(8,128)S(1)}, f32[128,128]{1,0:T(8,128)S(1)}, u32[]{:S(2)}, u32[]{:S(2)}) collective-permute-start(f32[128,128]{1,0:T(8,128)S(1)} %get-tuple-element.30.y_one), channel_id=1, source_target_pairs={{16,17},{17,18},{18,19},{19,3},{1,0},{2,1},{3,2},{0,16},{20,21},{2... | collective-permute-start | bytes 196616 | tf_op jit(solution)/shard_map/ppermute | solution.py:469
  15.5 5.1 %collective-permute-start.7 = (f32[128,128]{1,0:T(8,128)S(1)}, f32[128,128]{1,0:T(8,128)S(1)}, u32[]{:S(2)}, u32[]{:S(2)}) collective-permute-start(f32[128,128]{1,0:T(8,128)S(1)} %get-tuple-element.31.y_two), channel_id=1, source_target_pairs={{17,16},{18,17},{19,18},{3,19},{0,1},{1,2},{2,3},{16,0},{21,20},{2... | collective-permute-start | bytes 196616 | tf_op jit(solution)/shard_map/ppermute | solution.py:470

commit v4 on v3

--- a/solution.py
+++ b/solution.py
@@ -42,13 +42,29 @@
 
 def pack_kernel(dims, owner_hbm, source_hbm, target_hbm, grid_hbm, *rest):
     ncomp, len_x, len_y, len_z, n_yz, shells, slots, depth = dims
-    outs, plan, wrap = rest[:n_yz], rest[n_yz], rest[n_yz + 1]
-    grid_ref, owner_ref, source_ref, target_ref, table, spread, send, sems = rest[n_yz + 2 :]
+    outs, carried, wrap = rest[:n_yz], rest[n_yz], rest[n_yz + 1]
+    grid_ref, owner_ref, source_ref, target_ref, table, plan, spread, send, sems = rest[n_yz + 2 :]
     me = lax.axis_index("yz")
     plane = len_x * len_y
+    cell_rows = ncomp * plane
     grid_copies = [
         pltpu.make_async_copy(
-            grid_hbm.at[pl.ds(c * plane, plane), :], grid_ref.at[pl.ds(c * plane, plane), :], sems.at[3 + c]
+            grid_hbm.at[pl.ds(c * plane, plane), :], grid_ref.at[pl.ds(c * plane, plane), :], sems.at[5 + c]
+        )
+        for c in range(ncomp)
+    ]
+    end = jnp.where(lax.axis_index("gx") == 0, 0, plane - len_y)
+    wrap_copies = [
+        pltpu.make_async_copy(
+            grid_ref.at[pl.ds(pl.multiple_of(c * plane + end, BLK), len_y), :],
+            wrap.at[pl.ds(c * len_y, len_y), :],
+            sems.at[5 + ncomp + c],
+        )
+        for c in range(ncomp)
+    ]
+    onward = [
+        pltpu.make_async_copy(
+            grid_ref.at[pl.ds(c * plane, plane), :], carried.at[pl.ds(c * plane, plane), :], sems.at[5 + 2 * ncomp + c]
         )
         for c in range(ncomp)
     ]
@@ -61,6 +77,8 @@
     @pl.when(lax.axis_index("dom") == 1)
     def _():
         for copy in copies:
+            copy.start()
+        for copy in grid_copies:
             copy.start()
         for copy in copies:
             copy.wait()
@@ -80,8 +98,18 @@
             for k in range(depth):
                 entry = source_ref[0, 0, j, k]
                 spot = jnp.where(entry >= 0, table[jnp.clip(entry, 0, n_yz * CAP)], -1)
-                plan[j * depth + k : j * depth + k + 1, :] = jnp.full((1, LANES), spot, jnp.int32)
-            plan[slots * depth + j : slots * depth + j + 1, :] = jnp.full((1, LANES), target_ref[0, 0, j], jnp.int32)
+                plan[j * depth + k : j * depth + k + 1, :] = jnp.full((1, LANES), spot.astype(jnp.float32))
+            plan[slots * depth + j : slots * depth + j + 1, :] = jnp.full(
+                (1, LANES), target_ref[0, 0, j].astype(jnp.float32)
+            )
+        told = pltpu.make_async_copy(plan, carried.at[pl.ds(cell_rows, plan.shape[0]), :], sems.at[4])
+        told.start()
+        for arriving, leaving in zip(grid_copies, onward):
+            arriving.wait()
+            leaving.start()
+        told.wait()
+        for copy in onward:
+            copy.wait()
 
     @pl.when(lax.axis_index("dom") == 0)
     def _():
@@ -109,8 +137,10 @@
             else:
                 step = lax.rem(owner - me + n_yz, n_yz)
             spots.append(jnp.clip(step * CAP + rank, 0, n_yz * CAP - 1))
-        for copy in grid_copies:
-            copy.wait()
+        for arriving, leaving, wrapping in zip(grid_copies, onward, wrap_copies):
+            arriving.wait()
+            leaving.start()
+            wrapping.start()
         total = jnp.zeros((n_bx * n_by * half * ncomp, SR * LANES), jnp.float32)
         for ap in range(2):
             for cy in range(BLK):
@@ -129,21 +159,23 @@
             send[spots[b]] = total[
                 column_block * rows : (column_block + 1) * rows, br * LANES : (br + 1) * LANES
             ]
-        for step in range(n_yz):
-            for slot in range(CAP):
-                outs[step][slot * rows : (slot + 1) * rows, :] = send[step * CAP + slot]
-        end = jnp.where(lax.axis_index("gx") == 0, 0, plane - len_y)
-        for c in range(ncomp):
-            wrap[c * len_y : (c + 1) * len_y, :] = grid_ref[
-                pl.ds(pl.multiple_of(c * plane + end, BLK), len_y), :
-            ]
-
-
-def stage_kernel(weight_hbm, grid_hbm, plan_hbm, weight_ref, grid_ref, plan_ref, sems):
-    blocks = weight_ref.shape[0]
-    grid_copy = pltpu.make_async_copy(grid_hbm, grid_ref, sems.at[blocks])
+        sends = [
+            pltpu.make_async_copy(send.at[pl.ds(step * CAP, CAP)], outs[step], sems.at[5 + 3 * ncomp + step])
+            for step in range(n_yz)
+        ]
+        for copy in sends:
+            copy.start()
+        for copy in wrap_copies + onward + sends:
+            copy.wait()
+
+
+def stage_kernel(weight_hbm, carried, weight_ref, grid_ref, plan_ref, sems):
+    blocks, cell_rows, plan_rows = weight_ref.shape[0], grid_ref.shape[0], plan_ref.shape[0]
+    grid_copy = pltpu.make_async_copy(carried.at[pl.ds(0, cell_rows), :], grid_ref, sems.at[blocks])
     copies = [pltpu.make_async_copy(weight_hbm.at[i], weight_ref.at[i], sems.at[i]) for i in range(blocks)]
-    copies.append(pltpu.make_async_copy(plan_hbm, plan_ref, sems.at[blocks + 1]))
+    copies.append(
+        pltpu.make_async_copy(carried.at[pl.ds(cell_rows, plan_rows), :], plan_ref, sems.at[blocks + 1])
+    )
     grid_copy.start()
 
     @pl.when(lax.axis_index("dom") == 1)
@@ -171,7 +203,7 @@
         copy = pltpu.make_async_copy(plan_vmem, plan, sem)
         copy.start()
         held = [
-            got[step][slot * rows : (slot + 1) * rows, :].astype(jnp.float32)
+            got[step][slot].astype(jnp.float32)
             for step in range(n_yz)
             for slot in range(CAP)
         ]
@@ -183,7 +215,7 @@
                 spot = jnp.broadcast_to(plan_vmem[entry : entry + 1, :], (rows, LANES))
                 block = jnp.zeros((rows, LANES), jnp.float32)
                 for place, candidate in enumerate(held):
-                    block = jnp.where(spot == place, candidate, block)
+                    block = jnp.where(spot == float(place), candidate, block)
                 cells = jnp.concatenate(
                     [block[a2 * ncomp : (a2 + 1) * ncomp, :] for a2 in range(half)], axis=1
                 ).astype(jnp.bfloat16)
@@ -207,7 +239,7 @@
         lane = lax.broadcasted_iota(jnp.int32, (ncomp, LANES), 1)
         per_y, per_z = len_y // BLK, len_z // BLK
         for j in range(slots):
-            target = plan[slots * depth + j, 0]
+            target = plan[slots * depth + j, 0].astype(jnp.int32)
 
             @pl.when(target >= 0)
             def _():
@@ -282,7 +314,7 @@
     return out
 
 
-def inner_kernel(dims, filled, out):
+def inner_kernel(dims, filled, out, rim_x_low, rim_x_high, rim_y_low, rim_y_high, part, sems):
     ncomp, len_x, len_y, len_z = dims
     plane = len_x * len_y
     half_ratio = jnp.where(lax.axis_index("dom") == 0, 0.5 * CORONA_RATIO, 0.5 * HELIO_RATIO).astype(jnp.float32)
@@ -321,9 +353,11 @@
             below = jnp.where(lane == 0, own, pltpu.roll(face, 1, 1))
             total[c] = total[c] + (face - below)
         for c in range(ncomp):
-            spot = pl.ds(pl.multiple_of(c * plane + x * len_y, BLK), len_y)
-            out[spot, :] = cells[c] + half_ratio * total[c]
+            part[c, x] = cells[c] + half_ratio * total[c]
         return next_carry
+
+    def line_copy(x):
+        return pltpu.make_async_copy(part.at[:, x], out.at[:, x], sems.at[x])
 
     cells = load(0)
     prims = primitives(cells)
@@ -340,18 +374,32 @@
         cells, prims, flux, speed, low = carry
         return cells, prims, flux[:4] + [None] + flux[4:], speed, low
 
-    carry = lax.fori_loop(
-        0, len_x - 1, lambda x, carry: pack(step(x, unpack(carry), False)), pack(carry)
-    )
+    def line(x, carry):
+        carry = pack(step(x, unpack(carry), False))
+
+        @pl.when(x > 0)
+        def _():
+            line_copy(x).start()
+
+        return carry
+
+    carry = lax.fori_loop(0, len_x - 1, line, pack(carry), unroll=3)
     step(len_x - 1, unpack(carry), True)
-
-
-def edge_kernel(dims, part, x_one, x_two, y_one, y_two, from_x_one, from_x_two, from_y_one, from_y_two, wrap, out):
+    for c in range(ncomp):
+        rim_x_low[c] = part[c, 0]
+        rim_x_high[c] = part[c, len_x - 1]
+        rim_y_low[c] = part[c, :, 0, :]
+        rim_y_high[c] = part[c, :, len_y - 1, :]
+    for x in range(1, len_x - 1):
+        line_copy(x).wait()
+
+
+def edge_kernel(dims, part, rim_x_low, rim_x_high, rim_y_low, rim_y_high, *rest):
     ncomp, len_x, len_y, len_z = dims
-    plane = len_x * len_y
+    x_one, x_two, y_one, y_two, from_x_one, from_x_two, from_y_one, from_y_two, wrap = rest[:9]
+    out, row_x_low, row_x_high, row_y_low, row_y_high, sems = rest[9:]
     helio = lax.axis_index("dom") == 1
     half_ratio = jnp.where(helio, 0.5 * HELIO_RATIO, 0.5 * CORONA_RATIO).astype(jnp.float32)
-    out[...] = part[...]
 
     def state(cells, direction):
         flux, speed = flux_of(cells, primitives(cells), direction)
@@ -369,20 +417,34 @@
 
     def both(x_low, x_high, y_low, y_high, from_x_low, from_x_high, from_y_low, from_y_high, x_end):
         column, line = lax.axis_index("gx"), lax.axis_index("yz")
+        low_end, high_end = line == 0, line == lax.axis_size("yz") - 1
+        y_lows = faces(y_low, from_y_low, low_end, None, 1, False, len_x)
+        y_highs = faces(y_high, from_y_high, high_end, None, 1, True, len_x)
+        for c in range(ncomp):
+            row_y_low[c] = (rim_y_low[c] + y_lows[c])[1 : len_x - 1]
+            row_y_high[c] = (rim_y_high[c] + y_highs[c])[1 : len_x - 1]
+        inner_x = pl.ds(1, len_x - 2)
+        copies = [
+            pltpu.make_async_copy(row_y_low, out.at[:, inner_x, 0], sems.at[0]),
+            pltpu.make_async_copy(row_y_high, out.at[:, inner_x, len_y - 1], sems.at[1]),
+        ]
+        copies[0].start()
+        copies[1].start()
         low_end, high_end = column == 0, column == lax.axis_size("gx") - 1
-        for c, change in enumerate(faces(x_low, from_x_low, low_end, x_end, 0, False, len_y)):
-            spot = pl.ds(c * plane, len_y)
-            out[spot, :] = out[spot, :] + change
-        for c, change in enumerate(faces(x_high, from_x_high, high_end, x_end, 0, True, len_y)):
-            spot = pl.ds((c + 1) * plane - len_y, len_y)
-            out[spot, :] = out[spot, :] + change
-        low_end, high_end = line == 0, line == lax.axis_size("yz") - 1
-        for c, change in enumerate(faces(y_low, from_y_low, low_end, None, 1, False, len_x)):
-            spot = pl.ds(c * plane, len_x, stride=len_y)
-            out[spot, :] = out[spot, :] + change
-        for c, change in enumerate(faces(y_high, from_y_high, high_end, None, 1, True, len_x)):
-            spot = pl.ds(c * plane + len_y - 1, len_x, stride=len_y)
-            out[spot, :] = out[spot, :] + change
+        x_lows = faces(x_low, from_x_low, low_end, x_end, 0, False, len_y)
+        x_highs = faces(x_high, from_x_high, high_end, x_end, 0, True, len_y)
+        for row, rim, changes, x, sem in (
+            (row_x_low, rim_x_low, x_lows, 0, 2),
+            (row_x_high, rim_x_high, x_highs, len_x - 1, 3),
+        ):
+            for c in range(ncomp):
+                row[c] = rim[c] + changes[c]
+                row[c, 0:1] = row[c, 0:1] + y_lows[c][x : x + 1]
+                row[c, len_y - 1 : len_y] = row[c, len_y - 1 : len_y] + y_highs[c][x : x + 1]
+            copies.append(pltpu.make_async_copy(row, out.at[:, x], sems.at[sem]))
+            copies[-1].start()
+        for copy in copies:
+            copy.wait()
 
     @pl.when(helio)
     def _():
@@ -408,21 +470,23 @@
     plan_rows = -(-slots * (depth + 1) // BLK) * BLK
     face_x = jax.ShapeDtypeStruct((ncomp * len_y, len_z), jnp.float32)
     face_y = jax.ShapeDtypeStruct((ncomp * len_x, len_z), jnp.float32)
-    *packed, plan, wrap = pl.pallas_call(
+    carried_rows = max(cell_rows + plan_rows, 8 * MIB // (4 * LANES))
+    *packed, carried, wrap = pl.pallas_call(
         functools.partial(pack_kernel, dims + (n_yz, shells, slots, depth)),
-        out_shape=[jax.ShapeDtypeStruct((CAP * rows, LANES), jnp.bfloat16)] * n_yz
-        + [jax.ShapeDtypeStruct((plan_rows, LANES), jnp.int32), face_x],
+        out_shape=[jax.ShapeDtypeStruct((CAP, rows, LANES), jnp.bfloat16)] * n_yz
+        + [jax.ShapeDtypeStruct((carried_rows, LANES), jnp.float32), face_x],
         in_specs=[HB] * 4,
-        out_specs=[VM] * (n_yz + 2),
+        out_specs=[HB] * (n_yz + 2),
         scratch_shapes=[
             pltpu.VMEM((cell_rows, len_z), jnp.float32),
             pltpu.SMEM(shell_owner.shape, jnp.int32),
             pltpu.SMEM(block_sources.shape, jnp.int32),
             pltpu.SMEM(block_targets.shape, jnp.int32),
             pltpu.SMEM((n_yz * CAP + 1,), jnp.int32),
+            pltpu.VMEM((plan_rows, LANES), jnp.float32),
             pltpu.VMEM((2 * BLK, LANES, SR * LANES), jnp.bfloat16),
             pltpu.VMEM((n_yz * CAP, rows, LANES), jnp.bfloat16),
-            pltpu.SemaphoreType.DMA((3 + ncomp,)),
+            pltpu.SemaphoreType.DMA((5 + 3 * ncomp + n_yz,)),
         ],
         compiler_params=pltpu.CompilerParams(vmem_limit_bytes=VMEM_BYTES - 8 * MIB),
         name="pack_shell",
@@ -435,18 +499,22 @@
         moved.append(lax.ppermute(packed[step], ("dom", "yz"), pairs))
     wrap = lax.ppermute(wrap, ("dom", "gx"), wrap_pairs(n_gx))
 
-    staged = (weights, grid, plan)
+    staged = [
+        jax.ShapeDtypeStruct(weights.shape, weights.dtype),
+        jax.ShapeDtypeStruct((cell_rows, len_z), jnp.float32),
+        jax.ShapeDtypeStruct((plan_rows, LANES), jnp.float32),
+    ]
     staged_bytes = sum(x.size * x.dtype.itemsize for x in staged)
     weights, grid, plan = pl.pallas_call(
         stage_kernel,
-        out_shape=[jax.ShapeDtypeStruct(x.shape, x.dtype) for x in staged],
-        in_specs=[HB] * 3,
+        out_shape=staged,
+        in_specs=[HB] * 2,
         out_specs=[VM] * 3,
         scratch_shapes=[pltpu.SemaphoreType.DMA((slots * depth + 2,))],
         compiler_params=pltpu.CompilerParams(vmem_limit_bytes=VMEM_BYTES - 13 * staged_bytes // 4),
         cost_estimate=pl.CostEstimate(flops=0, bytes_accessed=4 * interp_weights.size, transcendentals=0),
         name="stage_operands",
-    )(*staged)
+    )(weights, carried)
 
     filled, x_one, x_two, y_one, y_two = pl.pallas_call(
         functools.partial(fill_kernel, dims + (n_yz, slots, depth)),
@@ -455,7 +523,7 @@
         out_specs=[VM] * 5,
         scratch_shapes=[
             pltpu.VMEM((2 * BLK, slots * rows, LANES), jnp.float32),
-            pltpu.SMEM((plan_rows, LANES), jnp.int32),
+            pltpu.SMEM((plan_rows, LANES), jnp.float32),
             pltpu.SemaphoreType.DMA,
         ],
         input_output_aliases={2: 0},
@@ -469,24 +537,41 @@
     from_y_one = lax.ppermute(y_one, ("dom", "yz"), once_y)
     from_y_two = lax.ppermute(y_two, ("dom", "yz"), [(b, a) for a, b in once_y])
 
-    part = pl.pallas_call(
+    whole = jax.ShapeDtypeStruct((ncomp, len_x, len_y, len_z), jnp.float32)
+    rim_x = jax.ShapeDtypeStruct((ncomp, len_y, len_z), jnp.float32)
+    rim_y = jax.ShapeDtypeStruct((ncomp, len_x, len_z), jnp.float32)
+    part, *rims = pl.pallas_call(
         functools.partial(inner_kernel, dims),
-        out_shape=jax.ShapeDtypeStruct((cell_rows, len_z), jnp.float32),
+        out_shape=[whole, rim_x, rim_x, rim_y, rim_y],
         in_specs=[VM],
-        out_specs=VM,
-        cost_estimate=pl.CostEstimate(flops=300 * cell_rows * len_z, bytes_accessed=8 * cell_rows * len_z, transcendentals=0),
+        out_specs=[HB] + [VM] * 4,
+        scratch_shapes=[
+            pltpu.VMEM((ncomp, len_x, len_y, len_z), jnp.float32),
+            pltpu.SemaphoreType.DMA((len_x,)),
+        ],
         compiler_params=pltpu.CompilerParams(vmem_limit_bytes=8 * MIB),
+        cost_estimate=pl.CostEstimate(
+            flops=300 * cell_rows * len_z, bytes_accessed=8 * cell_rows * len_z, transcendentals=0
+        ),
         name="inner_faces",
     )(filled)
 
     updated = pl.pallas_call(
         functools.partial(edge_kernel, dims),
-        out_shape=jax.ShapeDtypeStruct((cell_rows, len_z), jnp.float32),
-        in_specs=[VM] * 10,
-        out_specs=VM,
+        out_shape=whole,
+        in_specs=[HB] + [VM] * 13,
+        out_specs=HB,
+        scratch_shapes=[
+            pltpu.VMEM((ncomp, len_y, len_z), jnp.float32),
+            pltpu.VMEM((ncomp, len_y, len_z), jnp.float32),
+            pltpu.VMEM((ncomp, len_x - 2, len_z), jnp.float32),
+            pltpu.VMEM((ncomp, len_x - 2, len_z), jnp.float32),
+            pltpu.SemaphoreType.DMA((4,)),
+        ],
+        input_output_aliases={0: 0},
         compiler_params=pltpu.CompilerParams(vmem_limit_bytes=8 * MIB),
         name="edge_faces",
-    )(part, x_one, x_two, y_one, y_two, from_x_one, from_x_two, from_y_one, from_y_two, wrap)
+    )(part, *rims, x_one, x_two, y_one, y_two, from_x_one, from_x_two, from_y_one, from_y_two, wrap)
     return updated.reshape(1, ncomp, len_x, len_y, len_z)
 
 

time: 22.2 us -> 21.1 us (0.950)
  the two profiles are of different devices: /device:TPU:0 before, /device:TPU:4 now
where the time goes in v4:
time: 21.1 us; the launch traced here: 20.9 us
  starting transfers between devices  11.1 us (53%)
  Pallas kernels  7.63 us (36%)
  waiting for transfers between devices  2.1 us (10%)
    ppermute x1, starting transfers between devices, local(): wrap = lax.ppermute(wrap, ('dom', 'gx'), wrap_pairs(n_gx))  3.6 us
    ppermute x4, starting transfers between devices, local(): moved.append(lax.ppermute(packed[step], ('dom', 'yz'), pairs))  3.39 us
    pallas_call x1, Pallas kernels, local(): pl.pallas_call(functools.partial(pack_kernel, dims + (n_yz, shells, slots...  2.9 us
    pallas_call x1, Pallas kernels, local(): pl.pallas_call(functools.partial(inner_kernel, dims), out_shape=[whole, r...  2.44 us
    ppermute x1, waiting for transfers between devices, local(): from_y_two = lax.ppermute(y_two, ('dom', 'yz'), [(b, a) for a, b in once_y])  2.08 us
    ppermute x1, starting transfers between devices, local(): from_y_one = lax.ppermute(y_one, ('dom', 'yz'), once_y)  1.43 us
    ppermute x1, starting transfers between devices, local(): from_x_two = lax.ppermute(x_two, ('dom', 'gx'), [(b, a) for a, b in once_x])  1.38 us
    pallas_call x1, Pallas kernels, local(): pl.pallas_call(stage_kernel, out_shape=staged, in_specs=[HB] * 2, out_spe...  1.31 us
  transfers between devices with their start and end apart: 9, of which 1 were waited for; matrix products, arithmetic and copies ran while one was open for 0% of the time, Pallas kernels for 18%

profile of v4, /device:TPU:4, one launch (start us, length us, event | category | flops | bytes accessed | tf_op | source)
XLA Modules:
  0.0 20.9 jit_solution(4834938338357730282)
XLA Ops:
  0.0 2.9 %pack_shell.1 = (bf16[2,32,128]{2,1,0:T(8,128)(2,1)}, bf16[2,32,128]{2,1,0:T(8,128)(2,1)}, bf16[2,32,128]{2,1,0:T(8,128)(2,1)}, bf16[2,32,128]{2,1,0:T(8,128)(2,...) custom-call(s32[1,4,8]{2,1,0:T(4,128)} %owner_hbm.1, s32[1,1,2,4]{3,2,1,0:T(2,128)} %source_hbm.1, s32[1,1,2]{2,1,0:T(1,128)} %target_hbm.1, ...), custom_call_target="tpu_custom_call" | custom-call | tf_op jit(solution)/shard_map/pack_shell/pallas_call | solution.py:474
  2.9 0.1 collective-permute-start
  3.0 1.6 %collective-permute-start.1 = (bf16[2,32,128]{2,1,0:T(8,128)(2,1)}, bf16[2,32,128]{2,1,0:T(8,128)(2,1)S(1)}, u32[]{:S(2)}, u32[]{:S(2)}) collective-permute-start(bf16[2,32,128]{2,1,0:T(8,128)(2,1)} %get-tuple-element.29), channel_id=1, source_target_pairs={{0,17},{1,16},{2,19},{3,18},{17,0},{16,1},{19,2},{18,3},{4,21},{5,... | collective-permute-start | bytes 49160 | tf_op jit(solution)/shard_map/ppermute | solution.py:499
  4.6 0.2 collective-permute-start.2
  4.8 1.5 %collective-permute-start.3 = (bf16[2,32,128]{2,1,0:T(8,128)(2,1)}, bf16[2,32,128]{2,1,0:T(8,128)(2,1)S(1)}, u32[]{:S(2)}, u32[]{:S(2)}) collective-permute-start(bf16[2,32,128]{2,1,0:T(8,128)(2,1)} %get-tuple-element.31), channel_id=1, source_target_pairs={{0,19},{1,18},{2,17},{3,16},{19,0},{18,1},{17,2},{16,3},{4,23},{5,... | collective-permute-start | bytes 49160 | tf_op jit(solution)/shard_map/ppermute | solution.py:499
  6.3 3.6 %collective-permute-start.8 = (f32[128,128]{1,0:T(8,128)}, f32[128,128]{1,0:T(8,128)S(1)}, u32[]{:S(2)}, u32[]{:S(2)}) collective-permute-start(f32[128,128]{1,0:T(8,128)} %get-tuple-element.42), channel_id=1, source_target_pairs={{0,12},{4,8},{16,20},{24,28},{12,0},{8,4},{20,16},{28,24},{1,13},{... | collective-permute-start | bytes 196616 | tf_op jit(solution)/shard_map/ppermute | solution.py:500
  9.9 1.3 %stage_operands.1 = (bf16[8,512,512]{2,1,0:T(8,128)(2,1)S(1)}, f32[2048,128]{1,0:T(8,128)S(1)}, f32[16,128]{1,0:T(8,128)S(1)}) custom-call(bf16[8,512,512]{2,1,0:T(8,128)(2,1)} %bitcast.3, f32[16384,128]{1,0:T(8,128)} %get-tuple-element.24.carried), custom_call_target="tpu_custom_call" | custom-call | bytes 8388608 | tf_op jit(solution)/shard_map/stage_operands/pallas_call | solution.py:508
  11.2 0.0 collective-permute-done.rest_0_
  11.2 0.0 collective-permute-done.1.rest_1_
  11.3 0.0 collective-permute-done.2.rest_2_
  11.3 0.0 collective-permute-done.3.rest_3_
  11.3 0.1 fill_blocks.1
  11.4 0.7 %collective-permute-start.4 = (f32[128,128]{1,0:T(8,128)S(1)}, f32[128,128]{1,0:T(8,128)S(1)}, u32[]{:S(2)}, u32[]{:S(2)}) collective-permute-start(f32[128,128]{1,0:T(8,128)S(1)} %get-tuple-element.38.rest_0_), channel_id=1, source_target_pairs={{16,20},{20,24},{24,28},{28,12},{4,0},{8,4},{12,8},{0,16},{17,21},... | collective-permute-start | bytes 196616 | tf_op jit(solution)/shard_map/ppermute | solution.py:535
  12.0 1.4 %collective-permute-start.5 = (f32[128,128]{1,0:T(8,128)S(1)}, f32[128,128]{1,0:T(8,128)S(1)}, u32[]{:S(2)}, u32[]{:S(2)}) collective-permute-start(f32[128,128]{1,0:T(8,128)S(1)} %get-tuple-element.39.rest_1_), channel_id=1, source_target_pairs={{20,16},{24,20},{28,24},{12,28},{0,4},{4,8},{8,12},{16,0},{21,17},... | collective-permute-start | bytes 196616 | tf_op jit(solution)/shard_map/ppermute | solution.py:536
  13.4 1.4 %collective-permute-start.6 = (f32[128,128]{1,0:T(8,128)S(1)}, f32[128,128]{1,0:T(8,128)S(1)}, u32[]{:S(2)}, u32[]{:S(2)}) collective-permute-start(f32[128,128]{1,0:T(8,128)S(1)} %get-tuple-element.40.rest_2_), channel_id=1, source_target_pairs={{16,17},{17,18},{18,19},{19,3},{1,0},{2,1},{3,2},{0,16},{20,21},{2... | collective-permute-start | bytes 196616 | tf_op jit(solution)/shard_map/ppermute | solution.py:537
  14.8 0.6 %collective-permute-start.7 = (f32[128,128]{1,0:T(8,128)S(1)}, f32[128,128]{1,0:T(8,128)S(1)}, u32[]{:S(2)}, u32[]{:S(2)}) collective-permute-start(f32[128,128]{1,0:T(8,128)S(1)} %get-tuple-element.41.rest_3_), channel_id=1, source_target_pairs={{17,16},{18,17},{19,18},{3,19},{0,1},{1,2},{2,3},{16,0},{21,20},{2... | collective-permute-start | bytes 196616 | tf_op jit(solution)/shard_map/ppermute | solution.py:538
  15.4 2.4 %inner_faces.1 = (f32[8,16,16,128]{3,2,1,0:T(8,128)}, f32[8,16,128]{2,1,0:T(8,128)S(1)}, f32[8,16,128]{2,1,0:T(8,128)S(1)}, f32[8,16,128]{2,1,0:T(8,128)S(1)}, f32[8,16,128]{2,1,0:T(8,128)S(1)}) custom-call(f32[2048,128]{1,0:T(8,128)S(1)} %get-tuple-element.32.filled), custom_call_target="tpu_custom_call" | custom-call | flops 78643200 | bytes 2097152 | tf_op jit(solution)/shard_map/inner_faces/pallas_call | solution.py:543
  17.9 0.0 collective-permute-done.8.rest_8_
  17.9 0.0 collective-permute-done.4.rest_4_
  17.9 0.0 collective-permute-done.5.rest_5_
  17.9 0.0 collective-permute-done.6.rest_6_
  17.9 2.1 %collective-permute-done.7.rest_7_ = f32[128,128]{1,0:T(8,128)S(1)} collective-permute-done((f32[128,128]{1,0:T(8,128)S(1)}, f32[128,128]{1,0:T(8,128)S(1)}, u32[]{:S(2)}, u32[]{:S(2)}) %collective-permute-start.7) | collective-permute-done | bytes 65568 | tf_op jit(solution)/shard_map/ppermute | solution.py:538
  20.0 0.9 %edge_faces.1 = f32[8,16,16,128]{3,2,1,0:T(8,128)} custom-call(f32[8,16,16,128]{3,2,1,0:T(8,128)} %get-tuple-element.33.part, f32[8,16,128]{2,1,0:T(8,128)S(1)} %get-tuple-element.34.rim_x_low, f32[8,16,128]{2,1,0:T(8,128)S(1)} %get-tuple-element.35.rim_x_high, f32[8,16,128]{2,1,0:T(8,128)S(1)} %get-tuple-element.36.rim_y_low, ...), custom_call_target="tpu_custom_call", output_to_operand_aliasing={{}: (0, {})} | custom-call | tf_op jit(solution)/shard_map/edge_faces/pallas_call | solution.py:559
Async XLA Ops:
  2.9 8.3 %collective-permute-start = (bf16[2,32,128]{2,1,0:T(8,128)(2,1)}, bf16[2,32,128]{2,1,0:T(8,128)(2,1)S(1)}, u32[]{:S(2)}, u32[]{:S(2)}) collective-permute-start(bf16[2,32,128]{2,1,0:T(8,128)(2,1)} %get-tuple-element.28), channel_id=1, source_target_pairs={{0,16},{1,17},{2,18},{3,19},{16,0},{17,1},{18,2},{19,3},{4,20},{5,... | collective-permute-start | bytes 49160 | tf_op jit(solution)/shard_map/ppermute | solution.py:499
  3.0 8.3 %collective-permute-start.1 = (bf16[2,32,128]{2,1,0:T(8,128)(2,1)}, bf16[2,32,128]{2,1,0:T(8,128)(2,1)S(1)}, u32[]{:S(2)}, u32[]{:S(2)}) collective-permute-start(bf16[2,32,128]{2,1,0:T(8,128)(2,1)} %get-tuple-element.29), channel_id=1, source_target_pairs={{0,17},{1,16},{2,19},{3,18},{17,0},{16,1},{19,2},{18,3},{4,21},{5,... | collective-permute-start | bytes 49160 | tf_op jit(solution)/shard_map/ppermute | solution.py:499
  4.6 6.7 %collective-permute-start.2 = (bf16[2,32,128]{2,1,0:T(8,128)(2,1)}, bf16[2,32,128]{2,1,0:T(8,128)(2,1)S(1)}, u32[]{:S(2)}, u32[]{:S(2)}) collective-permute-start(bf16[2,32,128]{2,1,0:T(8,128)(2,1)} %get-tuple-element.30), channel_id=1, source_target_pairs={{0,18},{1,19},{2,16},{3,17},{18,0},{19,1},{16,2},{17,3},{4,22},{5,... | collective-permute-start | bytes 49160 | tf_op jit(solution)/shard_map/ppermute | solution.py:499
  4.8 6.5 %collective-permute-start.3 = (bf16[2,32,128]{2,1,0:T(8,128)(2,1)}, bf16[2,32,128]{2,1,0:T(8,128)(2,1)S(1)}, u32[]{:S(2)}, u32[]{:S(2)}) collective-permute-start(bf16[2,32,128]{2,1,0:T(8,128)(2,1)} %get-tuple-element.31), channel_id=1, source_target_pairs={{0,19},{1,18},{2,17},{3,16},{19,0},{18,1},{17,2},{16,3},{4,23},{5,... | collective-permute-start | bytes 49160 | tf_op jit(solution)/shard_map/ppermute | solution.py:499
  6.3 11.6 %collective-permute-start.8 = (f32[128,128]{1,0:T(8,128)}, f32[128,128]{1,0:T(8,128)S(1)}, u32[]{:S(2)}, u32[]{:S(2)}) collective-permute-start(f32[128,128]{1,0:T(8,128)} %get-tuple-element.42), channel_id=1, source_target_pairs={{0,12},{4,8},{16,20},{24,28},{12,0},{8,4},{20,16},{28,24},{1,13},{... | collective-permute-start | bytes 196616 | tf_op jit(solution)/shard_map/ppermute | solution.py:500
  11.4 6.5 %collective-permute-start.4 = (f32[128,128]{1,0:T(8,128)S(1)}, f32[128,128]{1,0:T(8,128)S(1)}, u32[]{:S(2)}, u32[]{:S(2)}) collective-permute-start(f32[128,128]{1,0:T(8,128)S(1)} %get-tuple-element.38.rest_0_), channel_id=1, source_target_pairs={{16,20},{20,24},{24,28},{28,12},{4,0},{8,4},{12,8},{0,16},{17,21},... | collective-permute-start | bytes 196616 | tf_op jit(solution)/shard_map/ppermute | solution.py:535
  12.0 5.9 %collective-permute-start.5 = (f32[128,128]{1,0:T(8,128)S(1)}, f32[128,128]{1,0:T(8,128)S(1)}, u32[]{:S(2)}, u32[]{:S(2)}) collective-permute-start(f32[128,128]{1,0:T(8,128)S(1)} %get-tuple-element.39.rest_1_), channel_id=1, source_target_pairs={{20,16},{24,20},{28,24},{12,28},{0,4},{4,8},{8,12},{16,0},{21,17},... | collective-permute-start | bytes 196616 | tf_op jit(solution)/shard_map/ppermute | solution.py:536
  13.4 4.5 %collective-permute-start.6 = (f32[128,128]{1,0:T(8,128)S(1)}, f32[128,128]{1,0:T(8,128)S(1)}, u32[]{:S(2)}, u32[]{:S(2)}) collective-permute-start(f32[128,128]{1,0:T(8,128)S(1)} %get-tuple-element.40.rest_2_), channel_id=1, source_target_pairs={{16,17},{17,18},{18,19},{19,3},{1,0},{2,1},{3,2},{0,16},{20,21},{2... | collective-permute-start | bytes 196616 | tf_op jit(solution)/shard_map/ppermute | solution.py:537
  14.8 5.2 %collective-permute-start.7 = (f32[128,128]{1,0:T(8,128)S(1)}, f32[128,128]{1,0:T(8,128)S(1)}, u32[]{:S(2)}, u32[]{:S(2)}) collective-permute-start(f32[128,128]{1,0:T(8,128)S(1)} %get-tuple-element.41.rest_3_), channel_id=1, source_target_pairs={{17,16},{18,17},{19,18},{3,19},{0,1},{1,2},{2,3},{16,0},{21,20},{2... | collective-permute-start | bytes 196616 | tf_op jit(solution)/shard_map/ppermute | solution.py:538

commit v5 on v4

--- a/solution.py
+++ b/solution.py
@@ -33,10 +33,15 @@
     return pairs + [(i + 1, i) for i in range(count - 1)] + [(0, count)]
 
 
-def wrap_pairs(count):
-    pairs = [(0, count - 1)]
-    pairs += [(i, i + 1) for i in range(1, count - 2, 2)]
-    pairs += [(count + i, count + i + 1) for i in range(0, count - 1, 2)]
+def wrap_pairs(count, lines):
+    def index(domain, column, line):
+        return (domain * count + column) * lines + line
+
+    pairs = []
+    for t in range(lines):
+        pairs.append((index(0, 0, t), index(0, count - 1, t)))
+        pairs += [(index(0, g, t), index(1, g, t)) for g in range(1, count - 1)]
+    pairs += [(index(1, g, t), index(1, g, t + 1)) for g in (0, count - 1) for t in range(0, lines - 1, 2)]
     return pairs + [(b, a) for a, b in pairs]
 
 
@@ -47,31 +52,26 @@
     me = lax.axis_index("yz")
     plane = len_x * len_y
     cell_rows = ncomp * plane
+    n_bx, n_by, half = len_x // BLK, len_y // BLK, BLK // 2
+    flat = grid_ref.reshape(cell_rows, len_z)
+    onto = carried.at[pl.ds(0, ncomp)]
+    slabs = [pl.ds(bx * BLK * len_y, BLK * len_y) for bx in range(n_bx)]
     grid_copies = [
-        pltpu.make_async_copy(
-            grid_hbm.at[pl.ds(c * plane, plane), :], grid_ref.at[pl.ds(c * plane, plane), :], sems.at[5 + c]
-        )
-        for c in range(ncomp)
+        pltpu.make_async_copy(grid_hbm.at[:, slab, :], grid_ref.at[:, slab, :], sems.at[bx]) for bx, slab in enumerate(slabs)
+    ]
+    onward = [
+        pltpu.make_async_copy(grid_ref.at[:, slab, :], onto.at[:, slab, :], sems.at[n_bx + bx])
+        for bx, slab in enumerate(slabs)
     ]
     end = jnp.where(lax.axis_index("gx") == 0, 0, plane - len_y)
-    wrap_copies = [
-        pltpu.make_async_copy(
-            grid_ref.at[pl.ds(pl.multiple_of(c * plane + end, BLK), len_y), :],
-            wrap.at[pl.ds(c * len_y, len_y), :],
-            sems.at[5 + ncomp + c],
-        )
-        for c in range(ncomp)
-    ]
-    onward = [
-        pltpu.make_async_copy(
-            grid_ref.at[pl.ds(c * plane, plane), :], carried.at[pl.ds(c * plane, plane), :], sems.at[5 + 2 * ncomp + c]
-        )
-        for c in range(ncomp)
-    ]
+    first_sem = 2 * n_bx + 1
+    wrap_copy = pltpu.make_async_copy(
+        grid_ref.at[:, pl.ds(pl.multiple_of(end, BLK), len_y), :], wrap, sems.at[2 * n_bx]
+    )
     copies = [
-        pltpu.make_async_copy(owner_hbm, owner_ref, sems.at[0]),
-        pltpu.make_async_copy(source_hbm, source_ref, sems.at[1]),
-        pltpu.make_async_copy(target_hbm, target_ref, sems.at[2]),
+        pltpu.make_async_copy(owner_hbm, owner_ref, sems.at[first_sem]),
+        pltpu.make_async_copy(source_hbm, source_ref, sems.at[first_sem + 1]),
+        pltpu.make_async_copy(target_hbm, target_ref, sems.at[first_sem + 2]),
     ]
 
     @pl.when(lax.axis_index("dom") == 1)
@@ -102,7 +102,7 @@
             plan[slots * depth + j : slots * depth + j + 1, :] = jnp.full(
                 (1, LANES), target_ref[0, 0, j].astype(jnp.float32)
             )
-        told = pltpu.make_async_copy(plan, carried.at[pl.ds(cell_rows, plan.shape[0]), :], sems.at[4])
+        told = pltpu.make_async_copy(plan, carried.at[ncomp, pl.ds(0, plan.shape[0])], sems.at[first_sem + 3])
         told.start()
         for arriving, leaving in zip(grid_copies, onward):
             arriving.wait()
@@ -116,14 +116,13 @@
         copies[0].start()
         for copy in grid_copies:
             copy.start()
-        n_bx, n_by, half = len_x // BLK, len_y // BLK, BLK // 2
         z_from = len_z - SR * BLK
         row_z = lax.broadcasted_iota(jnp.int32, (LANES, SR * LANES), 0) + (len_z - LANES)
         column = lax.broadcasted_iota(jnp.int32, (LANES, SR * LANES), 1)
         hit = row_z == z_from + column // LANES * BLK + column % BLK
         place = jnp.where(hit, column % LANES // BLK, -1)
         for m in range(2 * BLK):
-            spread[m] = jnp.where(place == m, 1.0, 0.0).astype(jnp.bfloat16)
+            spread[m * LANES : (m + 1) * LANES, :] = jnp.where(place == m, 1.0, 0.0).astype(jnp.bfloat16)
         send[...] = jnp.zeros_like(send)
         copies[0].wait()
         spots = []
@@ -137,46 +136,57 @@
             else:
                 step = lax.rem(owner - me + n_yz, n_yz)
             spots.append(jnp.clip(step * CAP + rank, 0, n_yz * CAP - 1))
-        for arriving, leaving, wrapping in zip(grid_copies, onward, wrap_copies):
-            arriving.wait()
-            leaving.start()
-            wrapping.start()
-        total = jnp.zeros((n_bx * n_by * half * ncomp, SR * LANES), jnp.float32)
-        for ap in range(2):
-            for cy in range(BLK):
-                pieces = []
-                for bx in range(n_bx):
+        rows = half * ncomp
+        lines = []
+        for bx in range(n_bx):
+            grid_copies[bx].wait()
+            onward[bx].start()
+            line = []
+            for ap in range(2):
+                for cy in range(BLK):
+                    pieces = []
                     for by in range(n_by):
                         for a2 in range(half):
                             first = (bx * BLK + a2 * 2 + ap) * len_y + by * BLK + cy
-                            pieces.append(grid_ref[pl.ds(first, ncomp, stride=plane), :])
-                cells = jnp.concatenate(pieces, axis=0).astype(jnp.bfloat16)
-                total = total + jnp.dot(cells, spread[ap * BLK + cy], preferred_element_type=jnp.float32)
-        rows = half * ncomp
+                            pieces.append(flat[pl.ds(first, ncomp, stride=plane), :])
+                    line.append(jnp.concatenate(pieces, axis=0).astype(jnp.bfloat16))
+            lines.append(jnp.concatenate(line, axis=1))
+        total = jnp.dot(jnp.concatenate(lines, axis=0), spread[...], preferred_element_type=jnp.float32)
         total = total.astype(jnp.bfloat16)
         for b in range(shells):
             column_block, br = b // SR, b % SR
             send[spots[b]] = total[
                 column_block * rows : (column_block + 1) * rows, br * LANES : (br + 1) * LANES
             ]
+        wrap_copy.start()
         sends = [
-            pltpu.make_async_copy(send.at[pl.ds(step * CAP, CAP)], outs[step], sems.at[5 + 3 * ncomp + step])
+            pltpu.make_async_copy(send.at[pl.ds(step * CAP, CAP)], outs[step], sems.at[first_sem + 4 + step])
             for step in range(n_yz)
         ]
         for copy in sends:
             copy.start()
-        for copy in wrap_copies + onward + sends:
+        for copy in [wrap_copy] + onward + sends:
             copy.wait()
 
 
-def stage_kernel(weight_hbm, carried, weight_ref, grid_ref, plan_ref, sems):
-    blocks, cell_rows, plan_rows = weight_ref.shape[0], grid_ref.shape[0], plan_ref.shape[0]
-    grid_copy = pltpu.make_async_copy(carried.at[pl.ds(0, cell_rows), :], grid_ref, sems.at[blocks])
+def early(size):
+    return (lax.axis_index("dom") == 0) & (lax.axis_index("gx") < size)
+
+
+def early_kernel(carried, wrap_in, grid_ref, wrap_out, sem):
+    @pl.when(early(1))
+    def _():
+        copy = pltpu.make_async_copy(carried.at[pl.ds(0, grid_ref.shape[0])], grid_ref, sem)
+        copy.start()
+        copy.wait()
+
+
+def stage_kernel(weight_hbm, carried, grid_in, weight_ref, grid_ref, plan_ref, sems):
+    blocks, ncomp, plan_rows = weight_ref.shape[0], grid_ref.shape[0], plan_ref.shape[0]
+    grid_copy = pltpu.make_async_copy(carried.at[pl.ds(0, ncomp)], grid_ref, sems.at[blocks])
     copies = [pltpu.make_async_copy(weight_hbm.at[i], weight_ref.at[i], sems.at[i]) for i in range(blocks)]
-    copies.append(
-        pltpu.make_async_copy(carried.at[pl.ds(cell_rows, plan_rows), :], plan_ref, sems.at[blocks + 1])
-    )
-    grid_copy.start()
+    copies.append(pltpu.make_async_copy(carried.at[ncomp, pl.ds(0, plan_rows)], plan_ref, sems.at[blocks + 1]))
+    copies.append(grid_copy)
 
     @pl.when(lax.axis_index("dom") == 1)
     def _():
@@ -185,7 +195,10 @@
         for copy in copies:
             copy.wait()
 
-    grid_copy.wait()
+    @pl.when((lax.axis_index("dom") == 0) & jnp.logical_not(early(1)))
+    def _():
+        grid_copy.start()
+        grid_copy.wait()
 
 
 def fill_kernel(dims, plan_vmem, weight_ref, grid_ref, *rest):
@@ -209,17 +222,17 @@
         ]
         lines = []
         for j in range(slots):
-            total = jnp.zeros((ncomp, BLK * BLK * BLK), jnp.float32)
+            sources = []
             for k in range(depth):
                 entry = j * depth + k
                 spot = jnp.broadcast_to(plan_vmem[entry : entry + 1, :], (rows, LANES))
                 block = jnp.zeros((rows, LANES), jnp.float32)
                 for place, candidate in enumerate(held):
                     block = jnp.where(spot == float(place), candidate, block)
-                cells = jnp.concatenate(
-                    [block[a2 * ncomp : (a2 + 1) * ncomp, :] for a2 in range(half)], axis=1
-                ).astype(jnp.bfloat16)
-                total = total + jnp.dot(cells, weight_ref[entry], preferred_element_type=jnp.float32)
+                sources += [block[a2 * ncomp : (a2 + 1) * ncomp, :] for a2 in range(half)]
+            cells = jnp.concatenate(sources, axis=1).astype(jnp.bfloat16)
+            dense = weight_ref[j * depth : (j + 1) * depth].reshape(depth * weight_ref.shape[1], weight_ref.shape[2])
+            total = jnp.dot(cells, dense, preferred_element_type=jnp.float32)
             lines += [total[:, a2 * LANES : (a2 + 1) * LANES] for a2 in range(half)]
         lines = jnp.concatenate(lines, axis=0)
         top = lines.astype(jnp.bfloat16)
@@ -228,15 +241,16 @@
         bottom = (rest - middle.astype(jnp.float32)).astype(jnp.bfloat16)
         lines = jnp.concatenate([top, middle, bottom], axis=0)
         count = slots * rows
+        pitch = count + BLK
         from_lane = lax.broadcasted_iota(jnp.int32, (LANES, LANES), 0)
         to_lane = lax.broadcasted_iota(jnp.int32, (LANES, LANES), 1)
         same = from_lane % BLK == to_lane % BLK
         for m in range(2 * BLK):
             spread = jnp.where(same & (from_lane // BLK == m), 1.0, 0.0).astype(jnp.bfloat16)
             parts = jnp.dot(lines, spread, preferred_element_type=jnp.float32)
-            result[m] = parts[:count] + parts[count : 2 * count] + parts[2 * count :]
+            result[m * pitch : m * pitch + count, :] = parts[:count] + parts[count : 2 * count] + parts[2 * count :]
         copy.wait()
-        lane = lax.broadcasted_iota(jnp.int32, (ncomp, LANES), 1)
+        lane = lax.broadcasted_iota(jnp.int32, (BLK, LANES), 1)
         per_y, per_z = len_y // BLK, len_z // BLK
         for j in range(slots):
             target = plan[slots * depth + j, 0].astype(jnp.int32)
@@ -249,10 +263,12 @@
                 inside = (lane >= z_from) & (lane < z_from + BLK)
                 first = block_x * BLK * len_y + block_y * BLK
                 for a in range(BLK):
-                    spots = [pl.ds(first + a * len_y + cy, ncomp, stride=plane) for cy in range(BLK)]
-                    row = j * rows + a // 2 * ncomp
+                    spots = [
+                        pl.ds(pl.multiple_of(first + c * plane + a * len_y, BLK), BLK) for c in range(ncomp)
+                    ]
+                    row = a % 2 * BLK * pitch + j * rows + a // 2 * ncomp
                     old = [filled[spot, :] for spot in spots]
-                    new = [result[a % 2 * BLK + cy, row : row + ncomp, :] for cy in range(BLK)]
+                    new = [result[pl.ds(row + c, BLK, stride=pitch), :] for c in range(ncomp)]
                     for spot, before, after in zip(spots, old, new):
                         filled[spot, :] = jnp.where(inside, after, before)
 
@@ -462,7 +478,7 @@
     slots, depth = block_sources.shape[2:]
     volume = BLK * BLK * BLK
     cell_rows = ncomp * len_x * len_y
-    grid = field_state.reshape(cell_rows, len_z)
+    grid = field_state.reshape(ncomp, len_x * len_y, len_z)
     weights = interp_weights.reshape(slots * depth, volume, volume)
     rows = BLK // 2 * ncomp
     dims = (ncomp, len_x, len_y, len_z)
@@ -470,23 +486,27 @@
     plan_rows = -(-slots * (depth + 1) // BLK) * BLK
     face_x = jax.ShapeDtypeStruct((ncomp * len_y, len_z), jnp.float32)
     face_y = jax.ShapeDtypeStruct((ncomp * len_x, len_z), jnp.float32)
-    carried_rows = max(cell_rows + plan_rows, 8 * MIB // (4 * LANES))
+    plane = len_x * len_y
+    carried_planes = max(ncomp + 1, 8 * MIB // (4 * LANES * plane))
     *packed, carried, wrap = pl.pallas_call(
         functools.partial(pack_kernel, dims + (n_yz, shells, slots, depth)),
         out_shape=[jax.ShapeDtypeStruct((CAP, rows, LANES), jnp.bfloat16)] * n_yz
-        + [jax.ShapeDtypeStruct((carried_rows, LANES), jnp.float32), face_x],
+        + [
+            jax.ShapeDtypeStruct((carried_planes, plane, len_z), jnp.float32),
+            jax.ShapeDtypeStruct((ncomp, len_y, len_z), jnp.float32),
+        ],
         in_specs=[HB] * 4,
         out_specs=[HB] * (n_yz + 2),
         scratch_shapes=[
-            pltpu.VMEM((cell_rows, len_z), jnp.float32),
+            pltpu.VMEM((ncomp, len_x * len_y, len_z), jnp.float32),
             pltpu.SMEM(shell_owner.shape, jnp.int32),
             pltpu.SMEM(block_sources.shape, jnp.int32),
             pltpu.SMEM(block_targets.shape, jnp.int32),
             pltpu.SMEM((n_yz * CAP + 1,), jnp.int32),
             pltpu.VMEM((plan_rows, LANES), jnp.float32),
-            pltpu.VMEM((2 * BLK, LANES, SR * LANES), jnp.bfloat16),
+            pltpu.VMEM((2 * BLK * LANES, SR * LANES), jnp.bfloat16),
             pltpu.VMEM((n_yz * CAP, rows, LANES), jnp.bfloat16),
-            pltpu.SemaphoreType.DMA((5 + 3 * ncomp + n_yz,)),
+            pltpu.SemaphoreType.DMA((2 * (len_x // BLK) + 5 + n_yz,)),
         ],
         compiler_params=pltpu.CompilerParams(vmem_limit_bytes=VMEM_BYTES - 8 * MIB),
         name="pack_shell",
@@ -497,24 +517,36 @@
         pairs = [(t, n_yz + partner(t, step, n_yz)) for t in range(n_yz)]
         pairs = pairs + [(b, a) for a, b in pairs]
         moved.append(lax.ppermute(packed[step], ("dom", "yz"), pairs))
-    wrap = lax.ppermute(wrap, ("dom", "gx"), wrap_pairs(n_gx))
 
     staged = [
         jax.ShapeDtypeStruct(weights.shape, weights.dtype),
-        jax.ShapeDtypeStruct((cell_rows, len_z), jnp.float32),
+        jax.ShapeDtypeStruct((ncomp, plane, len_z), jnp.float32),
         jax.ShapeDtypeStruct((plan_rows, LANES), jnp.float32),
     ]
     staged_bytes = sum(x.size * x.dtype.itemsize for x in staged)
+    room = pltpu.CompilerParams(vmem_limit_bytes=VMEM_BYTES - 13 * staged_bytes // 4)
+    grid, wrap = pl.pallas_call(
+        early_kernel,
+        out_shape=[staged[1], jax.ShapeDtypeStruct(wrap.shape, wrap.dtype)],
+        in_specs=[HB] * 2,
+        out_specs=[VM, HB],
+        scratch_shapes=[pltpu.SemaphoreType.DMA],
+        input_output_aliases={1: 1},
+        compiler_params=room,
+        name="early_grid",
+    )(carried, wrap)
+    wrap = lax.ppermute(wrap, ("dom", "gx", "yz"), wrap_pairs(n_gx, n_yz))
     weights, grid, plan = pl.pallas_call(
         stage_kernel,
         out_shape=staged,
-        in_specs=[HB] * 2,
+        in_specs=[HB, HB, VM],
         out_specs=[VM] * 3,
         scratch_shapes=[pltpu.SemaphoreType.DMA((slots * depth + 2,))],
-        compiler_params=pltpu.CompilerParams(vmem_limit_bytes=VMEM_BYTES - 13 * staged_bytes // 4),
+        input_output_aliases={2: 1},
+        compiler_params=room,
         cost_estimate=pl.CostEstimate(flops=0, bytes_accessed=4 * interp_weights.size, transcendentals=0),
         name="stage_operands",
-    )(weights, carried)
+    )(weights, carried, grid)
 
     filled, x_one, x_two, y_one, y_two = pl.pallas_call(
         functools.partial(fill_kernel, dims + (n_yz, slots, depth)),
@@ -522,14 +554,14 @@
         in_specs=[VM, VM, VM] + [VM] * n_yz,
         out_specs=[VM] * 5,
         scratch_shapes=[
-            pltpu.VMEM((2 * BLK, slots * rows, LANES), jnp.float32),
+            pltpu.VMEM((2 * BLK * (slots * rows + BLK), LANES), jnp.float32),
             pltpu.SMEM((plan_rows, LANES), jnp.float32),
             pltpu.SemaphoreType.DMA,
         ],
         input_output_aliases={2: 0},
         compiler_params=pltpu.CompilerParams(vmem_limit_bytes=16 * MIB),
         name="fill_blocks",
-    )(plan, weights, grid, *moved)
+    )(plan, weights, grid.reshape(cell_rows, len_z), *moved)
 
     once_x, once_y = cycle(n_gx), cycle(n_yz)
     from_x_one = lax.ppermute(x_one, ("dom", "gx"), once_x)
@@ -571,7 +603,7 @@
         input_output_aliases={0: 0},
         compiler_params=pltpu.CompilerParams(vmem_limit_bytes=8 * MIB),
         name="edge_faces",
-    )(part, *rims, x_one, x_two, y_one, y_two, from_x_one, from_x_two, from_y_one, from_y_two, wrap)
+    )(part, *rims, x_one, x_two, y_one, y_two, from_x_one, from_x_two, from_y_one, from_y_two, wrap.reshape(ncomp * len_y, len_z))
     return updated.reshape(1, ncomp, len_x, len_y, len_z)
 
 

time: 21.1 us -> 19.6 us (0.929)
  the two profiles are of different devices: /device:TPU:4 before, /device:TPU:0 now
where the time goes in v5:
time: 19.6 us; the launch traced here: 19.3 us
  starting transfers between devices  11.4 us (58%)
  Pallas kernels  7.32 us (37%)
  waiting for transfers between devices  0.49 us (2%)
    ppermute x4, starting transfers between devices, local(): moved.append(lax.ppermute(packed[step], ('dom', 'yz'), pairs))  4.35 us
    ppermute x1, starting transfers between devices, local(): wrap = lax.ppermute(wrap, ('dom', 'gx', 'yz'), wrap_pairs(n_gx, n_yz))  2.94 us
    pallas_call x1, Pallas kernels, local(): pl.pallas_call(functools.partial(pack_kernel, dims + (n_yz, shells, slots...  2.58 us
    pallas_call x1, Pallas kernels, local(): pl.pallas_call(functools.partial(inner_kernel, dims), out_shape=[whole, r...  2.43 us
    ppermute x1, starting transfers between devices, local(): from_x_one = lax.ppermute(x_one, ('dom', 'gx'), once_x)  1.69 us
    ppermute x1, starting transfers between devices, local(): from_y_two = lax.ppermute(y_two, ('dom', 'yz'), [(b, a) for a, b in once_y])  1.25 us
    pallas_call x1, Pallas kernels, local(): pl.pallas_call(early_kernel, out_shape=[staged[1], jax.ShapeDtypeStruct(w...  1.23 us
    pallas_call x1, Pallas kernels, local(): pl.pallas_call(functools.partial(edge_kernel, dims), out_shape=whole, in_...  0.91 us
  transfers between devices with their start and end apart: 9, of which 1 were waited for; matrix products, arithmetic and copies ran while one was open for 0% of the time, Pallas kernels for 20%

profile of v5, /device:TPU:0, one launch (start us, length us, event | category | flops | bytes accessed | tf_op | source)
XLA Modules:
  0.0 19.3 jit_solution(972336630818837694)
XLA Ops:
  0.0 2.6 %pack_shell.1 = (bf16[2,32,128]{2,1,0:T(8,128)(2,1)}, bf16[2,32,128]{2,1,0:T(8,128)(2,1)}, bf16[2,32,128]{2,1,0:T(8,128)(2,1)}, bf16[2,32,128]{2,1,0:T(8,128)(2,...) custom-call(s32[1,4,8]{2,1,0:T(4,128)} %owner_hbm.1, s32[1,1,2,4]{3,2,1,0:T(2,128)} %source_hbm.1, ...), custom_call_target="tpu_custom_call" | custom-call | tf_op jit(solution)/shard_map/pack_shell/pallas_call | solution.py:491
  2.6 0.1 collective-permute-start
  2.7 3.1 %collective-permute-start.1 = (bf16[2,32,128]{2,1,0:T(8,128)(2,1)}, bf16[2,32,128]{2,1,0:T(8,128)(2,1)S(1)}, u32[]{:S(2)}, u32[]{:S(2)}) collective-permute-start(bf16[2,32,128]{2,1,0:T(8,128)(2,1)} %get-tuple-element.33), channel_id=1, source_target_pairs={{0,17},{1,16},{2,19},{3,18},{17,0},{16,1},{19,2},{18,3},{4,21},{5,... | collective-permute-start | bytes 49160 | tf_op jit(solution)/shard_map/ppermute | solution.py:519
  5.7 1.2 %collective-permute-start.2 = (bf16[2,32,128]{2,1,0:T(8,128)(2,1)}, bf16[2,32,128]{2,1,0:T(8,128)(2,1)S(1)}, u32[]{:S(2)}, u32[]{:S(2)}) collective-permute-start(bf16[2,32,128]{2,1,0:T(8,128)(2,1)} %get-tuple-element.34), channel_id=1, source_target_pairs={{0,18},{1,19},{2,16},{3,17},{18,0},{19,1},{16,2},{17,3},{4,22},{5,... | collective-permute-start | bytes 49160 | tf_op jit(solution)/shard_map/ppermute | solution.py:519
  6.9 0.0 collective-permute-start.3
  6.9 1.2 %early_grid.1 = (f32[8,256,128]{2,1,0:T(8,128)S(1)}, f32[8,16,128]{2,1,0:T(8,128)}) custom-call(f32[64,256,128]{2,1,0:T(8,128)} %get-tuple-element.26.carried, f32[8,16,128]{2,1,0:T(8,128)} %get-tuple-element.27.wrap_in), custom_call_target="tpu_custom_call", output_to_operand_aliasing={{1}: (1, {})} | custom-call | tf_op jit(solution)/shard_map/early_grid/pallas_call | solution.py:528
  8.2 2.9 %collective-permute-start.8 = (f32[8,16,128]{2,1,0:T(8,128)}, f32[8,16,128]{2,1,0:T(8,128)S(1)}, u32[]{:S(2)}, u32[]{:S(2)}) collective-permute-start(f32[8,16,128]{2,1,0:T(8,128)} %get-tuple-element.46), channel_id=1, source_target_pairs={{0,12},{4,20},{8,24},{1,13},{5,21},{9,25},{2,14},{6,22},{10,26},{3... | collective-permute-start | bytes 196616 | tf_op jit(solution)/shard_map/ppermute | solution.py:538
  11.1 0.1 stage_operands.1
  11.2 0.0 collective-permute-done.rest_0_
  11.2 0.0 collective-permute-done.1.rest_1_
  11.2 0.0 collective-permute-done.2.rest_2_
  11.3 0.0 collective-permute-done.3.rest_3_
  11.3 0.1 fill_blocks.1
  11.3 1.7 %collective-permute-start.4 = (f32[128,128]{1,0:T(8,128)S(1)}, f32[128,128]{1,0:T(8,128)S(1)}, u32[]{:S(2)}, u32[]{:S(2)}) collective-permute-start(f32[128,128]{1,0:T(8,128)S(1)} %get-tuple-element.42.rest_0_), channel_id=1, source_target_pairs={{16,20},{20,24},{24,28},{28,12},{4,0},{8,4},{12,8},{0,16},{17,21},... | collective-permute-start | bytes 196616 | tf_op jit(solution)/shard_map/ppermute | solution.py:567
  13.0 0.3 %collective-permute-start.5 = (f32[128,128]{1,0:T(8,128)S(1)}, f32[128,128]{1,0:T(8,128)S(1)}, u32[]{:S(2)}, u32[]{:S(2)}) collective-permute-start(f32[128,128]{1,0:T(8,128)S(1)} %get-tuple-element.43.rest_1_), channel_id=1, source_target_pairs={{20,16},{24,20},{28,24},{12,28},{0,4},{4,8},{8,12},{16,0},{21,17},... | collective-permute-start | bytes 196616 | tf_op jit(solution)/shard_map/ppermute | solution.py:568
  13.4 0.8 %collective-permute-start.6 = (f32[128,128]{1,0:T(8,128)S(1)}, f32[128,128]{1,0:T(8,128)S(1)}, u32[]{:S(2)}, u32[]{:S(2)}) collective-permute-start(f32[128,128]{1,0:T(8,128)S(1)} %get-tuple-element.44.rest_2_), channel_id=1, source_target_pairs={{16,17},{17,18},{18,19},{19,3},{1,0},{2,1},{3,2},{0,16},{20,21},{2... | collective-permute-start | bytes 196616 | tf_op jit(solution)/shard_map/ppermute | solution.py:569
  14.2 1.3 %collective-permute-start.7 = (f32[128,128]{1,0:T(8,128)S(1)}, f32[128,128]{1,0:T(8,128)S(1)}, u32[]{:S(2)}, u32[]{:S(2)}) collective-permute-start(f32[128,128]{1,0:T(8,128)S(1)} %get-tuple-element.45.rest_3_), channel_id=1, source_target_pairs={{17,16},{18,17},{19,18},{3,19},{0,1},{1,2},{2,3},{16,0},{21,20},{2... | collective-permute-start | bytes 196616 | tf_op jit(solution)/shard_map/ppermute | solution.py:570
  15.4 2.4 %inner_faces.1 = (f32[8,16,16,128]{3,2,1,0:T(8,128)}, f32[8,16,128]{2,1,0:T(8,128)S(1)}, f32[8,16,128]{2,1,0:T(8,128)S(1)}, f32[8,16,128]{2,1,0:T(8,128)S(1)}, f32[8,16,128]{2,1,0:T(8,128)S(1)}) custom-call(f32[2048,128]{1,0:T(8,128)S(1)} %get-tuple-element.36.filled), custom_call_target="tpu_custom_call" | custom-call | flops 78643200 | bytes 2097152 | tf_op jit(solution)/shard_map/inner_faces/pallas_call | solution.py:575
  17.9 0.0 collective-permute-done.8
  17.9 0.0 collective-permute-done.4.rest_4_
  17.9 0.0 collective-permute-done.5.rest_5_
  17.9 0.5 %collective-permute-done.6.rest_6_ = f32[128,128]{1,0:T(8,128)S(1)} collective-permute-done((f32[128,128]{1,0:T(8,128)S(1)}, f32[128,128]{1,0:T(8,128)S(1)}, u32[]{:S(2)}, u32[]{:S(2)}) %collective-permute-start.6) | collective-permute-done | bytes 65568 | tf_op jit(solution)/shard_map/ppermute | solution.py:569
  18.4 0.0 collective-permute-done.7.rest_7_
  18.4 0.9 %edge_faces.1 = f32[8,16,16,128]{3,2,1,0:T(8,128)} custom-call(f32[8,16,16,128]{3,2,1,0:T(8,128)} %get-tuple-element.37.part, f32[8,16,128]{2,1,0:T(8,128)S(1)} %get-tuple-element.38.rim_x_low, f32[8,16,128]{2,1,0:T(8,128)S(1)} %get-tuple-element.39.rim_x_high, f32[8,16,128]{2,1,0:T(8,128)S(1)} %get-tuple-element.40.rim_y_low, ...), custom_call_target="tpu_custom_call", output_to_operand_aliasing={{}: (0, {})} | custom-call | tf_op jit(solution)/shard_map/edge_faces/pallas_call | solution.py:591
Async XLA Ops:
  2.6 8.6 %collective-permute-start = (bf16[2,32,128]{2,1,0:T(8,128)(2,1)}, bf16[2,32,128]{2,1,0:T(8,128)(2,1)S(1)}, u32[]{:S(2)}, u32[]{:S(2)}) collective-permute-start(bf16[2,32,128]{2,1,0:T(8,128)(2,1)} %get-tuple-element.32), channel_id=1, source_target_pairs={{0,16},{1,17},{2,18},{3,19},{16,0},{17,1},{18,2},{19,3},{4,20},{5,... | collective-permute-start | bytes 49160 | tf_op jit(solution)/shard_map/ppermute | solution.py:519
  2.7 8.6 %collective-permute-start.1 = (bf16[2,32,128]{2,1,0:T(8,128)(2,1)}, bf16[2,32,128]{2,1,0:T(8,128)(2,1)S(1)}, u32[]{:S(2)}, u32[]{:S(2)}) collective-permute-start(bf16[2,32,128]{2,1,0:T(8,128)(2,1)} %get-tuple-element.33), channel_id=1, source_target_pairs={{0,17},{1,16},{2,19},{3,18},{17,0},{16,1},{19,2},{18,3},{4,21},{5,... | collective-permute-start | bytes 49160 | tf_op jit(solution)/shard_map/ppermute | solution.py:519
  5.7 5.5 %collective-permute-start.2 = (bf16[2,32,128]{2,1,0:T(8,128)(2,1)}, bf16[2,32,128]{2,1,0:T(8,128)(2,1)S(1)}, u32[]{:S(2)}, u32[]{:S(2)}) collective-permute-start(bf16[2,32,128]{2,1,0:T(8,128)(2,1)} %get-tuple-element.34), channel_id=1, source_target_pairs={{0,18},{1,19},{2,16},{3,17},{18,0},{19,1},{16,2},{17,3},{4,22},{5,... | collective-permute-start | bytes 49160 | tf_op jit(solution)/shard_map/ppermute | solution.py:519
  6.9 4.3 %collective-permute-start.3 = (bf16[2,32,128]{2,1,0:T(8,128)(2,1)}, bf16[2,32,128]{2,1,0:T(8,128)(2,1)S(1)}, u32[]{:S(2)}, u32[]{:S(2)}) collective-permute-start(bf16[2,32,128]{2,1,0:T(8,128)(2,1)} %get-tuple-element.35), channel_id=1, source_target_pairs={{0,19},{1,18},{2,17},{3,16},{19,0},{18,1},{17,2},{16,3},{4,23},{5,... | collective-permute-start | bytes 49160 | tf_op jit(solution)/shard_map/ppermute | solution.py:519
  8.2 9.7 %collective-permute-start.8 = (f32[8,16,128]{2,1,0:T(8,128)}, f32[8,16,128]{2,1,0:T(8,128)S(1)}, u32[]{:S(2)}, u32[]{:S(2)}) collective-permute-start(f32[8,16,128]{2,1,0:T(8,128)} %get-tuple-element.46), channel_id=1, source_target_pairs={{0,12},{4,20},{8,24},{1,13},{5,21},{9,25},{2,14},{6,22},{10,26},{3... | collective-permute-start | bytes 196616 | tf_op jit(solution)/shard_map/ppermute | solution.py:538
  11.3 6.5 %collective-permute-start.4 = (f32[128,128]{1,0:T(8,128)S(1)}, f32[128,128]{1,0:T(8,128)S(1)}, u32[]{:S(2)}, u32[]{:S(2)}) collective-permute-start(f32[128,128]{1,0:T(8,128)S(1)} %get-tuple-element.42.rest_0_), channel_id=1, source_target_pairs={{16,20},{20,24},{24,28},{28,12},{4,0},{8,4},{12,8},{0,16},{17,21},... | collective-permute-start | bytes 196616 | tf_op jit(solution)/shard_map/ppermute | solution.py:567
  13.0 4.8 %collective-permute-start.5 = (f32[128,128]{1,0:T(8,128)S(1)}, f32[128,128]{1,0:T(8,128)S(1)}, u32[]{:S(2)}, u32[]{:S(2)}) collective-permute-start(f32[128,128]{1,0:T(8,128)S(1)} %get-tuple-element.43.rest_1_), channel_id=1, source_target_pairs={{20,16},{24,20},{28,24},{12,28},{0,4},{4,8},{8,12},{16,0},{21,17},... | collective-permute-start | bytes 196616 | tf_op jit(solution)/shard_map/ppermute | solution.py:568
  13.4 5.0 %collective-permute-start.6 = (f32[128,128]{1,0:T(8,128)S(1)}, f32[128,128]{1,0:T(8,128)S(1)}, u32[]{:S(2)}, u32[]{:S(2)}) collective-permute-start(f32[128,128]{1,0:T(8,128)S(1)} %get-tuple-element.44.rest_2_), channel_id=1, source_target_pairs={{16,17},{17,18},{18,19},{19,3},{1,0},{2,1},{3,2},{0,16},{20,21},{2... | collective-permute-start | bytes 196616 | tf_op jit(solution)/shard_map/ppermute | solution.py:569
  14.2 4.2 %collective-permute-start.7 = (f32[128,128]{1,0:T(8,128)S(1)}, f32[128,128]{1,0:T(8,128)S(1)}, u32[]{:S(2)}, u32[]{:S(2)}) collective-permute-start(f32[128,128]{1,0:T(8,128)S(1)} %get-tuple-element.45.rest_3_), channel_id=1, source_target_pairs={{17,16},{18,17},{19,18},{3,19},{0,1},{1,2},{2,3},{16,0},{21,20},{2... | collective-permute-start | bytes 196616 | tf_op jit(solution)/shard_map/ppermute | solution.py:570

commit v6 on v5

--- a/solution.py
+++ b/solution.py
@@ -51,9 +51,9 @@
     grid_ref, owner_ref, source_ref, target_ref, table, plan, spread, send, sems = rest[n_yz + 2 :]
     me = lax.axis_index("yz")
     plane = len_x * len_y
-    cell_rows = ncomp * plane
     n_bx, n_by, half = len_x // BLK, len_y // BLK, BLK // 2
-    flat = grid_ref.reshape(cell_rows, len_z)
+    pitch = grid_ref.shape[1]
+    flat = grid_ref.reshape(ncomp * pitch, len_z)
     onto = carried.at[pl.ds(0, ncomp)]
     slabs = [pl.ds(bx * BLK * len_y, BLK * len_y) for bx in range(n_bx)]
     grid_copies = [
@@ -148,7 +148,7 @@
                     for by in range(n_by):
                         for a2 in range(half):
                             first = (bx * BLK + a2 * 2 + ap) * len_y + by * BLK + cy
-                            pieces.append(flat[pl.ds(first, ncomp, stride=plane), :])
+                            pieces.append(flat[pl.ds(first, ncomp, stride=pitch), :])
                     line.append(jnp.concatenate(pieces, axis=0).astype(jnp.bfloat16))
             lines.append(jnp.concatenate(line, axis=1))
         total = jnp.dot(jnp.concatenate(lines, axis=0), spread[...], preferred_element_type=jnp.float32)
@@ -204,7 +204,7 @@
 def fill_kernel(dims, plan_vmem, weight_ref, grid_ref, *rest):
     ncomp, len_x, len_y, len_z, n_yz, slots, depth = dims
     got = rest[:n_yz]
-    filled, x_one, x_two, y_one, y_two, result, plan, sem = rest[n_yz:]
+    filled, y_one, y_two, x_one, x_two, result, plan, sem = rest[n_yz:]
     half = BLK // 2
     rows = half * ncomp
     plane = len_x * len_y
@@ -412,7 +412,7 @@
 
 def edge_kernel(dims, part, rim_x_low, rim_x_high, rim_y_low, rim_y_high, *rest):
     ncomp, len_x, len_y, len_z = dims
-    x_one, x_two, y_one, y_two, from_x_one, from_x_two, from_y_one, from_y_two, wrap = rest[:9]
+    y_one, y_two, x_one, x_two, from_y_one, from_y_two, from_x_one, from_x_two, wrap = rest[:9]
     out, row_x_low, row_x_high, row_y_low, row_y_high, sems = rest[9:]
     helio = lax.axis_index("dom") == 1
     half_ratio = jnp.where(helio, 0.5 * HELIO_RATIO, 0.5 * CORONA_RATIO).astype(jnp.float32)
@@ -498,7 +498,7 @@
         in_specs=[HB] * 4,
         out_specs=[HB] * (n_yz + 2),
         scratch_shapes=[
-            pltpu.VMEM((ncomp, len_x * len_y, len_z), jnp.float32),
+            pltpu.VMEM((ncomp, plane + BLK, len_z), jnp.float32),
             pltpu.SMEM(shell_owner.shape, jnp.int32),
             pltpu.SMEM(block_sources.shape, jnp.int32),
             pltpu.SMEM(block_targets.shape, jnp.int32),
@@ -548,9 +548,9 @@
         name="stage_operands",
     )(weights, carried, grid)
 
-    filled, x_one, x_two, y_one, y_two = pl.pallas_call(
+    filled, y_one, y_two, x_one, x_two = pl.pallas_call(
         functools.partial(fill_kernel, dims + (n_yz, slots, depth)),
-        out_shape=[jax.ShapeDtypeStruct((cell_rows, len_z), jnp.float32), face_x, face_x, face_y, face_y],
+        out_shape=[jax.ShapeDtypeStruct((cell_rows, len_z), jnp.float32), face_y, face_y, face_x, face_x],
         in_specs=[VM, VM, VM] + [VM] * n_yz,
         out_specs=[VM] * 5,
         scratch_shapes=[
@@ -564,10 +564,10 @@
     )(plan, weights, grid.reshape(cell_rows, len_z), *moved)
 
     once_x, once_y = cycle(n_gx), cycle(n_yz)
+    from_y_one = lax.ppermute(y_one, ("dom", "yz"), once_y)
+    from_y_two = lax.ppermute(y_two, ("dom", "yz"), [(b, a) for a, b in once_y])
     from_x_one = lax.ppermute(x_one, ("dom", "gx"), once_x)
     from_x_two = lax.ppermute(x_two, ("dom", "gx"), [(b, a) for a, b in once_x])
-    from_y_one = lax.ppermute(y_one, ("dom", "yz"), once_y)
-    from_y_two = lax.ppermute(y_two, ("dom", "yz"), [(b, a) for a, b in once_y])
 
     whole = jax.ShapeDtypeStruct((ncomp, len_x, len_y, len_z), jnp.float32)
     rim_x = jax.ShapeDtypeStruct((ncomp, len_y, len_z), jnp.float32)
@@ -603,7 +603,7 @@
         input_output_aliases={0: 0},
         compiler_params=pltpu.CompilerParams(vmem_limit_bytes=8 * MIB),
         name="edge_faces",
-    )(part, *rims, x_one, x_two, y_one, y_two, from_x_one, from_x_two, from_y_one, from_y_two, wrap.reshape(ncomp * len_y, len_z))
+    )(part, *rims, y_one, y_two, x_one, x_two, from_y_one, from_y_two, from_x_one, from_x_two, wrap.reshape(ncomp * len_y, len_z))
     return updated.reshape(1, ncomp, len_x, len_y, len_z)
 
 

time: 19.6 us -> 18.9 us (0.964)
  Pallas kernels: 7.32 us -> 6.92 us
  waiting for transfers between devices: 0.49 us -> 0.17 us
    ppermute x1, starting transfers between devices: 1.69 us -> 0.16 us  [local(): from_x_one = lax.ppermute(x_one, ('dom', 'gx'), once_x)]
    ppermute x1, starting transfers between devices: 0.35 us -> 1.86 us  [local(): from_x_two = lax.ppermute(x_two, ('dom', 'gx'), [(b, a) for a, b in once_x])]
    ppermute x1, starting transfers between devices: 0.78 us -> 1.74 us  [local(): from_y_one = lax.ppermute(y_one, ('dom', 'yz'), once_y)]
    ppermute x1, starting transfers between devices: 1.25 us -> 0.35 us  [local(): from_y_two = lax.ppermute(y_two, ('dom', 'yz'), [(b, a) for a, b in once_y])]
    ppermute x1, waiting for transfers between devices: 0.47 us -> 0.01 us  [local(): from_y_one = lax.ppermute(y_one, ('dom', 'yz'), once_y)]
    pallas_call x1, Pallas kernels: 2.58 us -> 2.19 us  [local(): pl.pallas_call(functools.partial(pack_kernel, dims + (n_yz, shells, slots...]
  transfers between devices with their start and end apart: 9 -> 9, of which waited for: 1 -> 1; matrix products, arithmetic and copies ran while one was open for 0% -> 0% of each run, Pallas kernels for 20% -> 21%
where the time goes in v6:
time: 18.9 us; the launch traced here: 18.6 us
  starting transfers between devices  11.4 us (60%)
  Pallas kernels  6.92 us (37%)
    ppermute x4, starting transfers between devices, local(): moved.append(lax.ppermute(packed[step], ('dom', 'yz'), pairs))  4.36 us
    ppermute x1, starting transfers between devices, local(): wrap = lax.ppermute(wrap, ('dom', 'gx', 'yz'), wrap_pairs(n_gx, n_yz))  2.94 us
    pallas_call x1, Pallas kernels, local(): pl.pallas_call(functools.partial(inner_kernel, dims), out_shape=[whole, r...  2.43 us
    pallas_call x1, Pallas kernels, local(): pl.pallas_call(functools.partial(pack_kernel, dims + (n_yz, shells, slots...  2.19 us
    ppermute x1, starting transfers between devices, local(): from_x_two = lax.ppermute(x_two, ('dom', 'gx'), [(b, a) for a, b in once_x])  1.86 us
    ppermute x1, starting transfers between devices, local(): from_y_one = lax.ppermute(y_one, ('dom', 'yz'), once_y)  1.74 us
    pallas_call x1, Pallas kernels, local(): pl.pallas_call(early_kernel, out_shape=[staged[1], jax.ShapeDtypeStruct(w...  1.23 us
    pallas_call x1, Pallas kernels, local(): pl.pallas_call(functools.partial(edge_kernel, dims), out_shape=whole, in_...  0.91 us
  transfers between devices with their start and end apart: 9, of which 1 were waited for; matrix products, arithmetic and copies ran while one was open for 0% of the time, Pallas kernels for 21%

profile of v6, /device:TPU:0, one launch (start us, length us, event | category | flops | bytes accessed | tf_op | source)
XLA Modules:
  0.0 18.6 jit_solution(11131496492020678142)
XLA Ops:
  0.0 2.2 %pack_shell.1 = (bf16[2,32,128]{2,1,0:T(8,128)(2,1)}, bf16[2,32,128]{2,1,0:T(8,128)(2,1)}, bf16[2,32,128]{2,1,0:T(8,128)(2,1)}, bf16[2,32,128]{2,1,0:T(8,128)(2,...) custom-call(s32[1,4,8]{2,1,0:T(4,128)} %owner_hbm.1, s32[1,1,2,4]{3,2,1,0:T(2,128)} %source_hbm.1, ...), custom_call_target="tpu_custom_call" | custom-call | tf_op jit(solution)/shard_map/pack_shell/pallas_call | solution.py:491
  2.2 0.5 %collective-permute-start = (bf16[2,32,128]{2,1,0:T(8,128)(2,1)}, bf16[2,32,128]{2,1,0:T(8,128)(2,1)S(1)}, u32[]{:S(2)}, u32[]{:S(2)}) collective-permute-start(bf16[2,32,128]{2,1,0:T(8,128)(2,1)} %get-tuple-element.32), channel_id=1, source_target_pairs={{0,16},{1,17},{2,18},{3,19},{16,0},{17,1},{18,2},{19,3},{4,20},{5,... | collective-permute-start | bytes 49160 | tf_op jit(solution)/shard_map/ppermute | solution.py:519
  2.7 2.7 %collective-permute-start.1 = (bf16[2,32,128]{2,1,0:T(8,128)(2,1)}, bf16[2,32,128]{2,1,0:T(8,128)(2,1)S(1)}, u32[]{:S(2)}, u32[]{:S(2)}) collective-permute-start(bf16[2,32,128]{2,1,0:T(8,128)(2,1)} %get-tuple-element.33), channel_id=1, source_target_pairs={{0,17},{1,16},{2,19},{3,18},{17,0},{16,1},{19,2},{18,3},{4,21},{5,... | collective-permute-start | bytes 49160 | tf_op jit(solution)/shard_map/ppermute | solution.py:519
  5.3 1.2 %collective-permute-start.2 = (bf16[2,32,128]{2,1,0:T(8,128)(2,1)}, bf16[2,32,128]{2,1,0:T(8,128)(2,1)S(1)}, u32[]{:S(2)}, u32[]{:S(2)}) collective-permute-start(bf16[2,32,128]{2,1,0:T(8,128)(2,1)} %get-tuple-element.34), channel_id=1, source_target_pairs={{0,18},{1,19},{2,16},{3,17},{18,0},{19,1},{16,2},{17,3},{4,22},{5,... | collective-permute-start | bytes 49160 | tf_op jit(solution)/shard_map/ppermute | solution.py:519
  6.5 0.0 collective-permute-start.3
  6.6 1.2 %early_grid.1 = (f32[8,256,128]{2,1,0:T(8,128)S(1)}, f32[8,16,128]{2,1,0:T(8,128)}) custom-call(f32[64,256,128]{2,1,0:T(8,128)} %get-tuple-element.26.carried, f32[8,16,128]{2,1,0:T(8,128)} %get-tuple-element.27.wrap_in), custom_call_target="tpu_custom_call", output_to_operand_aliasing={{1}: (1, {})} | custom-call | tf_op jit(solution)/shard_map/early_grid/pallas_call | solution.py:528
  7.8 2.9 %collective-permute-start.8 = (f32[8,16,128]{2,1,0:T(8,128)}, f32[8,16,128]{2,1,0:T(8,128)S(1)}, u32[]{:S(2)}, u32[]{:S(2)}) collective-permute-start(f32[8,16,128]{2,1,0:T(8,128)} %get-tuple-element.46), channel_id=1, source_target_pairs={{0,12},{4,20},{8,24},{1,13},{5,21},{9,25},{2,14},{6,22},{10,26},{3... | collective-permute-start | bytes 196616 | tf_op jit(solution)/shard_map/ppermute | solution.py:538
  10.7 0.1 stage_operands.1
  10.8 0.0 collective-permute-done.rest_0_
  10.8 0.0 collective-permute-done.1.rest_1_
  10.8 0.0 collective-permute-done.2.rest_2_
  10.9 0.0 collective-permute-done.3.rest_3_
  10.9 0.1 fill_blocks.1
  11.0 1.7 %collective-permute-start.4 = (f32[128,128]{1,0:T(8,128)S(1)}, f32[128,128]{1,0:T(8,128)S(1)}, u32[]{:S(2)}, u32[]{:S(2)}) collective-permute-start(f32[128,128]{1,0:T(8,128)S(1)} %get-tuple-element.42.rest_0_), channel_id=1, source_target_pairs={{16,17},{17,18},{18,19},{19,3},{1,0},{2,1},{3,2},{0,16},{20,21},{2... | collective-permute-start | bytes 196616 | tf_op jit(solution)/shard_map/ppermute | solution.py:567
  12.7 0.3 %collective-permute-start.5 = (f32[128,128]{1,0:T(8,128)S(1)}, f32[128,128]{1,0:T(8,128)S(1)}, u32[]{:S(2)}, u32[]{:S(2)}) collective-permute-start(f32[128,128]{1,0:T(8,128)S(1)} %get-tuple-element.43.rest_1_), channel_id=1, source_target_pairs={{17,16},{18,17},{19,18},{3,19},{0,1},{1,2},{2,3},{16,0},{21,20},{2... | collective-permute-start | bytes 196616 | tf_op jit(solution)/shard_map/ppermute | solution.py:568
  13.0 0.2 collective-permute-start.6
  13.2 1.9 %collective-permute-start.7 = (f32[128,128]{1,0:T(8,128)S(1)}, f32[128,128]{1,0:T(8,128)S(1)}, u32[]{:S(2)}, u32[]{:S(2)}) collective-permute-start(f32[128,128]{1,0:T(8,128)S(1)} %get-tuple-element.45.rest_3_), channel_id=1, source_target_pairs={{20,16},{24,20},{28,24},{12,28},{0,4},{4,8},{8,12},{16,0},{21,17},... | collective-permute-start | bytes 196616 | tf_op jit(solution)/shard_map/ppermute | solution.py:570
  15.1 2.4 %inner_faces.1 = (f32[8,16,16,128]{3,2,1,0:T(8,128)}, f32[8,16,128]{2,1,0:T(8,128)S(1)}, f32[8,16,128]{2,1,0:T(8,128)S(1)}, f32[8,16,128]{2,1,0:T(8,128)S(1)}, f32[8,16,128]{2,1,0:T(8,128)S(1)}) custom-call(f32[2048,128]{1,0:T(8,128)S(1)} %get-tuple-element.36.filled), custom_call_target="tpu_custom_call" | custom-call | flops 78643200 | bytes 2097152 | tf_op jit(solution)/shard_map/inner_faces/pallas_call | solution.py:575
  17.5 0.0 collective-permute-done.8
  17.5 0.0 collective-permute-done.4.rest_4_
  17.5 0.0 collective-permute-done.5.rest_5_
  17.5 0.2 collective-permute-done.6.rest_6_
  17.7 0.0 collective-permute-done.7.rest_7_
  17.7 0.9 %edge_faces.1 = f32[8,16,16,128]{3,2,1,0:T(8,128)} custom-call(f32[8,16,16,128]{3,2,1,0:T(8,128)} %get-tuple-element.37.part, f32[8,16,128]{2,1,0:T(8,128)S(1)} %get-tuple-element.38.rim_x_low, f32[8,16,128]{2,1,0:T(8,128)S(1)} %get-tuple-element.39.rim_x_high, f32[8,16,128]{2,1,0:T(8,128)S(1)} %get-tuple-element.40.rim_y_low, ...), custom_call_target="tpu_custom_call", output_to_operand_aliasing={{}: (0, {})} | custom-call | tf_op jit(solution)/shard_map/edge_faces/pallas_call | solution.py:591
Async XLA Ops:
  2.2 8.6 %collective-permute-start = (bf16[2,32,128]{2,1,0:T(8,128)(2,1)}, bf16[2,32,128]{2,1,0:T(8,128)(2,1)S(1)}, u32[]{:S(2)}, u32[]{:S(2)}) collective-permute-start(bf16[2,32,128]{2,1,0:T(8,128)(2,1)} %get-tuple-element.32), channel_id=1, source_target_pairs={{0,16},{1,17},{2,18},{3,19},{16,0},{17,1},{18,2},{19,3},{4,20},{5,... | collective-permute-start | bytes 49160 | tf_op jit(solution)/shard_map/ppermute | solution.py:519
  2.7 8.2 %collective-permute-start.1 = (bf16[2,32,128]{2,1,0:T(8,128)(2,1)}, bf16[2,32,128]{2,1,0:T(8,128)(2,1)S(1)}, u32[]{:S(2)}, u32[]{:S(2)}) collective-permute-start(bf16[2,32,128]{2,1,0:T(8,128)(2,1)} %get-tuple-element.33), channel_id=1, source_target_pairs={{0,17},{1,16},{2,19},{3,18},{17,0},{16,1},{19,2},{18,3},{4,21},{5,... | collective-permute-start | bytes 49160 | tf_op jit(solution)/shard_map/ppermute | solution.py:519
  5.3 5.5 %collective-permute-start.2 = (bf16[2,32,128]{2,1,0:T(8,128)(2,1)}, bf16[2,32,128]{2,1,0:T(8,128)(2,1)S(1)}, u32[]{:S(2)}, u32[]{:S(2)}) collective-permute-start(bf16[2,32,128]{2,1,0:T(8,128)(2,1)} %get-tuple-element.34), channel_id=1, source_target_pairs={{0,18},{1,19},{2,16},{3,17},{18,0},{19,1},{16,2},{17,3},{4,22},{5,... | collective-permute-start | bytes 49160 | tf_op jit(solution)/shard_map/ppermute | solution.py:519
  6.5 4.3 %collective-permute-start.3 = (bf16[2,32,128]{2,1,0:T(8,128)(2,1)}, bf16[2,32,128]{2,1,0:T(8,128)(2,1)S(1)}, u32[]{:S(2)}, u32[]{:S(2)}) collective-permute-start(bf16[2,32,128]{2,1,0:T(8,128)(2,1)} %get-tuple-element.35), channel_id=1, source_target_pairs={{0,19},{1,18},{2,17},{3,16},{19,0},{18,1},{17,2},{16,3},{4,23},{5,... | collective-permute-start | bytes 49160 | tf_op jit(solution)/shard_map/ppermute | solution.py:519
  7.8 9.7 %collective-permute-start.8 = (f32[8,16,128]{2,1,0:T(8,128)}, f32[8,16,128]{2,1,0:T(8,128)S(1)}, u32[]{:S(2)}, u32[]{:S(2)}) collective-permute-start(f32[8,16,128]{2,1,0:T(8,128)} %get-tuple-element.46), channel_id=1, source_target_pairs={{0,12},{4,20},{8,24},{1,13},{5,21},{9,25},{2,14},{6,22},{10,26},{3... | collective-permute-start | bytes 196616 | tf_op jit(solution)/shard_map/ppermute | solution.py:538
  11.0 6.6 %collective-permute-start.4 = (f32[128,128]{1,0:T(8,128)S(1)}, f32[128,128]{1,0:T(8,128)S(1)}, u32[]{:S(2)}, u32[]{:S(2)}) collective-permute-start(f32[128,128]{1,0:T(8,128)S(1)} %get-tuple-element.42.rest_0_), channel_id=1, source_target_pairs={{16,17},{17,18},{18,19},{19,3},{1,0},{2,1},{3,2},{0,16},{20,21},{2... | collective-permute-start | bytes 196616 | tf_op jit(solution)/shard_map/ppermute | solution.py:567
  12.7 4.8 %collective-permute-start.5 = (f32[128,128]{1,0:T(8,128)S(1)}, f32[128,128]{1,0:T(8,128)S(1)}, u32[]{:S(2)}, u32[]{:S(2)}) collective-permute-start(f32[128,128]{1,0:T(8,128)S(1)} %get-tuple-element.43.rest_1_), channel_id=1, source_target_pairs={{17,16},{18,17},{19,18},{3,19},{0,1},{1,2},{2,3},{16,0},{21,20},{2... | collective-permute-start | bytes 196616 | tf_op jit(solution)/shard_map/ppermute | solution.py:568
  13.0 4.6 %collective-permute-start.6 = (f32[128,128]{1,0:T(8,128)S(1)}, f32[128,128]{1,0:T(8,128)S(1)}, u32[]{:S(2)}, u32[]{:S(2)}) collective-permute-start(f32[128,128]{1,0:T(8,128)S(1)} %get-tuple-element.44.rest_2_), channel_id=1, source_target_pairs={{16,20},{20,24},{24,28},{28,12},{4,0},{8,4},{12,8},{0,16},{17,21},... | collective-permute-start | bytes 196616 | tf_op jit(solution)/shard_map/ppermute | solution.py:569
  13.2 4.5 %collective-permute-start.7 = (f32[128,128]{1,0:T(8,128)S(1)}, f32[128,128]{1,0:T(8,128)S(1)}, u32[]{:S(2)}, u32[]{:S(2)}) collective-permute-start(f32[128,128]{1,0:T(8,128)S(1)} %get-tuple-element.45.rest_3_), channel_id=1, source_target_pairs={{20,16},{24,20},{28,24},{12,28},{0,4},{4,8},{8,12},{16,0},{21,17},... | collective-permute-start | bytes 196616 | tf_op jit(solution)/shard_map/ppermute | solution.py:570

commit v7 on v6

--- a/solution.py
+++ b/solution.py
@@ -195,6 +195,10 @@
         for copy in copies:
             copy.wait()
 
+    @pl.when(early(1))
+    def _():
+        grid_ref[...] = grid_in[...]
+
     @pl.when((lax.axis_index("dom") == 0) & jnp.logical_not(early(1)))
     def _():
         grid_copy.start()
@@ -210,6 +214,7 @@
     plane = len_x * len_y
 
     helio = lax.axis_index("dom") == 1
+    filled[...] = grid_ref[...]
 
     @pl.when(helio)
     def _():

time: 18.9 us -> 19.2 us (1.016)
  Pallas kernels: 6.92 us -> 7.2 us
  transfers between devices with their start and end apart: 9 -> 9, of which waited for: 1 -> 1; matrix products, arithmetic and copies ran while one was open for 0% -> 0% of each run, Pallas kernels for 21% -> 22%
where the time goes in v7:
time: 19.2 us; the launch traced here: 19 us
  starting transfers between devices  11.4 us (59%)
  Pallas kernels  7.2 us (38%)
  waiting for transfers between devices  0.33 us (2%)
    ppermute x4, starting transfers between devices, local(): moved.append(lax.ppermute(packed[step], ('dom', 'yz'), pairs))  4.36 us
    ppermute x1, starting transfers between devices, local(): wrap = lax.ppermute(wrap, ('dom', 'gx', 'yz'), wrap_pairs(n_gx, n_yz))  2.94 us
    pallas_call x1, Pallas kernels, local(): pl.pallas_call(functools.partial(inner_kernel, dims), out_shape=[whole, r...  2.43 us
    pallas_call x1, Pallas kernels, local(): pl.pallas_call(functools.partial(pack_kernel, dims + (n_yz, shells, slots...  2.19 us
    ppermute x1, starting transfers between devices, local(): from_x_two = lax.ppermute(x_two, ('dom', 'gx'), [(b, a) for a, b in once_x])  2.02 us
    ppermute x1, starting transfers between devices, local(): from_y_one = lax.ppermute(y_one, ('dom', 'yz'), once_y)  1.57 us
    pallas_call x1, Pallas kernels, local(): pl.pallas_call(early_kernel, out_shape=[staged[1], jax.ShapeDtypeStruct(w...  1.23 us
    pallas_call x1, Pallas kernels, local(): pl.pallas_call(functools.partial(edge_kernel, dims), out_shape=whole, in_...  0.91 us
  transfers between devices with their start and end apart: 9, of which 1 were waited for; matrix products, arithmetic and copies ran while one was open for 0% of the time, Pallas kernels for 22%

profile of v7, /device:TPU:0, one launch (start us, length us, event | category | flops | bytes accessed | tf_op | source)
XLA Modules:
  0.0 19.0 jit_solution(17331514550163471284)
XLA Ops:
  0.0 2.2 %pack_shell.1 = (bf16[2,32,128]{2,1,0:T(8,128)(2,1)}, bf16[2,32,128]{2,1,0:T(8,128)(2,1)}, bf16[2,32,128]{2,1,0:T(8,128)(2,1)}, bf16[2,32,128]{2,1,0:T(8,128)(2,...) custom-call(s32[1,4,8]{2,1,0:T(4,128)} %owner_hbm.1, s32[1,1,2,4]{3,2,1,0:T(2,128)} %source_hbm.1, ...), custom_call_target="tpu_custom_call" | custom-call | tf_op jit(solution)/shard_map/pack_shell/pallas_call | solution.py:496
  2.2 0.5 %collective-permute-start = (bf16[2,32,128]{2,1,0:T(8,128)(2,1)}, bf16[2,32,128]{2,1,0:T(8,128)(2,1)S(1)}, u32[]{:S(2)}, u32[]{:S(2)}) collective-permute-start(bf16[2,32,128]{2,1,0:T(8,128)(2,1)} %get-tuple-element.32), channel_id=1, source_target_pairs={{0,16},{1,17},{2,18},{3,19},{16,0},{17,1},{18,2},{19,3},{4,20},{5,... | collective-permute-start | bytes 49160 | tf_op jit(solution)/shard_map/ppermute | solution.py:524
  2.7 2.7 %collective-permute-start.1 = (bf16[2,32,128]{2,1,0:T(8,128)(2,1)}, bf16[2,32,128]{2,1,0:T(8,128)(2,1)S(1)}, u32[]{:S(2)}, u32[]{:S(2)}) collective-permute-start(bf16[2,32,128]{2,1,0:T(8,128)(2,1)} %get-tuple-element.33), channel_id=1, source_target_pairs={{0,17},{1,16},{2,19},{3,18},{17,0},{16,1},{19,2},{18,3},{4,21},{5,... | collective-permute-start | bytes 49160 | tf_op jit(solution)/shard_map/ppermute | solution.py:524
  5.3 1.2 %collective-permute-start.2 = (bf16[2,32,128]{2,1,0:T(8,128)(2,1)}, bf16[2,32,128]{2,1,0:T(8,128)(2,1)S(1)}, u32[]{:S(2)}, u32[]{:S(2)}) collective-permute-start(bf16[2,32,128]{2,1,0:T(8,128)(2,1)} %get-tuple-element.34), channel_id=1, source_target_pairs={{0,18},{1,19},{2,16},{3,17},{18,0},{19,1},{16,2},{17,3},{4,22},{5,... | collective-permute-start | bytes 49160 | tf_op jit(solution)/shard_map/ppermute | solution.py:524
  6.5 0.0 collective-permute-start.3
  6.6 1.2 %early_grid.1 = (f32[8,256,128]{2,1,0:T(8,128)S(1)}, f32[8,16,128]{2,1,0:T(8,128)}) custom-call(f32[64,256,128]{2,1,0:T(8,128)} %get-tuple-element.26.carried, f32[8,16,128]{2,1,0:T(8,128)} %get-tuple-element.27.wrap_in), custom_call_target="tpu_custom_call", output_to_operand_aliasing={{1}: (1, {})} | custom-call | tf_op jit(solution)/shard_map/early_grid/pallas_call | solution.py:533
  7.8 2.9 %collective-permute-start.8 = (f32[8,16,128]{2,1,0:T(8,128)}, f32[8,16,128]{2,1,0:T(8,128)S(1)}, u32[]{:S(2)}, u32[]{:S(2)}) collective-permute-start(f32[8,16,128]{2,1,0:T(8,128)} %get-tuple-element.46), channel_id=1, source_target_pairs={{0,12},{4,20},{8,24},{1,13},{5,21},{9,25},{2,14},{6,22},{10,26},{3... | collective-permute-start | bytes 196616 | tf_op jit(solution)/shard_map/ppermute | solution.py:543
  10.7 0.2 %stage_operands.1 = (bf16[8,512,512]{2,1,0:T(8,128)(2,1)S(1)}, f32[8,256,128]{2,1,0:T(8,128)S(1)}, f32[16,128]{1,0:T(8,128)S(1)}) custom-call(bf16[8,512,512]{2,1,0:T(8,128)(2,1)} %bitcast.7, f32[64,256,128]{2,1,0:T(8,128)} %get-tuple-element.26.carried, f32[8,256,128]{2,1,0:T(8,128)S(1)} %get-tuple-element.28.grid_in), custom_call_target="tpu_custom_call", output_to_operand_aliasing={{1}: (2, {})} | custom-call | bytes 8388608 | tf_op jit(solution)/shard_map/stage_operands/pallas_call | solution.py:544
  11.0 0.0 collective-permute-done.rest_0_
  11.0 0.0 collective-permute-done.1.rest_1_
  11.0 0.0 collective-permute-done.2.rest_2_
  11.0 0.0 collective-permute-done.3.rest_3_
  11.0 0.2 %fill_blocks.1 = (f32[2048,128]{1,0:T(8,128)S(1)}, f32[128,128]{1,0:T(8,128)S(1)}, f32[128,128]{1,0:T(8,128)S(1)}, f32[128,128]{1,0:T(8,128)S(1)}, f32[128,128]{1,0:T(8,128)S(1)}) custom-call(f32[16,128]{1,0:T(8,128)S(1)} %get-tuple-element.29.plan_vmem, bf16[8,512,512]{2,1,0:T(8,128)(2,1)S(1)} %get-tuple-element.30.weight_ref, ...), custom_call_target="tpu_custom_call", output_to_operand_aliasing={{0}: (2, {})} | custom-call | tf_op jit(solution)/shard_map/fill_blocks/pallas_call | solution.py:556
  11.2 1.6 %collective-permute-start.4 = (f32[128,128]{1,0:T(8,128)S(1)}, f32[128,128]{1,0:T(8,128)S(1)}, u32[]{:S(2)}, u32[]{:S(2)}) collective-permute-start(f32[128,128]{1,0:T(8,128)S(1)} %get-tuple-element.42.rest_0_), channel_id=1, source_target_pairs={{16,17},{17,18},{18,19},{19,3},{1,0},{2,1},{3,2},{0,16},{20,21},{2... | collective-permute-start | bytes 196616 | tf_op jit(solution)/shard_map/ppermute | solution.py:572
  12.8 0.5 %collective-permute-start.5 = (f32[128,128]{1,0:T(8,128)S(1)}, f32[128,128]{1,0:T(8,128)S(1)}, u32[]{:S(2)}, u32[]{:S(2)}) collective-permute-start(f32[128,128]{1,0:T(8,128)S(1)} %get-tuple-element.43.rest_1_), channel_id=1, source_target_pairs={{17,16},{18,17},{19,18},{3,19},{0,1},{1,2},{2,3},{16,0},{21,20},{2... | collective-permute-start | bytes 196616 | tf_op jit(solution)/shard_map/ppermute | solution.py:573
  13.3 0.0 collective-permute-start.6
  13.3 2.0 %collective-permute-start.7 = (f32[128,128]{1,0:T(8,128)S(1)}, f32[128,128]{1,0:T(8,128)S(1)}, u32[]{:S(2)}, u32[]{:S(2)}) collective-permute-start(f32[128,128]{1,0:T(8,128)S(1)} %get-tuple-element.45.rest_3_), channel_id=1, source_target_pairs={{20,16},{24,20},{28,24},{12,28},{0,4},{4,8},{8,12},{16,0},{21,17},... | collective-permute-start | bytes 196616 | tf_op jit(solution)/shard_map/ppermute | solution.py:575
  15.3 2.4 %inner_faces.1 = (f32[8,16,16,128]{3,2,1,0:T(8,128)}, f32[8,16,128]{2,1,0:T(8,128)S(1)}, f32[8,16,128]{2,1,0:T(8,128)S(1)}, f32[8,16,128]{2,1,0:T(8,128)S(1)}, f32[8,16,128]{2,1,0:T(8,128)S(1)}) custom-call(f32[2048,128]{1,0:T(8,128)S(1)} %get-tuple-element.36.filled), custom_call_target="tpu_custom_call" | custom-call | flops 78643200 | bytes 2097152 | tf_op jit(solution)/shard_map/inner_faces/pallas_call | solution.py:580
  17.8 0.0 collective-permute-done.8
  17.8 0.0 collective-permute-done.4.rest_4_
  17.8 0.0 collective-permute-done.5.rest_5_
  17.8 0.3 %collective-permute-done.6.rest_6_ = f32[128,128]{1,0:T(8,128)S(1)} collective-permute-done((f32[128,128]{1,0:T(8,128)S(1)}, f32[128,128]{1,0:T(8,128)S(1)}, u32[]{:S(2)}, u32[]{:S(2)}) %collective-permute-start.6) | collective-permute-done | bytes 65568 | tf_op jit(solution)/shard_map/ppermute | solution.py:574
  18.1 0.0 collective-permute-done.7.rest_7_
  18.1 0.9 %edge_faces.1 = f32[8,16,16,128]{3,2,1,0:T(8,128)} custom-call(f32[8,16,16,128]{3,2,1,0:T(8,128)} %get-tuple-element.37.part, f32[8,16,128]{2,1,0:T(8,128)S(1)} %get-tuple-element.38.rim_x_low, f32[8,16,128]{2,1,0:T(8,128)S(1)} %get-tuple-element.39.rim_x_high, f32[8,16,128]{2,1,0:T(8,128)S(1)} %get-tuple-element.40.rim_y_low, ...), custom_call_target="tpu_custom_call", output_to_operand_aliasing={{}: (0, {})} | custom-call | tf_op jit(solution)/shard_map/edge_faces/pallas_call | solution.py:596
Async XLA Ops:
  2.2 8.8 %collective-permute-start = (bf16[2,32,128]{2,1,0:T(8,128)(2,1)}, bf16[2,32,128]{2,1,0:T(8,128)(2,1)S(1)}, u32[]{:S(2)}, u32[]{:S(2)}) collective-permute-start(bf16[2,32,128]{2,1,0:T(8,128)(2,1)} %get-tuple-element.32), channel_id=1, source_target_pairs={{0,16},{1,17},{2,18},{3,19},{16,0},{17,1},{18,2},{19,3},{4,20},{5,... | collective-permute-start | bytes 49160 | tf_op jit(solution)/shard_map/ppermute | solution.py:524
  2.7 8.3 %collective-permute-start.1 = (bf16[2,32,128]{2,1,0:T(8,128)(2,1)}, bf16[2,32,128]{2,1,0:T(8,128)(2,1)S(1)}, u32[]{:S(2)}, u32[]{:S(2)}) collective-permute-start(bf16[2,32,128]{2,1,0:T(8,128)(2,1)} %get-tuple-element.33), channel_id=1, source_target_pairs={{0,17},{1,16},{2,19},{3,18},{17,0},{16,1},{19,2},{18,3},{4,21},{5,... | collective-permute-start | bytes 49160 | tf_op jit(solution)/shard_map/ppermute | solution.py:524
  5.3 5.7 %collective-permute-start.2 = (bf16[2,32,128]{2,1,0:T(8,128)(2,1)}, bf16[2,32,128]{2,1,0:T(8,128)(2,1)S(1)}, u32[]{:S(2)}, u32[]{:S(2)}) collective-permute-start(bf16[2,32,128]{2,1,0:T(8,128)(2,1)} %get-tuple-element.34), channel_id=1, source_target_pairs={{0,18},{1,19},{2,16},{3,17},{18,0},{19,1},{16,2},{17,3},{4,22},{5,... | collective-permute-start | bytes 49160 | tf_op jit(solution)/shard_map/ppermute | solution.py:524
  6.5 4.5 %collective-permute-start.3 = (bf16[2,32,128]{2,1,0:T(8,128)(2,1)}, bf16[2,32,128]{2,1,0:T(8,128)(2,1)S(1)}, u32[]{:S(2)}, u32[]{:S(2)}) collective-permute-start(bf16[2,32,128]{2,1,0:T(8,128)(2,1)} %get-tuple-element.35), channel_id=1, source_target_pairs={{0,19},{1,18},{2,17},{3,16},{19,0},{18,1},{17,2},{16,3},{4,23},{5,... | collective-permute-start | bytes 49160 | tf_op jit(solution)/shard_map/ppermute | solution.py:524
  7.8 10.0 %collective-permute-start.8 = (f32[8,16,128]{2,1,0:T(8,128)}, f32[8,16,128]{2,1,0:T(8,128)S(1)}, u32[]{:S(2)}, u32[]{:S(2)}) collective-permute-start(f32[8,16,128]{2,1,0:T(8,128)} %get-tuple-element.46), channel_id=1, source_target_pairs={{0,12},{4,20},{8,24},{1,13},{5,21},{9,25},{2,14},{6,22},{10,26},{3... | collective-permute-start | bytes 196616 | tf_op jit(solution)/shard_map/ppermute | solution.py:543
  11.2 6.6 %collective-permute-start.4 = (f32[128,128]{1,0:T(8,128)S(1)}, f32[128,128]{1,0:T(8,128)S(1)}, u32[]{:S(2)}, u32[]{:S(2)}) collective-permute-start(f32[128,128]{1,0:T(8,128)S(1)} %get-tuple-element.42.rest_0_), channel_id=1, source_target_pairs={{16,17},{17,18},{18,19},{19,3},{1,0},{2,1},{3,2},{0,16},{20,21},{2... | collective-permute-start | bytes 196616 | tf_op jit(solution)/shard_map/ppermute | solution.py:572
  12.8 5.0 %collective-permute-start.5 = (f32[128,128]{1,0:T(8,128)S(1)}, f32[128,128]{1,0:T(8,128)S(1)}, u32[]{:S(2)}, u32[]{:S(2)}) collective-permute-start(f32[128,128]{1,0:T(8,128)S(1)} %get-tuple-element.43.rest_1_), channel_id=1, source_target_pairs={{17,16},{18,17},{19,18},{3,19},{0,1},{1,2},{2,3},{16,0},{21,20},{2... | collective-permute-start | bytes 196616 | tf_op jit(solution)/shard_map/ppermute | solution.py:573
  13.3 4.8 %collective-permute-start.6 = (f32[128,128]{1,0:T(8,128)S(1)}, f32[128,128]{1,0:T(8,128)S(1)}, u32[]{:S(2)}, u32[]{:S(2)}) collective-permute-start(f32[128,128]{1,0:T(8,128)S(1)} %get-tuple-element.44.rest_2_), channel_id=1, source_target_pairs={{16,20},{20,24},{24,28},{28,12},{4,0},{8,4},{12,8},{0,16},{17,21},... | collective-permute-start | bytes 196616 | tf_op jit(solution)/shard_map/ppermute | solution.py:574
  13.3 4.8 %collective-permute-start.7 = (f32[128,128]{1,0:T(8,128)S(1)}, f32[128,128]{1,0:T(8,128)S(1)}, u32[]{:S(2)}, u32[]{:S(2)}) collective-permute-start(f32[128,128]{1,0:T(8,128)S(1)} %get-tuple-element.45.rest_3_), channel_id=1, source_target_pairs={{20,16},{24,20},{28,24},{12,28},{0,4},{4,8},{8,12},{16,0},{21,17},... | collective-permute-start | bytes 196616 | tf_op jit(solution)/shard_map/ppermute | solution.py:575

commit v8 on v6

--- a/solution.py
+++ b/solution.py
@@ -181,12 +181,10 @@
         copy.wait()
 
 
-def stage_kernel(weight_hbm, carried, grid_in, weight_ref, grid_ref, plan_ref, sems):
-    blocks, ncomp, plan_rows = weight_ref.shape[0], grid_ref.shape[0], plan_ref.shape[0]
-    grid_copy = pltpu.make_async_copy(carried.at[pl.ds(0, ncomp)], grid_ref, sems.at[blocks])
-    copies = [pltpu.make_async_copy(weight_hbm.at[i], weight_ref.at[i], sems.at[i]) for i in range(blocks)]
-    copies.append(pltpu.make_async_copy(carried.at[ncomp, pl.ds(0, plan_rows)], plan_ref, sems.at[blocks + 1]))
-    copies.append(grid_copy)
+def stage_kernel(carried, grid_ref, plan_ref, sems):
+    ncomp, plan_rows = grid_ref.shape[0], plan_ref.shape[0]
+    grid_copy = pltpu.make_async_copy(carried.at[pl.ds(0, ncomp)], grid_ref, sems.at[0])
+    copies = [pltpu.make_async_copy(carried.at[ncomp, pl.ds(0, plan_rows)], plan_ref, sems.at[1]), grid_copy]
 
     @pl.when(lax.axis_index("dom") == 1)
     def _():
@@ -201,7 +199,7 @@
         grid_copy.wait()
 
 
-def fill_kernel(dims, plan_vmem, weight_ref, grid_ref, *rest):
+def fill_kernel(dims, plan_vmem, weight_ref, grid_ref, early_ref, *rest):
     ncomp, len_x, len_y, len_z, n_yz, slots, depth = dims
     got = rest[:n_yz]
     filled, y_one, y_two, x_one, x_two, result, plan, sem = rest[n_yz:]
@@ -210,6 +208,15 @@
     plane = len_x * len_y
 
     helio = lax.axis_index("dom") == 1
+    ahead = early(1)
+
+    @pl.when(ahead)
+    def _():
+        filled[...] = early_ref[...]
+
+    @pl.when(jnp.logical_not(ahead))
+    def _():
+        filled[...] = grid_ref[...]
 
     @pl.when(helio)
     def _():
@@ -487,7 +494,7 @@
     face_x = jax.ShapeDtypeStruct((ncomp * len_y, len_z), jnp.float32)
     face_y = jax.ShapeDtypeStruct((ncomp * len_x, len_z), jnp.float32)
     plane = len_x * len_y
-    carried_planes = max(ncomp + 1, 8 * MIB // (4 * LANES * plane))
+    carried_planes = max(ncomp + 1, 16 * MIB // (4 * LANES * plane))
     *packed, carried, wrap = pl.pallas_call(
         functools.partial(pack_kernel, dims + (n_yz, shells, slots, depth)),
         out_shape=[jax.ShapeDtypeStruct((CAP, rows, LANES), jnp.bfloat16)] * n_yz
@@ -524,8 +531,8 @@
         jax.ShapeDtypeStruct((plan_rows, LANES), jnp.float32),
     ]
     staged_bytes = sum(x.size * x.dtype.itemsize for x in staged)
-    room = pltpu.CompilerParams(vmem_limit_bytes=VMEM_BYTES - 13 * staged_bytes // 4)
-    grid, wrap = pl.pallas_call(
+    room = pltpu.CompilerParams(vmem_limit_bytes=VMEM_BYTES - 17 * staged_bytes // 4)
+    early_grid, wrap = pl.pallas_call(
         early_kernel,
         out_shape=[staged[1], jax.ShapeDtypeStruct(wrap.shape, wrap.dtype)],
         in_specs=[HB] * 2,
@@ -536,22 +543,21 @@
         name="early_grid",
     )(carried, wrap)
     wrap = lax.ppermute(wrap, ("dom", "gx", "yz"), wrap_pairs(n_gx, n_yz))
-    weights, grid, plan = pl.pallas_call(
+    grid, plan = pl.pallas_call(
         stage_kernel,
-        out_shape=staged,
-        in_specs=[HB, HB, VM],
-        out_specs=[VM] * 3,
-        scratch_shapes=[pltpu.SemaphoreType.DMA((slots * depth + 2,))],
-        input_output_aliases={2: 1},
+        out_shape=staged[1:],
+        in_specs=[HB] * 1,
+        out_specs=[VM] * 2,
+        scratch_shapes=[pltpu.SemaphoreType.DMA((2,))],
         compiler_params=room,
         cost_estimate=pl.CostEstimate(flops=0, bytes_accessed=4 * interp_weights.size, transcendentals=0),
         name="stage_operands",
-    )(weights, carried, grid)
+    )(carried)
 
     filled, y_one, y_two, x_one, x_two = pl.pallas_call(
         functools.partial(fill_kernel, dims + (n_yz, slots, depth)),
         out_shape=[jax.ShapeDtypeStruct((cell_rows, len_z), jnp.float32), face_y, face_y, face_x, face_x],
-        in_specs=[VM, VM, VM] + [VM] * n_yz,
+        in_specs=[VM] * (4 + n_yz),
         out_specs=[VM] * 5,
         scratch_shapes=[
             pltpu.VMEM((2 * BLK * (slots * rows + BLK), LANES), jnp.float32),
@@ -561,7 +567,7 @@
         input_output_aliases={2: 0},
         compiler_params=pltpu.CompilerParams(vmem_limit_bytes=16 * MIB),
         name="fill_blocks",
-    )(plan, weights, grid.reshape(cell_rows, len_z), *moved)
+    )(plan, weights, grid.reshape(cell_rows, len_z), early_grid.reshape(cell_rows, len_z), *moved)
 
     once_x, once_y = cycle(n_gx), cycle(n_yz)
     from_y_one = lax.ppermute(y_one, ("dom", "yz"), once_y)

time: 18.9 us -> 18.7 us (0.989)
  no operation moved by 1% of the time
where the time goes in v8:
time: 18.7 us; the launch traced here: 18.6 us
  starting transfers between devices  11.3 us (60%)
  Pallas kernels  7.07 us (38%)
    ppermute x4, starting transfers between devices, local(): moved.append(lax.ppermute(packed[step], ('dom', 'yz'), pairs))  4.36 us
    ppermute x1, starting transfers between devices, local(): wrap = lax.ppermute(wrap, ('dom', 'gx', 'yz'), wrap_pairs(n_gx, n_yz))  2.79 us
    pallas_call x1, Pallas kernels, local(): pl.pallas_call(functools.partial(inner_kernel, dims), out_shape=[whole, r...  2.43 us
    pallas_call x1, Pallas kernels, local(): pl.pallas_call(functools.partial(pack_kernel, dims + (n_yz, shells, slots...  2.19 us
    ppermute x1, starting transfers between devices, local(): from_y_one = lax.ppermute(y_one, ('dom', 'yz'), once_y)  1.86 us
    ppermute x1, starting transfers between devices, local(): from_x_two = lax.ppermute(x_two, ('dom', 'gx'), [(b, a) for a, b in once_x])  1.74 us
    pallas_call x1, Pallas kernels, local(): pl.pallas_call(early_kernel, out_shape=[staged[1], jax.ShapeDtypeStruct(w...  1.38 us
    pallas_call x1, Pallas kernels, local(): pl.pallas_call(functools.partial(edge_kernel, dims), out_shape=whole, in_...  0.91 us
  transfers between devices with their start and end apart: 9, of which 1 were waited for; matrix products, arithmetic and copies ran while one was open for 0% of the time, Pallas kernels for 21%

profile of v8, /device:TPU:0, one launch (start us, length us, event | category | flops | bytes accessed | tf_op | source)
XLA Modules:
  0.0 18.6 jit_solution(11098929259266796533)
XLA Ops:
  0.0 2.2 %pack_shell.1 = (bf16[2,32,128]{2,1,0:T(8,128)(2,1)}, bf16[2,32,128]{2,1,0:T(8,128)(2,1)}, bf16[2,32,128]{2,1,0:T(8,128)(2,1)}, bf16[2,32,128]{2,1,0:T(8,128)(2,...) custom-call(s32[1,4,8]{2,1,0:T(4,128)} %owner_hbm.1, s32[1,1,2,4]{3,2,1,0:T(2,128)} %source_hbm.1, ...), custom_call_target="tpu_custom_call" | custom-call | tf_op jit(solution)/shard_map/pack_shell/pallas_call | solution.py:498
  2.2 0.5 %collective-permute-start = (bf16[2,32,128]{2,1,0:T(8,128)(2,1)}, bf16[2,32,128]{2,1,0:T(8,128)(2,1)S(1)}, u32[]{:S(2)}, u32[]{:S(2)}) collective-permute-start(bf16[2,32,128]{2,1,0:T(8,128)(2,1)} %get-tuple-element.30), channel_id=1, source_target_pairs={{0,16},{1,17},{2,18},{3,19},{16,0},{17,1},{18,2},{19,3},{4,20},{5,... | collective-permute-start | bytes 49160 | tf_op jit(solution)/shard_map/ppermute | solution.py:526
  2.7 2.7 %collective-permute-start.1 = (bf16[2,32,128]{2,1,0:T(8,128)(2,1)}, bf16[2,32,128]{2,1,0:T(8,128)(2,1)S(1)}, u32[]{:S(2)}, u32[]{:S(2)}) collective-permute-start(bf16[2,32,128]{2,1,0:T(8,128)(2,1)} %get-tuple-element.31), channel_id=1, source_target_pairs={{0,17},{1,16},{2,19},{3,18},{17,0},{16,1},{19,2},{18,3},{4,21},{5,... | collective-permute-start | bytes 49160 | tf_op jit(solution)/shard_map/ppermute | solution.py:526
  5.3 1.2 %collective-permute-start.2 = (bf16[2,32,128]{2,1,0:T(8,128)(2,1)}, bf16[2,32,128]{2,1,0:T(8,128)(2,1)S(1)}, u32[]{:S(2)}, u32[]{:S(2)}) collective-permute-start(bf16[2,32,128]{2,1,0:T(8,128)(2,1)} %get-tuple-element.32), channel_id=1, source_target_pairs={{0,18},{1,19},{2,16},{3,17},{18,0},{19,1},{16,2},{17,3},{4,22},{5,... | collective-permute-start | bytes 49160 | tf_op jit(solution)/shard_map/ppermute | solution.py:526
  6.5 0.0 collective-permute-start.3
  6.6 0.0 copy-start
  6.6 1.4 %early_grid.1 = (f32[8,256,128]{2,1,0:T(8,128)S(1)}, f32[8,16,128]{2,1,0:T(8,128)}) custom-call(f32[128,256,128]{2,1,0:T(8,128)} %get-tuple-element.25.carried, f32[8,16,128]{2,1,0:T(8,128)} %get-tuple-element.28.wrap_in), custom_call_target="tpu_custom_call", output_to_operand_aliasing={{1}: (1, {})} | custom-call | tf_op jit(solution)/shard_map/early_grid/pallas_call | solution.py:535
  7.9 2.8 %collective-permute-start.8 = (f32[8,16,128]{2,1,0:T(8,128)}, f32[8,16,128]{2,1,0:T(8,128)S(1)}, u32[]{:S(2)}, u32[]{:S(2)}) collective-permute-start(f32[8,16,128]{2,1,0:T(8,128)} %get-tuple-element.44), channel_id=1, source_target_pairs={{0,12},{4,20},{8,24},{1,13},{5,21},{9,25},{2,14},{6,22},{10,26},{3... | collective-permute-start | bytes 196616 | tf_op jit(solution)/shard_map/ppermute | solution.py:545
  10.8 0.0 collective-permute-done.rest_0_
  10.8 0.0 collective-permute-done.1.rest_1_
  10.8 0.0 collective-permute-done.2.rest_2_
  10.8 0.0 collective-permute-done.3.rest_3_
  10.8 0.0 copy-done
  10.8 0.1 fill_blocks.1
  11.0 1.9 %collective-permute-start.4 = (f32[128,128]{1,0:T(8,128)S(1)}, f32[128,128]{1,0:T(8,128)S(1)}, u32[]{:S(2)}, u32[]{:S(2)}) collective-permute-start(f32[128,128]{1,0:T(8,128)S(1)} %get-tuple-element.40.rest_0_), channel_id=1, source_target_pairs={{16,17},{17,18},{18,19},{19,3},{1,0},{2,1},{3,2},{0,16},{20,21},{2... | collective-permute-start | bytes 196616 | tf_op jit(solution)/shard_map/ppermute | solution.py:573
  12.8 0.2 %collective-permute-start.5 = (f32[128,128]{1,0:T(8,128)S(1)}, f32[128,128]{1,0:T(8,128)S(1)}, u32[]{:S(2)}, u32[]{:S(2)}) collective-permute-start(f32[128,128]{1,0:T(8,128)S(1)} %get-tuple-element.41.rest_1_), channel_id=1, source_target_pairs={{17,16},{18,17},{19,18},{3,19},{0,1},{1,2},{2,3},{16,0},{21,20},{2... | collective-permute-start | bytes 196616 | tf_op jit(solution)/shard_map/ppermute | solution.py:574
  13.1 0.3 %collective-permute-start.6 = (f32[128,128]{1,0:T(8,128)S(1)}, f32[128,128]{1,0:T(8,128)S(1)}, u32[]{:S(2)}, u32[]{:S(2)}) collective-permute-start(f32[128,128]{1,0:T(8,128)S(1)} %get-tuple-element.42.rest_2_), channel_id=1, source_target_pairs={{16,20},{20,24},{24,28},{28,12},{4,0},{8,4},{12,8},{0,16},{17,21},... | collective-permute-start | bytes 196616 | tf_op jit(solution)/shard_map/ppermute | solution.py:575
  13.3 1.7 %collective-permute-start.7 = (f32[128,128]{1,0:T(8,128)S(1)}, f32[128,128]{1,0:T(8,128)S(1)}, u32[]{:S(2)}, u32[]{:S(2)}) collective-permute-start(f32[128,128]{1,0:T(8,128)S(1)} %get-tuple-element.43.rest_3_), channel_id=1, source_target_pairs={{20,16},{24,20},{28,24},{12,28},{0,4},{4,8},{8,12},{16,0},{21,17},... | collective-permute-start | bytes 196616 | tf_op jit(solution)/shard_map/ppermute | solution.py:576
  15.1 2.4 %inner_faces.1 = (f32[8,16,16,128]{3,2,1,0:T(8,128)}, f32[8,16,128]{2,1,0:T(8,128)S(1)}, f32[8,16,128]{2,1,0:T(8,128)S(1)}, f32[8,16,128]{2,1,0:T(8,128)S(1)}, f32[8,16,128]{2,1,0:T(8,128)S(1)}) custom-call(f32[2048,128]{1,0:T(8,128)S(1)} %get-tuple-element.34.filled), custom_call_target="tpu_custom_call" | custom-call | flops 78643200 | bytes 2097152 | tf_op jit(solution)/shard_map/inner_faces/pallas_call | solution.py:581
  17.5 0.0 collective-permute-done.8
  17.5 0.0 collective-permute-done.4.rest_4_
  17.5 0.0 collective-permute-done.5.rest_5_
  17.5 0.1 collective-permute-done.6.rest_6_
  17.7 0.0 collective-permute-done.7.rest_7_
  17.7 0.9 %edge_faces.1 = f32[8,16,16,128]{3,2,1,0:T(8,128)} custom-call(f32[8,16,16,128]{3,2,1,0:T(8,128)} %get-tuple-element.35.part, f32[8,16,128]{2,1,0:T(8,128)S(1)} %get-tuple-element.36.rim_x_low, f32[8,16,128]{2,1,0:T(8,128)S(1)} %get-tuple-element.37.rim_x_high, f32[8,16,128]{2,1,0:T(8,128)S(1)} %get-tuple-element.38.rim_y_low, ...), custom_call_target="tpu_custom_call", output_to_operand_aliasing={{}: (0, {})} | custom-call | tf_op jit(solution)/shard_map/edge_faces/pallas_call | solution.py:597
  (1 shorter events, 0.0 us)
Async XLA Ops:
  2.2 8.6 %collective-permute-start = (bf16[2,32,128]{2,1,0:T(8,128)(2,1)}, bf16[2,32,128]{2,1,0:T(8,128)(2,1)S(1)}, u32[]{:S(2)}, u32[]{:S(2)}) collective-permute-start(bf16[2,32,128]{2,1,0:T(8,128)(2,1)} %get-tuple-element.30), channel_id=1, source_target_pairs={{0,16},{1,17},{2,18},{3,19},{16,0},{17,1},{18,2},{19,3},{4,20},{5,... | collective-permute-start | bytes 49160 | tf_op jit(solution)/shard_map/ppermute | solution.py:526
  2.7 8.1 %collective-permute-start.1 = (bf16[2,32,128]{2,1,0:T(8,128)(2,1)}, bf16[2,32,128]{2,1,0:T(8,128)(2,1)S(1)}, u32[]{:S(2)}, u32[]{:S(2)}) collective-permute-start(bf16[2,32,128]{2,1,0:T(8,128)(2,1)} %get-tuple-element.31), channel_id=1, source_target_pairs={{0,17},{1,16},{2,19},{3,18},{17,0},{16,1},{19,2},{18,3},{4,21},{5,... | collective-permute-start | bytes 49160 | tf_op jit(solution)/shard_map/ppermute | solution.py:526
  5.3 5.5 %collective-permute-start.2 = (bf16[2,32,128]{2,1,0:T(8,128)(2,1)}, bf16[2,32,128]{2,1,0:T(8,128)(2,1)S(1)}, u32[]{:S(2)}, u32[]{:S(2)}) collective-permute-start(bf16[2,32,128]{2,1,0:T(8,128)(2,1)} %get-tuple-element.32), channel_id=1, source_target_pairs={{0,18},{1,19},{2,16},{3,17},{18,0},{19,1},{16,2},{17,3},{4,22},{5,... | collective-permute-start | bytes 49160 | tf_op jit(solution)/shard_map/ppermute | solution.py:526
  6.5 4.3 %collective-permute-start.3 = (bf16[2,32,128]{2,1,0:T(8,128)(2,1)}, bf16[2,32,128]{2,1,0:T(8,128)(2,1)S(1)}, u32[]{:S(2)}, u32[]{:S(2)}) collective-permute-start(bf16[2,32,128]{2,1,0:T(8,128)(2,1)} %get-tuple-element.33), channel_id=1, source_target_pairs={{0,19},{1,18},{2,17},{3,16},{19,0},{18,1},{17,2},{16,3},{4,23},{5,... | collective-permute-start | bytes 49160 | tf_op jit(solution)/shard_map/ppermute | solution.py:526
  6.6 4.2 %copy-start = (bf16[1,1,2,4,512,512]{5,4,3,2,1,0:T(8,128)(2,1)S(1)}, bf16[1,1,2,4,512,512]{5,4,3,2,1,0:T(8,128)(2,1)}, u32[]{:S(2)}) copy-start(bf16[1,1,2,4,512,512]{5,4,3,2,1,0:T(8,128)(2,1)} %param.9) | copy-start | bytes 12582916
  7.9 9.6 %collective-permute-start.8 = (f32[8,16,128]{2,1,0:T(8,128)}, f32[8,16,128]{2,1,0:T(8,128)S(1)}, u32[]{:S(2)}, u32[]{:S(2)}) collective-permute-start(f32[8,16,128]{2,1,0:T(8,128)} %get-tuple-element.44), channel_id=1, source_target_pairs={{0,12},{4,20},{8,24},{1,13},{5,21},{9,25},{2,14},{6,22},{10,26},{3... | collective-permute-start | bytes 196616 | tf_op jit(solution)/shard_map/ppermute | solution.py:545
  11.0 6.6 %collective-permute-start.4 = (f32[128,128]{1,0:T(8,128)S(1)}, f32[128,128]{1,0:T(8,128)S(1)}, u32[]{:S(2)}, u32[]{:S(2)}) collective-permute-start(f32[128,128]{1,0:T(8,128)S(1)} %get-tuple-element.40.rest_0_), channel_id=1, source_target_pairs={{16,17},{17,18},{18,19},{19,3},{1,0},{2,1},{3,2},{0,16},{20,21},{2... | collective-permute-start | bytes 196616 | tf_op jit(solution)/shard_map/ppermute | solution.py:573
  12.8 4.7 %collective-permute-start.5 = (f32[128,128]{1,0:T(8,128)S(1)}, f32[128,128]{1,0:T(8,128)S(1)}, u32[]{:S(2)}, u32[]{:S(2)}) collective-permute-start(f32[128,128]{1,0:T(8,128)S(1)} %get-tuple-element.41.rest_1_), channel_id=1, source_target_pairs={{17,16},{18,17},{19,18},{3,19},{0,1},{1,2},{2,3},{16,0},{21,20},{2... | collective-permute-start | bytes 196616 | tf_op jit(solution)/shard_map/ppermute | solution.py:574
  13.1 4.6 %collective-permute-start.6 = (f32[128,128]{1,0:T(8,128)S(1)}, f32[128,128]{1,0:T(8,128)S(1)}, u32[]{:S(2)}, u32[]{:S(2)}) collective-permute-start(f32[128,128]{1,0:T(8,128)S(1)} %get-tuple-element.42.rest_2_), channel_id=1, source_target_pairs={{16,20},{20,24},{24,28},{28,12},{4,0},{8,4},{12,8},{0,16},{17,21},... | collective-permute-start | bytes 196616 | tf_op jit(solution)/shard_map/ppermute | solution.py:575
  13.3 4.3 %collective-permute-start.7 = (f32[128,128]{1,0:T(8,128)S(1)}, f32[128,128]{1,0:T(8,128)S(1)}, u32[]{:S(2)}, u32[]{:S(2)}) collective-permute-start(f32[128,128]{1,0:T(8,128)S(1)} %get-tuple-element.43.rest_3_), channel_id=1, source_target_pairs={{20,16},{24,20},{28,24},{12,28},{0,4},{4,8},{8,12},{16,0},{21,17},... | collective-permute-start | bytes 196616 | tf_op jit(solution)/shard_map/ppermute | solution.py:576

commit v9 on v8

--- a/solution.py
+++ b/solution.py
@@ -201,7 +201,7 @@
 
 def fill_kernel(dims, plan_vmem, weight_ref, grid_ref, early_ref, *rest):
     ncomp, len_x, len_y, len_z, n_yz, slots, depth = dims
-    got = rest[:n_yz]
+    got = rest[:n_yz][::-1]
     filled, y_one, y_two, x_one, x_two, result, plan, sem = rest[n_yz:]
     half = BLK // 2
     rows = half * ncomp
@@ -567,7 +567,7 @@
         input_output_aliases={2: 0},
         compiler_params=pltpu.CompilerParams(vmem_limit_bytes=16 * MIB),
         name="fill_blocks",
-    )(plan, weights, grid.reshape(cell_rows, len_z), early_grid.reshape(cell_rows, len_z), *moved)
+    )(plan, weights, grid.reshape(cell_rows, len_z), early_grid.reshape(cell_rows, len_z), *moved[::-1])
 
     once_x, once_y = cycle(n_gx), cycle(n_yz)
     from_y_one = lax.ppermute(y_one, ("dom", "yz"), once_y)

time: 18.7 us -> 18.6 us (level)
    ppermute x1, starting transfers between devices: 1.86 us -> 0.44 us  [local(): from_y_one = lax.ppermute(y_one, ('dom', 'yz'), once_y)]
    ppermute x1, starting transfers between devices: 0.22 us -> 1.64 us  [local(): from_y_two = lax.ppermute(y_two, ('dom', 'yz'), [(b, a) for a, b in once_y])]
    ppermute x1, starting transfers between devices: 0.29 us -> 0.01 us  [local(): from_x_one = lax.ppermute(x_one, ('dom', 'gx'), once_x)]
    ppermute x1, starting transfers between devices: 1.74 us -> 2.02 us  [local(): from_x_two = lax.ppermute(x_two, ('dom', 'gx'), [(b, a) for a, b in once_x])]
  transfers between devices with their start and end apart: 9 -> 9, of which waited for: 1 -> 0; matrix products, arithmetic and copies ran while one was open for 0% -> 0% of each run, Pallas kernels for 21% -> 22%
where the time goes in v9:
time: 18.6 us; the launch traced here: 18.5 us
  starting transfers between devices  11.2 us (60%)
  Pallas kernels  7.1 us (38%)
    ppermute x4, starting transfers between devices, local(): moved.append(lax.ppermute(packed[step], ('dom', 'yz'), pairs))  4.32 us
    ppermute x1, starting transfers between devices, local(): wrap = lax.ppermute(wrap, ('dom', 'gx', 'yz'), wrap_pairs(n_gx, n_yz))  2.81 us
    pallas_call x1, Pallas kernels, local(): pl.pallas_call(functools.partial(inner_kernel, dims), out_shape=[whole, r...  2.43 us
    pallas_call x1, Pallas kernels, local(): pl.pallas_call(functools.partial(pack_kernel, dims + (n_yz, shells, slots...  2.19 us
    ppermute x1, starting transfers between devices, local(): from_x_two = lax.ppermute(x_two, ('dom', 'gx'), [(b, a) for a, b in once_x])  2.02 us
    ppermute x1, starting transfers between devices, local(): from_y_two = lax.ppermute(y_two, ('dom', 'yz'), [(b, a) for a, b in once_y])  1.64 us
    pallas_call x1, Pallas kernels, local(): pl.pallas_call(early_kernel, out_shape=[staged[1], jax.ShapeDtypeStruct(w...  1.38 us
    pallas_call x1, Pallas kernels, local(): pl.pallas_call(functools.partial(edge_kernel, dims), out_shape=whole, in_...  0.93 us
  transfers between devices with their start and end apart: 9, of which 0 were waited for; matrix products, arithmetic and copies ran while one was open for 0% of the time, Pallas kernels for 22%

profile of v9, /device:TPU:0, one launch (start us, length us, event | category | flops | bytes accessed | tf_op | source)
XLA Modules:
  0.0 18.5 jit_solution(674020379269116714)
XLA Ops:
  0.0 2.2 %pack_shell.1 = (bf16[2,32,128]{2,1,0:T(8,128)(2,1)}, bf16[2,32,128]{2,1,0:T(8,128)(2,1)}, bf16[2,32,128]{2,1,0:T(8,128)(2,1)}, bf16[2,32,128]{2,1,0:T(8,128)(2,...) custom-call(s32[1,4,8]{2,1,0:T(4,128)} %owner_hbm.1, s32[1,1,2,4]{3,2,1,0:T(2,128)} %source_hbm.1, ...), custom_call_target="tpu_custom_call" | custom-call | tf_op jit(solution)/shard_map/pack_shell/pallas_call | solution.py:498
  2.2 3.4 %collective-permute-start = (bf16[2,32,128]{2,1,0:T(8,128)(2,1)}, bf16[2,32,128]{2,1,0:T(8,128)(2,1)S(1)}, u32[]{:S(2)}, u32[]{:S(2)}) collective-permute-start(bf16[2,32,128]{2,1,0:T(8,128)(2,1)} %get-tuple-element.30), channel_id=1, source_target_pairs={{0,19},{1,18},{2,17},{3,16},{19,0},{18,1},{17,2},{16,3},{4,23},{5,... | collective-permute-start | bytes 49160 | tf_op jit(solution)/shard_map/ppermute | solution.py:526
  5.6 0.8 %collective-permute-start.1 = (bf16[2,32,128]{2,1,0:T(8,128)(2,1)}, bf16[2,32,128]{2,1,0:T(8,128)(2,1)S(1)}, u32[]{:S(2)}, u32[]{:S(2)}) collective-permute-start(bf16[2,32,128]{2,1,0:T(8,128)(2,1)} %get-tuple-element.31), channel_id=1, source_target_pairs={{0,18},{1,19},{2,16},{3,17},{18,0},{19,1},{16,2},{17,3},{4,22},{5,... | collective-permute-start | bytes 49160 | tf_op jit(solution)/shard_map/ppermute | solution.py:526
  6.4 0.1 collective-permute-start.2
  6.5 0.0 collective-permute-start.3
  6.5 0.0 copy-start
  6.5 1.4 %early_grid.1 = (f32[8,256,128]{2,1,0:T(8,128)S(1)}, f32[8,16,128]{2,1,0:T(8,128)}) custom-call(f32[128,256,128]{2,1,0:T(8,128)} %get-tuple-element.25.carried, f32[8,16,128]{2,1,0:T(8,128)} %get-tuple-element.28.wrap_in), custom_call_target="tpu_custom_call", output_to_operand_aliasing={{1}: (1, {})} | custom-call | tf_op jit(solution)/shard_map/early_grid/pallas_call | solution.py:535
  7.9 2.8 %collective-permute-start.8 = (f32[8,16,128]{2,1,0:T(8,128)}, f32[8,16,128]{2,1,0:T(8,128)S(1)}, u32[]{:S(2)}, u32[]{:S(2)}) collective-permute-start(f32[8,16,128]{2,1,0:T(8,128)} %get-tuple-element.44), channel_id=1, source_target_pairs={{0,12},{4,20},{8,24},{1,13},{5,21},{9,25},{2,14},{6,22},{10,26},{3... | collective-permute-start | bytes 196616 | tf_op jit(solution)/shard_map/ppermute | solution.py:545
  10.7 0.0 collective-permute-done.rest_0_
  10.8 0.0 collective-permute-done.1.rest_1_
  10.8 0.0 collective-permute-done.2.rest_2_
  10.8 0.0 collective-permute-done.3.rest_3_
  10.8 0.0 copy-done
  10.8 0.1 fill_blocks.1
  11.0 0.4 %collective-permute-start.4 = (f32[128,128]{1,0:T(8,128)S(1)}, f32[128,128]{1,0:T(8,128)S(1)}, u32[]{:S(2)}, u32[]{:S(2)}) collective-permute-start(f32[128,128]{1,0:T(8,128)S(1)} %get-tuple-element.40.rest_0_), channel_id=1, source_target_pairs={{16,17},{17,18},{18,19},{19,3},{1,0},{2,1},{3,2},{0,16},{20,21},{2... | collective-permute-start | bytes 196616 | tf_op jit(solution)/shard_map/ppermute | solution.py:573
  11.4 1.6 %collective-permute-start.5 = (f32[128,128]{1,0:T(8,128)S(1)}, f32[128,128]{1,0:T(8,128)S(1)}, u32[]{:S(2)}, u32[]{:S(2)}) collective-permute-start(f32[128,128]{1,0:T(8,128)S(1)} %get-tuple-element.41.rest_1_), channel_id=1, source_target_pairs={{17,16},{18,17},{19,18},{3,19},{0,1},{1,2},{2,3},{16,0},{21,20},{2... | collective-permute-start | bytes 196616 | tf_op jit(solution)/shard_map/ppermute | solution.py:574
  13.0 0.0 collective-permute-start.6
  13.0 2.0 %collective-permute-start.7 = (f32[128,128]{1,0:T(8,128)S(1)}, f32[128,128]{1,0:T(8,128)S(1)}, u32[]{:S(2)}, u32[]{:S(2)}) collective-permute-start(f32[128,128]{1,0:T(8,128)S(1)} %get-tuple-element.43.rest_3_), channel_id=1, source_target_pairs={{20,16},{24,20},{28,24},{12,28},{0,4},{4,8},{8,12},{16,0},{21,17},... | collective-permute-start | bytes 196616 | tf_op jit(solution)/shard_map/ppermute | solution.py:576
  15.1 2.4 %inner_faces.1 = (f32[8,16,16,128]{3,2,1,0:T(8,128)}, f32[8,16,128]{2,1,0:T(8,128)S(1)}, f32[8,16,128]{2,1,0:T(8,128)S(1)}, f32[8,16,128]{2,1,0:T(8,128)S(1)}, f32[8,16,128]{2,1,0:T(8,128)S(1)}) custom-call(f32[2048,128]{1,0:T(8,128)S(1)} %get-tuple-element.34.filled), custom_call_target="tpu_custom_call" | custom-call | flops 78643200 | bytes 2097152 | tf_op jit(solution)/shard_map/inner_faces/pallas_call | solution.py:581
  17.5 0.0 collective-permute-done.8
  17.5 0.0 collective-permute-done.4.rest_4_
  17.5 0.0 collective-permute-done.5.rest_5_
  17.5 0.0 collective-permute-done.6.rest_6_
  17.5 0.0 collective-permute-done.7.rest_7_
  17.6 0.9 %edge_faces.1 = f32[8,16,16,128]{3,2,1,0:T(8,128)} custom-call(f32[8,16,16,128]{3,2,1,0:T(8,128)} %get-tuple-element.35.part, f32[8,16,128]{2,1,0:T(8,128)S(1)} %get-tuple-element.36.rim_x_low, f32[8,16,128]{2,1,0:T(8,128)S(1)} %get-tuple-element.37.rim_x_high, f32[8,16,128]{2,1,0:T(8,128)S(1)} %get-tuple-element.38.rim_y_low, ...), custom_call_target="tpu_custom_call", output_to_operand_aliasing={{}: (0, {})} | custom-call | tf_op jit(solution)/shard_map/edge_faces/pallas_call | solution.py:597
  (1 shorter events, 0.0 us)
Async XLA Ops:
  2.2 8.6 %collective-permute-start = (bf16[2,32,128]{2,1,0:T(8,128)(2,1)}, bf16[2,32,128]{2,1,0:T(8,128)(2,1)S(1)}, u32[]{:S(2)}, u32[]{:S(2)}) collective-permute-start(bf16[2,32,128]{2,1,0:T(8,128)(2,1)} %get-tuple-element.30), channel_id=1, source_target_pairs={{0,19},{1,18},{2,17},{3,16},{19,0},{18,1},{17,2},{16,3},{4,23},{5,... | collective-permute-start | bytes 49160 | tf_op jit(solution)/shard_map/ppermute | solution.py:526
  5.6 5.2 %collective-permute-start.1 = (bf16[2,32,128]{2,1,0:T(8,128)(2,1)}, bf16[2,32,128]{2,1,0:T(8,128)(2,1)S(1)}, u32[]{:S(2)}, u32[]{:S(2)}) collective-permute-start(bf16[2,32,128]{2,1,0:T(8,128)(2,1)} %get-tuple-element.31), channel_id=1, source_target_pairs={{0,18},{1,19},{2,16},{3,17},{18,0},{19,1},{16,2},{17,3},{4,22},{5,... | collective-permute-start | bytes 49160 | tf_op jit(solution)/shard_map/ppermute | solution.py:526
  6.4 4.4 %collective-permute-start.2 = (bf16[2,32,128]{2,1,0:T(8,128)(2,1)}, bf16[2,32,128]{2,1,0:T(8,128)(2,1)S(1)}, u32[]{:S(2)}, u32[]{:S(2)}) collective-permute-start(bf16[2,32,128]{2,1,0:T(8,128)(2,1)} %get-tuple-element.32), channel_id=1, source_target_pairs={{0,17},{1,16},{2,19},{3,18},{17,0},{16,1},{19,2},{18,3},{4,21},{5,... | collective-permute-start | bytes 49160 | tf_op jit(solution)/shard_map/ppermute | solution.py:526
  6.5 4.3 %collective-permute-start.3 = (bf16[2,32,128]{2,1,0:T(8,128)(2,1)}, bf16[2,32,128]{2,1,0:T(8,128)(2,1)S(1)}, u32[]{:S(2)}, u32[]{:S(2)}) collective-permute-start(bf16[2,32,128]{2,1,0:T(8,128)(2,1)} %get-tuple-element.33), channel_id=1, source_target_pairs={{0,16},{1,17},{2,18},{3,19},{16,0},{17,1},{18,2},{19,3},{4,20},{5,... | collective-permute-start | bytes 49160 | tf_op jit(solution)/shard_map/ppermute | solution.py:526
  6.5 4.3 %copy-start = (bf16[1,1,2,4,512,512]{5,4,3,2,1,0:T(8,128)(2,1)S(1)}, bf16[1,1,2,4,512,512]{5,4,3,2,1,0:T(8,128)(2,1)}, u32[]{:S(2)}) copy-start(bf16[1,1,2,4,512,512]{5,4,3,2,1,0:T(8,128)(2,1)} %param.9) | copy-start | bytes 12582916
  7.9 9.6 %collective-permute-start.8 = (f32[8,16,128]{2,1,0:T(8,128)}, f32[8,16,128]{2,1,0:T(8,128)S(1)}, u32[]{:S(2)}, u32[]{:S(2)}) collective-permute-start(f32[8,16,128]{2,1,0:T(8,128)} %get-tuple-element.44), channel_id=1, source_target_pairs={{0,12},{4,20},{8,24},{1,13},{5,21},{9,25},{2,14},{6,22},{10,26},{3... | collective-permute-start | bytes 196616 | tf_op jit(solution)/shard_map/ppermute | solution.py:545
  11.0 6.6 %collective-permute-start.4 = (f32[128,128]{1,0:T(8,128)S(1)}, f32[128,128]{1,0:T(8,128)S(1)}, u32[]{:S(2)}, u32[]{:S(2)}) collective-permute-start(f32[128,128]{1,0:T(8,128)S(1)} %get-tuple-element.40.rest_0_), channel_id=1, source_target_pairs={{16,17},{17,18},{18,19},{19,3},{1,0},{2,1},{3,2},{0,16},{20,21},{2... | collective-permute-start | bytes 196616 | tf_op jit(solution)/shard_map/ppermute | solution.py:573
  11.4 6.1 %collective-permute-start.5 = (f32[128,128]{1,0:T(8,128)S(1)}, f32[128,128]{1,0:T(8,128)S(1)}, u32[]{:S(2)}, u32[]{:S(2)}) collective-permute-start(f32[128,128]{1,0:T(8,128)S(1)} %get-tuple-element.41.rest_1_), channel_id=1, source_target_pairs={{17,16},{18,17},{19,18},{3,19},{0,1},{1,2},{2,3},{16,0},{21,20},{2... | collective-permute-start | bytes 196616 | tf_op jit(solution)/shard_map/ppermute | solution.py:574
  13.0 4.5 %collective-permute-start.6 = (f32[128,128]{1,0:T(8,128)S(1)}, f32[128,128]{1,0:T(8,128)S(1)}, u32[]{:S(2)}, u32[]{:S(2)}) collective-permute-start(f32[128,128]{1,0:T(8,128)S(1)} %get-tuple-element.42.rest_2_), channel_id=1, source_target_pairs={{16,20},{20,24},{24,28},{28,12},{4,0},{8,4},{12,8},{0,16},{17,21},... | collective-permute-start | bytes 196616 | tf_op jit(solution)/shard_map/ppermute | solution.py:575
  13.0 4.5 %collective-permute-start.7 = (f32[128,128]{1,0:T(8,128)S(1)}, f32[128,128]{1,0:T(8,128)S(1)}, u32[]{:S(2)}, u32[]{:S(2)}) collective-permute-start(f32[128,128]{1,0:T(8,128)S(1)} %get-tuple-element.43.rest_3_), channel_id=1, source_target_pairs={{20,16},{24,20},{28,24},{12,28},{0,4},{4,8},{8,12},{16,0},{21,17},... | collective-permute-start | bytes 196616 | tf_op jit(solution)/shard_map/ppermute | solution.py:576

commit v10 on v8

--- a/solution.py
+++ b/solution.py
@@ -151,6 +151,7 @@
                             pieces.append(flat[pl.ds(first, ncomp, stride=pitch), :])
                     line.append(jnp.concatenate(pieces, axis=0).astype(jnp.bfloat16))
             lines.append(jnp.concatenate(line, axis=1))
+        wrap_copy.start()
         total = jnp.dot(jnp.concatenate(lines, axis=0), spread[...], preferred_element_type=jnp.float32)
         total = total.astype(jnp.bfloat16)
         for b in range(shells):
@@ -158,7 +159,6 @@
             send[spots[b]] = total[
                 column_block * rows : (column_block + 1) * rows, br * LANES : (br + 1) * LANES
             ]
-        wrap_copy.start()
         sends = [
             pltpu.make_async_copy(send.at[pl.ds(step * CAP, CAP)], outs[step], sems.at[first_sem + 4 + step])
             for step in range(n_yz)
@@ -214,7 +214,7 @@
     def _():
         filled[...] = early_ref[...]
 
-    @pl.when(jnp.logical_not(ahead))
+    @pl.when(jnp.logical_not(ahead | helio))
     def _():
         filled[...] = grid_ref[...]
 
@@ -256,6 +256,7 @@
             spread = jnp.where(same & (from_lane // BLK == m), 1.0, 0.0).astype(jnp.bfloat16)
             parts = jnp.dot(lines, spread, preferred_element_type=jnp.float32)
             result[m * pitch : m * pitch + count, :] = parts[:count] + parts[count : 2 * count] + parts[2 * count :]
+        filled[...] = grid_ref[...]
         copy.wait()
         lane = lax.broadcasted_iota(jnp.int32, (BLK, LANES), 1)
         per_y, per_z = len_y // BLK, len_z // BLK

time: 18.7 us -> 18.8 us (level)
  no operation moved by 1% of the time
where the time goes in v10:
time: 18.8 us; the launch traced here: 18.7 us
  starting transfers between devices  11.3 us (60%)
  Pallas kernels  7.07 us (38%)
  waiting for transfers between devices  0.23 us (1%)
    ppermute x4, starting transfers between devices, local(): moved.append(lax.ppermute(packed[step], ('dom', 'yz'), pairs))  4.36 us
    ppermute x1, starting transfers between devices, local(): wrap = lax.ppermute(wrap, ('dom', 'gx', 'yz'), wrap_pairs(n_gx, n_yz))  2.79 us
    pallas_call x1, Pallas kernels, local(): pl.pallas_call(functools.partial(inner_kernel, dims), out_shape=[whole, r...  2.43 us
    pallas_call x1, Pallas kernels, local(): pl.pallas_call(functools.partial(pack_kernel, dims + (n_yz, shells, slots...  2.19 us
    ppermute x1, starting transfers between devices, local(): from_x_two = lax.ppermute(x_two, ('dom', 'gx'), [(b, a) for a, b in once_x])  1.82 us
    ppermute x1, starting transfers between devices, local(): from_y_one = lax.ppermute(y_one, ('dom', 'yz'), once_y)  1.78 us
    pallas_call x1, Pallas kernels, local(): pl.pallas_call(early_kernel, out_shape=[staged[1], jax.ShapeDtypeStruct(w...  1.38 us
    pallas_call x1, Pallas kernels, local(): pl.pallas_call(functools.partial(edge_kernel, dims), out_shape=whole, in_...  0.91 us
  transfers between devices with their start and end apart: 9, of which 1 were waited for; matrix products, arithmetic and copies ran while one was open for 0% of the time, Pallas kernels for 21%

profile of v10, /device:TPU:0, one launch (start us, length us, event | category | flops | bytes accessed | tf_op | source)
XLA Modules:
  0.0 18.7 jit_solution(1114463962878080489)
XLA Ops:
  0.0 2.2 %pack_shell.1 = (bf16[2,32,128]{2,1,0:T(8,128)(2,1)}, bf16[2,32,128]{2,1,0:T(8,128)(2,1)}, bf16[2,32,128]{2,1,0:T(8,128)(2,1)}, bf16[2,32,128]{2,1,0:T(8,128)(2,...) custom-call(s32[1,4,8]{2,1,0:T(4,128)} %owner_hbm.1, s32[1,1,2,4]{3,2,1,0:T(2,128)} %source_hbm.1, ...), custom_call_target="tpu_custom_call" | custom-call | tf_op jit(solution)/shard_map/pack_shell/pallas_call | solution.py:499
  2.2 0.5 %collective-permute-start = (bf16[2,32,128]{2,1,0:T(8,128)(2,1)}, bf16[2,32,128]{2,1,0:T(8,128)(2,1)S(1)}, u32[]{:S(2)}, u32[]{:S(2)}) collective-permute-start(bf16[2,32,128]{2,1,0:T(8,128)(2,1)} %get-tuple-element.30), channel_id=1, source_target_pairs={{0,16},{1,17},{2,18},{3,19},{16,0},{17,1},{18,2},{19,3},{4,20},{5,... | collective-permute-start | bytes 49160 | tf_op jit(solution)/shard_map/ppermute | solution.py:527
  2.7 2.7 %collective-permute-start.1 = (bf16[2,32,128]{2,1,0:T(8,128)(2,1)}, bf16[2,32,128]{2,1,0:T(8,128)(2,1)S(1)}, u32[]{:S(2)}, u32[]{:S(2)}) collective-permute-start(bf16[2,32,128]{2,1,0:T(8,128)(2,1)} %get-tuple-element.31), channel_id=1, source_target_pairs={{0,17},{1,16},{2,19},{3,18},{17,0},{16,1},{19,2},{18,3},{4,21},{5,... | collective-permute-start | bytes 49160 | tf_op jit(solution)/shard_map/ppermute | solution.py:527
  5.3 1.2 %collective-permute-start.2 = (bf16[2,32,128]{2,1,0:T(8,128)(2,1)}, bf16[2,32,128]{2,1,0:T(8,128)(2,1)S(1)}, u32[]{:S(2)}, u32[]{:S(2)}) collective-permute-start(bf16[2,32,128]{2,1,0:T(8,128)(2,1)} %get-tuple-element.32), channel_id=1, source_target_pairs={{0,18},{1,19},{2,16},{3,17},{18,0},{19,1},{16,2},{17,3},{4,22},{5,... | collective-permute-start | bytes 49160 | tf_op jit(solution)/shard_map/ppermute | solution.py:527
  6.5 0.0 collective-permute-start.3
  6.6 0.0 copy-start
  6.6 1.4 %early_grid.1 = (f32[8,256,128]{2,1,0:T(8,128)S(1)}, f32[8,16,128]{2,1,0:T(8,128)}) custom-call(f32[128,256,128]{2,1,0:T(8,128)} %get-tuple-element.25.carried, f32[8,16,128]{2,1,0:T(8,128)} %get-tuple-element.28.wrap_in), custom_call_target="tpu_custom_call", output_to_operand_aliasing={{1}: (1, {})} | custom-call | tf_op jit(solution)/shard_map/early_grid/pallas_call | solution.py:536
  7.9 2.8 %collective-permute-start.8 = (f32[8,16,128]{2,1,0:T(8,128)}, f32[8,16,128]{2,1,0:T(8,128)S(1)}, u32[]{:S(2)}, u32[]{:S(2)}) collective-permute-start(f32[8,16,128]{2,1,0:T(8,128)} %get-tuple-element.44), channel_id=1, source_target_pairs={{0,12},{4,20},{8,24},{1,13},{5,21},{9,25},{2,14},{6,22},{10,26},{3... | collective-permute-start | bytes 196616 | tf_op jit(solution)/shard_map/ppermute | solution.py:546
  10.8 0.0 collective-permute-done.rest_0_
  10.8 0.0 collective-permute-done.1.rest_1_
  10.8 0.0 collective-permute-done.2.rest_2_
  10.8 0.0 collective-permute-done.3.rest_3_
  10.8 0.0 copy-done
  10.8 0.1 fill_blocks.1
  11.0 1.8 %collective-permute-start.4 = (f32[128,128]{1,0:T(8,128)S(1)}, f32[128,128]{1,0:T(8,128)S(1)}, u32[]{:S(2)}, u32[]{:S(2)}) collective-permute-start(f32[128,128]{1,0:T(8,128)S(1)} %get-tuple-element.40.rest_0_), channel_id=1, source_target_pairs={{16,17},{17,18},{18,19},{19,3},{1,0},{2,1},{3,2},{0,16},{20,21},{2... | collective-permute-start | bytes 196616 | tf_op jit(solution)/shard_map/ppermute | solution.py:574
  12.7 0.3 %collective-permute-start.5 = (f32[128,128]{1,0:T(8,128)S(1)}, f32[128,128]{1,0:T(8,128)S(1)}, u32[]{:S(2)}, u32[]{:S(2)}) collective-permute-start(f32[128,128]{1,0:T(8,128)S(1)} %get-tuple-element.41.rest_1_), channel_id=1, source_target_pairs={{17,16},{18,17},{19,18},{3,19},{0,1},{1,2},{2,3},{16,0},{21,20},{2... | collective-permute-start | bytes 196616 | tf_op jit(solution)/shard_map/ppermute | solution.py:575
  13.1 0.2 %collective-permute-start.6 = (f32[128,128]{1,0:T(8,128)S(1)}, f32[128,128]{1,0:T(8,128)S(1)}, u32[]{:S(2)}, u32[]{:S(2)}) collective-permute-start(f32[128,128]{1,0:T(8,128)S(1)} %get-tuple-element.42.rest_2_), channel_id=1, source_target_pairs={{16,20},{20,24},{24,28},{28,12},{4,0},{8,4},{12,8},{0,16},{17,21},... | collective-permute-start | bytes 196616 | tf_op jit(solution)/shard_map/ppermute | solution.py:576
  13.3 1.8 %collective-permute-start.7 = (f32[128,128]{1,0:T(8,128)S(1)}, f32[128,128]{1,0:T(8,128)S(1)}, u32[]{:S(2)}, u32[]{:S(2)}) collective-permute-start(f32[128,128]{1,0:T(8,128)S(1)} %get-tuple-element.43.rest_3_), channel_id=1, source_target_pairs={{20,16},{24,20},{28,24},{12,28},{0,4},{4,8},{8,12},{16,0},{21,17},... | collective-permute-start | bytes 196616 | tf_op jit(solution)/shard_map/ppermute | solution.py:577
  15.1 2.4 %inner_faces.1 = (f32[8,16,16,128]{3,2,1,0:T(8,128)}, f32[8,16,128]{2,1,0:T(8,128)S(1)}, f32[8,16,128]{2,1,0:T(8,128)S(1)}, f32[8,16,128]{2,1,0:T(8,128)S(1)}, f32[8,16,128]{2,1,0:T(8,128)S(1)}) custom-call(f32[2048,128]{1,0:T(8,128)S(1)} %get-tuple-element.34.filled), custom_call_target="tpu_custom_call" | custom-call | flops 78643200 | bytes 2097152 | tf_op jit(solution)/shard_map/inner_faces/pallas_call | solution.py:582
  17.5 0.0 collective-permute-done.8
  17.5 0.0 collective-permute-done.4.rest_4_
  17.5 0.0 collective-permute-done.5.rest_5_
  17.6 0.2 %collective-permute-done.6.rest_6_ = f32[128,128]{1,0:T(8,128)S(1)} collective-permute-done((f32[128,128]{1,0:T(8,128)S(1)}, f32[128,128]{1,0:T(8,128)S(1)}, u32[]{:S(2)}, u32[]{:S(2)}) %collective-permute-start.6) | collective-permute-done | bytes 65568 | tf_op jit(solution)/shard_map/ppermute | solution.py:576
  17.8 0.0 collective-permute-done.7.rest_7_
  17.8 0.9 %edge_faces.1 = f32[8,16,16,128]{3,2,1,0:T(8,128)} custom-call(f32[8,16,16,128]{3,2,1,0:T(8,128)} %get-tuple-element.35.part, f32[8,16,128]{2,1,0:T(8,128)S(1)} %get-tuple-element.36.rim_x_low, f32[8,16,128]{2,1,0:T(8,128)S(1)} %get-tuple-element.37.rim_x_high, f32[8,16,128]{2,1,0:T(8,128)S(1)} %get-tuple-element.38.rim_y_low, ...), custom_call_target="tpu_custom_call", output_to_operand_aliasing={{}: (0, {})} | custom-call | tf_op jit(solution)/shard_map/edge_faces/pallas_call | solution.py:598
  (1 shorter events, 0.0 us)
Async XLA Ops:
  2.2 8.6 %collective-permute-start = (bf16[2,32,128]{2,1,0:T(8,128)(2,1)}, bf16[2,32,128]{2,1,0:T(8,128)(2,1)S(1)}, u32[]{:S(2)}, u32[]{:S(2)}) collective-permute-start(bf16[2,32,128]{2,1,0:T(8,128)(2,1)} %get-tuple-element.30), channel_id=1, source_target_pairs={{0,16},{1,17},{2,18},{3,19},{16,0},{17,1},{18,2},{19,3},{4,20},{5,... | collective-permute-start | bytes 49160 | tf_op jit(solution)/shard_map/ppermute | solution.py:527
  2.7 8.1 %collective-permute-start.1 = (bf16[2,32,128]{2,1,0:T(8,128)(2,1)}, bf16[2,32,128]{2,1,0:T(8,128)(2,1)S(1)}, u32[]{:S(2)}, u32[]{:S(2)}) collective-permute-start(bf16[2,32,128]{2,1,0:T(8,128)(2,1)} %get-tuple-element.31), channel_id=1, source_target_pairs={{0,17},{1,16},{2,19},{3,18},{17,0},{16,1},{19,2},{18,3},{4,21},{5,... | collective-permute-start | bytes 49160 | tf_op jit(solution)/shard_map/ppermute | solution.py:527
  5.3 5.5 %collective-permute-start.2 = (bf16[2,32,128]{2,1,0:T(8,128)(2,1)}, bf16[2,32,128]{2,1,0:T(8,128)(2,1)S(1)}, u32[]{:S(2)}, u32[]{:S(2)}) collective-permute-start(bf16[2,32,128]{2,1,0:T(8,128)(2,1)} %get-tuple-element.32), channel_id=1, source_target_pairs={{0,18},{1,19},{2,16},{3,17},{18,0},{19,1},{16,2},{17,3},{4,22},{5,... | collective-permute-start | bytes 49160 | tf_op jit(solution)/shard_map/ppermute | solution.py:527
  6.5 4.3 %collective-permute-start.3 = (bf16[2,32,128]{2,1,0:T(8,128)(2,1)}, bf16[2,32,128]{2,1,0:T(8,128)(2,1)S(1)}, u32[]{:S(2)}, u32[]{:S(2)}) collective-permute-start(bf16[2,32,128]{2,1,0:T(8,128)(2,1)} %get-tuple-element.33), channel_id=1, source_target_pairs={{0,19},{1,18},{2,17},{3,16},{19,0},{18,1},{17,2},{16,3},{4,23},{5,... | collective-permute-start | bytes 49160 | tf_op jit(solution)/shard_map/ppermute | solution.py:527
  6.6 4.2 %copy-start = (bf16[1,1,2,4,512,512]{5,4,3,2,1,0:T(8,128)(2,1)S(1)}, bf16[1,1,2,4,512,512]{5,4,3,2,1,0:T(8,128)(2,1)}, u32[]{:S(2)}) copy-start(bf16[1,1,2,4,512,512]{5,4,3,2,1,0:T(8,128)(2,1)} %param.9) | copy-start | bytes 12582916
  7.9 9.6 %collective-permute-start.8 = (f32[8,16,128]{2,1,0:T(8,128)}, f32[8,16,128]{2,1,0:T(8,128)S(1)}, u32[]{:S(2)}, u32[]{:S(2)}) collective-permute-start(f32[8,16,128]{2,1,0:T(8,128)} %get-tuple-element.44), channel_id=1, source_target_pairs={{0,12},{4,20},{8,24},{1,13},{5,21},{9,25},{2,14},{6,22},{10,26},{3... | collective-permute-start | bytes 196616 | tf_op jit(solution)/shard_map/ppermute | solution.py:546
  11.0 6.6 %collective-permute-start.4 = (f32[128,128]{1,0:T(8,128)S(1)}, f32[128,128]{1,0:T(8,128)S(1)}, u32[]{:S(2)}, u32[]{:S(2)}) collective-permute-start(f32[128,128]{1,0:T(8,128)S(1)} %get-tuple-element.40.rest_0_), channel_id=1, source_target_pairs={{16,17},{17,18},{18,19},{19,3},{1,0},{2,1},{3,2},{0,16},{20,21},{2... | collective-permute-start | bytes 196616 | tf_op jit(solution)/shard_map/ppermute | solution.py:574
  12.7 4.8 %collective-permute-start.5 = (f32[128,128]{1,0:T(8,128)S(1)}, f32[128,128]{1,0:T(8,128)S(1)}, u32[]{:S(2)}, u32[]{:S(2)}) collective-permute-start(f32[128,128]{1,0:T(8,128)S(1)} %get-tuple-element.41.rest_1_), channel_id=1, source_target_pairs={{17,16},{18,17},{19,18},{3,19},{0,1},{1,2},{2,3},{16,0},{21,20},{2... | collective-permute-start | bytes 196616 | tf_op jit(solution)/shard_map/ppermute | solution.py:575
  13.1 4.7 %collective-permute-start.6 = (f32[128,128]{1,0:T(8,128)S(1)}, f32[128,128]{1,0:T(8,128)S(1)}, u32[]{:S(2)}, u32[]{:S(2)}) collective-permute-start(f32[128,128]{1,0:T(8,128)S(1)} %get-tuple-element.42.rest_2_), channel_id=1, source_target_pairs={{16,20},{20,24},{24,28},{28,12},{4,0},{8,4},{12,8},{0,16},{17,21},... | collective-permute-start | bytes 196616 | tf_op jit(solution)/shard_map/ppermute | solution.py:576
  13.3 4.5 %collective-permute-start.7 = (f32[128,128]{1,0:T(8,128)S(1)}, f32[128,128]{1,0:T(8,128)S(1)}, u32[]{:S(2)}, u32[]{:S(2)}) collective-permute-start(f32[128,128]{1,0:T(8,128)S(1)} %get-tuple-element.43.rest_3_), channel_id=1, source_target_pairs={{20,16},{24,20},{28,24},{12,28},{0,4},{4,8},{8,12},{16,0},{21,17},... | collective-permute-start | bytes 196616 | tf_op jit(solution)/shard_map/ppermute | solution.py:577

commit v11 on v9

--- a/solution.py
+++ b/solution.py
@@ -201,7 +201,7 @@
 
 def fill_kernel(dims, plan_vmem, weight_ref, grid_ref, early_ref, *rest):
     ncomp, len_x, len_y, len_z, n_yz, slots, depth = dims
-    got = rest[:n_yz][::-1]
+    got = rest[:1] + rest[1:n_yz][::-1]
     filled, y_one, y_two, x_one, x_two, result, plan, sem = rest[n_yz:]
     half = BLK // 2
     rows = half * ncomp
@@ -567,7 +567,7 @@
         input_output_aliases={2: 0},
         compiler_params=pltpu.CompilerParams(vmem_limit_bytes=16 * MIB),
         name="fill_blocks",
-    )(plan, weights, grid.reshape(cell_rows, len_z), early_grid.reshape(cell_rows, len_z), *moved[::-1])
+    )(plan, weights, grid.reshape(cell_rows, len_z), early_grid.reshape(cell_rows, len_z), moved[0], *moved[:0:-1])
 
     once_x, once_y = cycle(n_gx), cycle(n_yz)
     from_y_one = lax.ppermute(y_one, ("dom", "yz"), once_y)

time: 18.6 us -> 18.7 us (level)
    ppermute x1, starting transfers between devices: 0.44 us -> 0.82 us  [local(): from_y_one = lax.ppermute(y_one, ('dom', 'yz'), once_y)]
    ppermute x1, starting transfers between devices: 1.64 us -> 1.27 us  [local(): from_y_two = lax.ppermute(y_two, ('dom', 'yz'), [(b, a) for a, b in once_y])]
  transfers between devices with their start and end apart: 9 -> 9, of which waited for: 0 -> 0; matrix products, arithmetic and copies ran while one was open for 0% -> 0% of each run, Pallas kernels for 22% -> 21%
where the time goes in v11:
time: 18.7 us; the launch traced here: 18.5 us
  starting transfers between devices  11.3 us (60%)
  Pallas kernels  7.09 us (38%)
    ppermute x4, starting transfers between devices, local(): moved.append(lax.ppermute(packed[step], ('dom', 'yz'), pairs))  4.41 us
    ppermute x1, starting transfers between devices, local(): wrap = lax.ppermute(wrap, ('dom', 'gx', 'yz'), wrap_pairs(n_gx, n_yz))  2.73 us
    pallas_call x1, Pallas kernels, local(): pl.pallas_call(functools.partial(inner_kernel, dims), out_shape=[whole, r...  2.43 us
    pallas_call x1, Pallas kernels, local(): pl.pallas_call(functools.partial(pack_kernel, dims + (n_yz, shells, slots...  2.19 us
    ppermute x1, starting transfers between devices, local(): from_x_two = lax.ppermute(x_two, ('dom', 'gx'), [(b, a) for a, b in once_x])  2.02 us
    pallas_call x1, Pallas kernels, local(): pl.pallas_call(early_kernel, out_shape=[staged[1], jax.ShapeDtypeStruct(w...  1.38 us
    ppermute x1, starting transfers between devices, local(): from_y_two = lax.ppermute(y_two, ('dom', 'yz'), [(b, a) for a, b in once_y])  1.27 us
    pallas_call x1, Pallas kernels, local(): pl.pallas_call(functools.partial(edge_kernel, dims), out_shape=whole, in_...  0.92 us
  transfers between devices with their start and end apart: 9, of which 0 were waited for; matrix products, arithmetic and copies ran while one was open for 0% of the time, Pallas kernels for 21%

profile of v11, /device:TPU:0, one launch (start us, length us, event | category | flops | bytes accessed | tf_op | source)
XLA Modules:
  0.0 18.5 jit_solution(4398216387428690209)
XLA Ops:
  0.0 2.2 %pack_shell.1 = (bf16[2,32,128]{2,1,0:T(8,128)(2,1)}, bf16[2,32,128]{2,1,0:T(8,128)(2,1)}, bf16[2,32,128]{2,1,0:T(8,128)(2,1)}, bf16[2,32,128]{2,1,0:T(8,128)(2,...) custom-call(s32[1,4,8]{2,1,0:T(4,128)} %owner_hbm.1, s32[1,1,2,4]{3,2,1,0:T(2,128)} %source_hbm.1, ...), custom_call_target="tpu_custom_call" | custom-call | tf_op jit(solution)/shard_map/pack_shell/pallas_call | solution.py:498
  2.2 0.5 %collective-permute-start = (bf16[2,32,128]{2,1,0:T(8,128)(2,1)}, bf16[2,32,128]{2,1,0:T(8,128)(2,1)S(1)}, u32[]{:S(2)}, u32[]{:S(2)}) collective-permute-start(bf16[2,32,128]{2,1,0:T(8,128)(2,1)} %get-tuple-element.30), channel_id=1, source_target_pairs={{0,16},{1,17},{2,18},{3,19},{16,0},{17,1},{18,2},{19,3},{4,20},{5,... | collective-permute-start | bytes 49160 | tf_op jit(solution)/shard_map/ppermute | solution.py:526
  2.7 3.6 %collective-permute-start.1 = (bf16[2,32,128]{2,1,0:T(8,128)(2,1)}, bf16[2,32,128]{2,1,0:T(8,128)(2,1)S(1)}, u32[]{:S(2)}, u32[]{:S(2)}) collective-permute-start(bf16[2,32,128]{2,1,0:T(8,128)(2,1)} %get-tuple-element.31), channel_id=1, source_target_pairs={{0,19},{1,18},{2,17},{3,16},{19,0},{18,1},{17,2},{16,3},{4,23},{5,... | collective-permute-start | bytes 49160 | tf_op jit(solution)/shard_map/ppermute | solution.py:526
  6.3 0.2 collective-permute-start.2
  6.5 0.1 collective-permute-start.3
  6.6 0.0 copy-start
  6.6 1.4 %early_grid.1 = (f32[8,256,128]{2,1,0:T(8,128)S(1)}, f32[8,16,128]{2,1,0:T(8,128)}) custom-call(f32[128,256,128]{2,1,0:T(8,128)} %get-tuple-element.25.carried, f32[8,16,128]{2,1,0:T(8,128)} %get-tuple-element.28.wrap_in), custom_call_target="tpu_custom_call", output_to_operand_aliasing={{1}: (1, {})} | custom-call | tf_op jit(solution)/shard_map/early_grid/pallas_call | solution.py:535
  8.0 2.7 %collective-permute-start.8 = (f32[8,16,128]{2,1,0:T(8,128)}, f32[8,16,128]{2,1,0:T(8,128)S(1)}, u32[]{:S(2)}, u32[]{:S(2)}) collective-permute-start(f32[8,16,128]{2,1,0:T(8,128)} %get-tuple-element.44), channel_id=1, source_target_pairs={{0,12},{4,20},{8,24},{1,13},{5,21},{9,25},{2,14},{6,22},{10,26},{3... | collective-permute-start | bytes 196616 | tf_op jit(solution)/shard_map/ppermute | solution.py:545
  10.8 0.0 collective-permute-done.rest_0_
  10.8 0.0 collective-permute-done.1.rest_1_
  10.8 0.0 collective-permute-done.2.rest_2_
  10.8 0.0 collective-permute-done.3.rest_3_
  10.8 0.0 copy-done
  10.8 0.1 fill_blocks.1
  11.0 0.8 %collective-permute-start.4 = (f32[128,128]{1,0:T(8,128)S(1)}, f32[128,128]{1,0:T(8,128)S(1)}, u32[]{:S(2)}, u32[]{:S(2)}) collective-permute-start(f32[128,128]{1,0:T(8,128)S(1)} %get-tuple-element.40.rest_0_), channel_id=1, source_target_pairs={{16,17},{17,18},{18,19},{19,3},{1,0},{2,1},{3,2},{0,16},{20,21},{2... | collective-permute-start | bytes 196616 | tf_op jit(solution)/shard_map/ppermute | solution.py:573
  11.8 1.3 %collective-permute-start.5 = (f32[128,128]{1,0:T(8,128)S(1)}, f32[128,128]{1,0:T(8,128)S(1)}, u32[]{:S(2)}, u32[]{:S(2)}) collective-permute-start(f32[128,128]{1,0:T(8,128)S(1)} %get-tuple-element.41.rest_1_), channel_id=1, source_target_pairs={{17,16},{18,17},{19,18},{3,19},{0,1},{1,2},{2,3},{16,0},{21,20},{2... | collective-permute-start | bytes 196616 | tf_op jit(solution)/shard_map/ppermute | solution.py:574
  13.1 0.0 collective-permute-start.6
  13.1 2.0 %collective-permute-start.7 = (f32[128,128]{1,0:T(8,128)S(1)}, f32[128,128]{1,0:T(8,128)S(1)}, u32[]{:S(2)}, u32[]{:S(2)}) collective-permute-start(f32[128,128]{1,0:T(8,128)S(1)} %get-tuple-element.43.rest_3_), channel_id=1, source_target_pairs={{20,16},{24,20},{28,24},{12,28},{0,4},{4,8},{8,12},{16,0},{21,17},... | collective-permute-start | bytes 196616 | tf_op jit(solution)/shard_map/ppermute | solution.py:576
  15.1 2.4 %inner_faces.1 = (f32[8,16,16,128]{3,2,1,0:T(8,128)}, f32[8,16,128]{2,1,0:T(8,128)S(1)}, f32[8,16,128]{2,1,0:T(8,128)S(1)}, f32[8,16,128]{2,1,0:T(8,128)S(1)}, f32[8,16,128]{2,1,0:T(8,128)S(1)}) custom-call(f32[2048,128]{1,0:T(8,128)S(1)} %get-tuple-element.34.filled), custom_call_target="tpu_custom_call" | custom-call | flops 78643200 | bytes 2097152 | tf_op jit(solution)/shard_map/inner_faces/pallas_call | solution.py:581
  17.5 0.0 collective-permute-done.8
  17.5 0.0 collective-permute-done.4.rest_4_
  17.5 0.0 collective-permute-done.5.rest_5_
  17.6 0.0 collective-permute-done.6.rest_6_
  17.6 0.0 collective-permute-done.7.rest_7_
  17.6 0.9 %edge_faces.1 = f32[8,16,16,128]{3,2,1,0:T(8,128)} custom-call(f32[8,16,16,128]{3,2,1,0:T(8,128)} %get-tuple-element.35.part, f32[8,16,128]{2,1,0:T(8,128)S(1)} %get-tuple-element.36.rim_x_low, f32[8,16,128]{2,1,0:T(8,128)S(1)} %get-tuple-element.37.rim_x_high, f32[8,16,128]{2,1,0:T(8,128)S(1)} %get-tuple-element.38.rim_y_low, ...), custom_call_target="tpu_custom_call", output_to_operand_aliasing={{}: (0, {})} | custom-call | tf_op jit(solution)/shard_map/edge_faces/pallas_call | solution.py:597
  (1 shorter events, 0.0 us)
Async XLA Ops:
  2.2 8.6 %collective-permute-start = (bf16[2,32,128]{2,1,0:T(8,128)(2,1)}, bf16[2,32,128]{2,1,0:T(8,128)(2,1)S(1)}, u32[]{:S(2)}, u32[]{:S(2)}) collective-permute-start(bf16[2,32,128]{2,1,0:T(8,128)(2,1)} %get-tuple-element.30), channel_id=1, source_target_pairs={{0,16},{1,17},{2,18},{3,19},{16,0},{17,1},{18,2},{19,3},{4,20},{5,... | collective-permute-start | bytes 49160 | tf_op jit(solution)/shard_map/ppermute | solution.py:526
  2.7 8.1 %collective-permute-start.1 = (bf16[2,32,128]{2,1,0:T(8,128)(2,1)}, bf16[2,32,128]{2,1,0:T(8,128)(2,1)S(1)}, u32[]{:S(2)}, u32[]{:S(2)}) collective-permute-start(bf16[2,32,128]{2,1,0:T(8,128)(2,1)} %get-tuple-element.31), channel_id=1, source_target_pairs={{0,19},{1,18},{2,17},{3,16},{19,0},{18,1},{17,2},{16,3},{4,23},{5,... | collective-permute-start | bytes 49160 | tf_op jit(solution)/shard_map/ppermute | solution.py:526
  6.3 4.5 %collective-permute-start.2 = (bf16[2,32,128]{2,1,0:T(8,128)(2,1)}, bf16[2,32,128]{2,1,0:T(8,128)(2,1)S(1)}, u32[]{:S(2)}, u32[]{:S(2)}) collective-permute-start(bf16[2,32,128]{2,1,0:T(8,128)(2,1)} %get-tuple-element.32), channel_id=1, source_target_pairs={{0,18},{1,19},{2,16},{3,17},{18,0},{19,1},{16,2},{17,3},{4,22},{5,... | collective-permute-start | bytes 49160 | tf_op jit(solution)/shard_map/ppermute | solution.py:526
  6.5 4.3 %collective-permute-start.3 = (bf16[2,32,128]{2,1,0:T(8,128)(2,1)}, bf16[2,32,128]{2,1,0:T(8,128)(2,1)S(1)}, u32[]{:S(2)}, u32[]{:S(2)}) collective-permute-start(bf16[2,32,128]{2,1,0:T(8,128)(2,1)} %get-tuple-element.33), channel_id=1, source_target_pairs={{0,17},{1,16},{2,19},{3,18},{17,0},{16,1},{19,2},{18,3},{4,21},{5,... | collective-permute-start | bytes 49160 | tf_op jit(solution)/shard_map/ppermute | solution.py:526
  6.6 4.2 %copy-start = (bf16[1,1,2,4,512,512]{5,4,3,2,1,0:T(8,128)(2,1)S(1)}, bf16[1,1,2,4,512,512]{5,4,3,2,1,0:T(8,128)(2,1)}, u32[]{:S(2)}) copy-start(bf16[1,1,2,4,512,512]{5,4,3,2,1,0:T(8,128)(2,1)} %param.9) | copy-start | bytes 12582916
  8.0 9.5 %collective-permute-start.8 = (f32[8,16,128]{2,1,0:T(8,128)}, f32[8,16,128]{2,1,0:T(8,128)S(1)}, u32[]{:S(2)}, u32[]{:S(2)}) collective-permute-start(f32[8,16,128]{2,1,0:T(8,128)} %get-tuple-element.44), channel_id=1, source_target_pairs={{0,12},{4,20},{8,24},{1,13},{5,21},{9,25},{2,14},{6,22},{10,26},{3... | collective-permute-start | bytes 196616 | tf_op jit(solution)/shard_map/ppermute | solution.py:545
  11.0 6.6 %collective-permute-start.4 = (f32[128,128]{1,0:T(8,128)S(1)}, f32[128,128]{1,0:T(8,128)S(1)}, u32[]{:S(2)}, u32[]{:S(2)}) collective-permute-start(f32[128,128]{1,0:T(8,128)S(1)} %get-tuple-element.40.rest_0_), channel_id=1, source_target_pairs={{16,17},{17,18},{18,19},{19,3},{1,0},{2,1},{3,2},{0,16},{20,21},{2... | collective-permute-start | bytes 196616 | tf_op jit(solution)/shard_map/ppermute | solution.py:573
  11.8 5.8 %collective-permute-start.5 = (f32[128,128]{1,0:T(8,128)S(1)}, f32[128,128]{1,0:T(8,128)S(1)}, u32[]{:S(2)}, u32[]{:S(2)}) collective-permute-start(f32[128,128]{1,0:T(8,128)S(1)} %get-tuple-element.41.rest_1_), channel_id=1, source_target_pairs={{17,16},{18,17},{19,18},{3,19},{0,1},{1,2},{2,3},{16,0},{21,20},{2... | collective-permute-start | bytes 196616 | tf_op jit(solution)/shard_map/ppermute | solution.py:574
  13.1 4.5 %collective-permute-start.6 = (f32[128,128]{1,0:T(8,128)S(1)}, f32[128,128]{1,0:T(8,128)S(1)}, u32[]{:S(2)}, u32[]{:S(2)}) collective-permute-start(f32[128,128]{1,0:T(8,128)S(1)} %get-tuple-element.42.rest_2_), channel_id=1, source_target_pairs={{16,20},{20,24},{24,28},{28,12},{4,0},{8,4},{12,8},{0,16},{17,21},... | collective-permute-start | bytes 196616 | tf_op jit(solution)/shard_map/ppermute | solution.py:575
  13.1 4.5 %collective-permute-start.7 = (f32[128,128]{1,0:T(8,128)S(1)}, f32[128,128]{1,0:T(8,128)S(1)}, u32[]{:S(2)}, u32[]{:S(2)}) collective-permute-start(f32[128,128]{1,0:T(8,128)S(1)} %get-tuple-element.43.rest_3_), channel_id=1, source_target_pairs={{20,16},{24,20},{28,24},{12,28},{0,4},{4,8},{8,12},{16,0},{21,17},... | collective-permute-start | bytes 196616 | tf_op jit(solution)/shard_map/ppermute | solution.py:576
